TPU v7x, 128 devices: a whole 4x4x4 slice. The times are simulated.
128 devices in a mesh: frame: 8 (over y, core), spatial: 2 (over x_lo), head: 8 (over x_hi, z).
Axes of the slice: x: 4 (x_hi: 2, x_lo: 2; x = x_hi * 2 + x_lo), y: 4, z: 4, core: 2. Of those that a mesh axis runs over, the one named last changes fastest.
Arguments:
- tokens: bfloat16 [16, 512, 3072], P('frame', 'spatial'), may hold values from -6 to 6
- w_qkv: bfloat16 [3072, 3, 3072], P(None, None, 'head'), may hold values from -0.109375 to 0.109375
- w_out: bfloat16 [3072, 3072], P('head'), may hold values from -0.109375 to 0.109375
- shift: float32 [3072], replicated, may hold values from -3 to 3
- scale: float32 [3072], replicated, may hold values from -2 to 2
- gate: float32 [3072], P('head'), may hold values from 0.5 to 1.5
- q_gain: float32 [128], replicated, may hold values from 1 to 2
- k_gain: float32 [128], replicated, may hold values from 1 to 2
- band: int32 [16], replicated, may hold values from 1 to 2
- far_tiles: int32 [16, 4, 4, 2], replicated, may hold values from 0 to 15, as said below
Outputs:
- update: bfloat16 [16, 512, 3072], P('frame', 'spatial', 'head')
Inputs may be any that keep to these rules, and one draw needn't show every extreme that they name: `far_tiles`: A region is 2 consecutive frames starting at a multiple of 2, times the tiles 2 * s to 2 * s + 1 of each such frame; a block is 2 such frames. Every entry names a frame whose block differs from the query tile's block by 2 or more, counted cyclically over the 16 / 2 blocks, and a tile index below 4. The entries of all query tiles of one region name at most 2 distinct tiles of any one region, exactly 2 for some pair of regions. Entries of one query tile may repeat.
All inputs are finite; a program needn't handle non-finite values.
Results may differ from a plain program's by a relative error of at most 0.019.
Values may be sent and summed in bfloat16 or wider, within the bound.
No kernel may reach another device: no remote copies, remote signals or barrier semaphores. Data moves between devices by JAX's collectives and lax.ppermute only.
A program may use at most 128 MiB of HBM per device.

v0:
```python
import jax
import jax.numpy as jnp
from jax import lax
from jax.sharding import PartitionSpec as P

HEAD_DIM = 128
TILE = 128


NORM_EPS = 1e-06


def rms_norm(projected, gain):
    squares = jnp.mean(projected * projected, axis=-1, keepdims=True)
    return (projected * lax.rsqrt(squares + NORM_EPS) * gain).astype(jnp.bfloat16)


def shards(tokens, w_qkv, w_out, shift, scale, gate, q_gain, k_gain, band, far_tiles):
    frames_dev, half_tok, model_width = tokens.shape
    row_count = frames_dev * half_tok
    heads_dev = w_qkv.shape[2] // HEAD_DIM
    n_spatial = lax.axis_size("spatial")
    tiles_half = half_tok // TILE
    frame_index = lax.axis_index("frame")
    half_index = lax.axis_index("spatial")
    score_scale = HEAD_DIM ** (-0.5)
    flat_rows = tokens.reshape(row_count, model_width).astype(jnp.float32)
    row_mean = jnp.mean(flat_rows, axis=1, keepdims=True)
    centred = flat_rows - row_mean
    row_var = jnp.mean(centred * centred, axis=1, keepdims=True)
    normed = (centred * lax.rsqrt(row_var + NORM_EPS) * (1.0 + scale) + shift).astype(jnp.bfloat16)
    projected = jnp.dot(normed, w_qkv.reshape(model_width, -1), preferred_element_type=jnp.float32)
    projected = projected.reshape(row_count, 3, heads_dev, HEAD_DIM)
    queries = rms_norm(projected[:, 0], q_gain)
    keys_normed = rms_norm(projected[:, 1], k_gain)
    values_bf = projected[:, 2].astype(jnp.bfloat16)
    packed = jnp.stack([keys_normed, values_bf], axis=1).reshape(
        frames_dev, half_tok, 2 * heads_dev * HEAD_DIM
    )
    query_heads = jnp.transpose(queries, (1, 0, 2))
    first_frame = frame_index * frames_dev
    query_frames = first_frame + jnp.arange(frames_dev, dtype=jnp.int32)
    band_widths = lax.dynamic_slice_in_dim(band, first_frame, frames_dev, 0)
    my_lists = lax.dynamic_slice_in_dim(far_tiles, first_frame, frames_dev, 0)
    my_lists = lax.dynamic_slice_in_dim(my_lists, half_index * tiles_half, tiles_half, 1)
    shard_piece = lax.all_gather(packed, ("frame", "spatial"), axis=0, tiled=True)
    piece_rows = shard_piece.shape[0]
    global_rows = jnp.arange(piece_rows, dtype=jnp.int32)
    owner = global_rows // frames_dev
    key_frames = owner // n_spatial * frames_dev + global_rows % frames_dev
    key_tiles = (owner % n_spatial)[:, None] * tiles_half + jnp.arange(tiles_half, dtype=jnp.int32)[
        None, :
    ]
    in_band = jnp.abs(query_frames[:, None] - key_frames[None, :]) <= band_widths[:, None]
    listed_hit = (
        my_lists[:, :, :, 0][:, :, :, None, None] == key_frames[None, None, None, :, None]
    ) & (my_lists[:, :, :, 1][:, :, :, None, None] == key_tiles[None, None, None, :, :])
    allowed = jnp.any(listed_hit, axis=2) | in_band[:, None, :, None]
    spread = jnp.broadcast_to(
        allowed[:, :, None, :, :, None],
        (frames_dev, tiles_half, TILE, piece_rows, tiles_half, TILE),
    )
    key_mask = spread.reshape(row_count, piece_rows * half_tok).astype(jnp.float32)
    key_parts = shard_piece.reshape(piece_rows * half_tok, -1).reshape(-1, 2, heads_dev, HEAD_DIM)
    numer_list = []
    denom_list = []
    for head_at in range(heads_dev):
        scores = (
            jnp.einsum(
                "qd,kd->qk",
                query_heads[head_at],
                key_parts[:, 0, head_at],
                preferred_element_type=jnp.float32,
            )
            * score_scale
        )
        weights = jnp.exp(scores) * key_mask
        denom_list.append(jnp.sum(weights, axis=1))
        numer_list.append(
            jnp.dot(
                weights.astype(jnp.bfloat16),
                key_parts[:, 1, head_at],
                preferred_element_type=jnp.float32,
            )
        )
    numer_sum = jnp.stack(numer_list)
    denom_sum = jnp.stack(denom_list)
    attended = (numer_sum / denom_sum[:, :, None]).astype(jnp.bfloat16)
    mixed_heads = jnp.transpose(attended, (1, 0, 2)).reshape(row_count, heads_dev * HEAD_DIM)
    term_rows = jnp.dot(mixed_heads, w_out, preferred_element_type=jnp.float32)
    summed = lax.psum_scatter(
        term_rows.astype(jnp.bfloat16), "head", scatter_dimension=1, tiled=True
    ).astype(jnp.float32)
    result = (summed * gate).astype(jnp.bfloat16)
    return result.reshape(frames_dev, half_tok, -1)


def solution(mesh):
    return jax.shard_map(
        shards,
        mesh=mesh,
        in_specs=(
            P("frame", "spatial", None),
            P(None, None, "head"),
            P("head", None),
            P(),
            P(),
            P("head"),
            P(),
            P(),
            P(),
            P(),
        ),
        out_specs=P("frame", "spatial", "head"),
        check_vma=False,
    )
```

profile of v0, /device:TPU:0, one launch (start us, length us, event | category | flops | bytes accessed | tf_op | source)
XLA Modules:
  0.0 284.7 jit_solution(14288065957138805211)
XLA Ops:
  6.5 0.0 all-gather.2.cloned.1.call-start
  6.5 2.5 convert_reduce_fusion
  9.1 2.8 fusion.8
  12.0 0.0 copy-start.5
  12.0 10.3 %copy.34 = bf16[3072,3,384]{0,2,1:T(8,128)(2,1)} copy(bf16[3072,3,384]{2,0,1:T(8,128)(2,1)} %param.11) | data formatting | bytes 14155776 | tf_op args[1]
  22.3 3.6 %fusion.11 = bf16[2,256,3072]{2,1,0:T(8,128)(2,1)S(1)} fusion(bf16[2,256,3072]{2,1,0:T(8,128)(2,1)} %param.10, f32[3072]{0:T(1024)S(1)} %copy-done.5, f32[3072]{0:T(1024)S(1)} %broadcast_add_fusion, f32[2,256]{1,0:T(2,128)S(1)} %add_rsqrt_fusion.2, f32[2,256]{1,0:T(2,128)S(1)} %broadcast_multiply_fusion), kind=kLoop, calls=%fused_computation.16 | loop fusion | flops 9437184 | bytes 6320128 | tf_op jit(solution)/shard_map/convert_element_type | solution.py:31
  25.9 0.0 copy-start.8
  25.9 6.4 %fusion.28 = f32[512,3,3,128]{0,3,2,1:T(8,128)S(1)} fusion(bf16[512,3072,1,1]{1,0,3,2:T(8,128)(2,1)S(1)} %bitcast.103, bf16[3,3,128,3072]{3,2,1,0:T(8,128)(2,1)} %bitcast.102), kind=kOutput, calls=%fused_computation.70 | convolution fusion | flops 3623878656 | bytes 12582912 | tf_op jit(solution)/shard_map/dot_general | solution.py:32
  32.3 0.0 copy-start.10
  32.3 0.0 copy-start.6
  32.3 0.1 multiply_reduce_fusion
  32.4 0.1 slice.103
  32.4 1.2 copy-done.2
  33.7 0.1 multiply_convert_fusion.1
  33.8 0.1 pad_maximum_fusion
  33.9 1.1 reshape.263
  34.9 3.1 %copy.35 = bf16[2,256,768]{2,1,0:T(8,128)(2,1)} copy(bf16[2,256,768]{1,0,2:T(2,128)(2,1)} %reshape.263) | data formatting | bytes 1572864 | tf_op jit(solution)/shard_map/reshape | solution.py:37
  38.0 0.0 all-gather.2.cloned.1.call-update
  38.0 0.2 reduce-scatter.4.cloned.1.call-start
  38.3 0.1 dynamic_slice.9
  38.4 0.1 constant_dynamic-slice_fusion
  38.5 0.1 copy.31
  38.6 0.1 copy.32
  38.7 0.1 broadcast_compare_fusion
  38.8 0.1 and_reduce_fusion
  38.9 0.1 abs_compare_fusion
  39.0 0.1 copy.33
  39.1 6.7 %broadcast_in_dim.2 = pred[2,2,128,32,2,128]{5,4,3,2,1,0:T(4,128)(4,1)} broadcast(pred[2,2,32,2]{3,2,1,0:T(8,128)(4,1)S(1)} %copy.33), dimensions={0,1,3,4} | broadcast | bytes 4194560 | tf_op jit(solution)/shard_map/broadcast_in_dim | solution.py:59
  45.8 21.5 %reshape.261 = pred[512,8192]{1,0:T(32,128)(4,1)} reshape(pred[2,2,128,32,2,128]{5,4,3,2,1,0:T(4,128)(4,1)} %broadcast_in_dim.2) | data formatting | bytes 8388608 | tf_op jit(solution)/shard_map/reshape | solution.py:63
  67.3 1.2 multiply_reduce_fusion.1
  68.6 1.3 fusion.22
  69.8 45.9 %all-gather.2.cloned.1.call-done = bf16[32,256,768]{2,1,0:T(8,128)(2,1)} async-done(((bf16[2,256,768]{2,1,0:T(8,128)(2,1)}), bf16[32,256,768]{2,1,0:T(8,128)(2,1)}) %all-gather.2.cloned.1.call-update) | async-done | bytes 12582928 | tf_op jit(solution)/shard_map/all_gather | solution.py:46
  115.8 16.9 %copy.36 = bf16[32,256,768]{1,0,2:T(8,128)(2,1)} copy(bf16[32,256,768]{2,1,0:T(8,128)(2,1)} %all-gather.2.cloned.1.call-done) | data formatting | bytes 25165824 | tf_op jit(solution)/shard_map/all_gather | solution.py:46
  132.7 19.6 %reshape_reshape.3 = bf16[8192,2,3,128]{0,3,2,1:T(8,128)(2,1)} reshape(bf16[32,256,768]{1,0,2:T(8,128)(2,1)} %copy.36) | data formatting | bytes 25165824 | tf_op jit(solution)/shard_map/reshape;reshape | solution.py:64
  152.2 7.9 %fusion.25 = (f32[512]{0:T(512)S(1)}, bf16[512,8192]{1,0:T(8,128)(2,1)S(1)}) fusion(pred[512,8192]{1,0:T(32,128)(4,1)} %reshape.261, bf16[8192,2,3,128]{0,3,2,1:T(8,128)(2,1)} %reshape_reshape.3, bf16[3,512,128]{1,2,0:T(8,128)(2,1)S(1)} %fusion.22), kind=kOutput, calls=%fused_computation.67 | convolution fusion | flops 1090518528 | bytes 14813184 | tf_op jit(solution)/shard_map/qd,kd->qk/dot_general | solution.py:69
  160.1 7.2 %fusion.26 = (f32[512]{0:T(512)S(1)}, bf16[512,8192]{1,0:T(8,128)(2,1)}) fusion(pred[512,8192]{1,0:T(32,128)(4,1)S(1)} %copy-done.3, bf16[8192,2,3,128]{0,3,2,1:T(8,128)(2,1)S(1)} %copy-done.1, bf16[3,512,128]{1,2,0:T(8,128)(2,1)S(1)} %fusion.22), kind=kOutput, calls=%fused_computation.68 | convolution fusion | flops 1090518528 | bytes 14813184 | tf_op jit(solution)/shard_map/qd,kd->qk/dot_general | solution.py:69
  167.3 7.0 %fusion.27 = (f32[512]{0:T(512)S(1)}, bf16[512,8192]{1,0:T(8,128)(2,1)}) fusion(pred[512,8192]{1,0:T(32,128)(4,1)S(1)} %copy-done.3, bf16[8192,2,3,128]{0,3,2,1:T(8,128)(2,1)S(1)} %copy-done.1, bf16[3,512,128]{1,2,0:T(8,128)(2,1)S(1)} %fusion.22), kind=kOutput, calls=%fused_computation.69 | convolution fusion | flops 1090518528 | bytes 14813184 | tf_op jit(solution)/shard_map/qd,kd->qk/dot_general | solution.py:69
  174.3 3.0 %fusion.18 = f32[1,512,128]{1,2,0:T(8,128)S(1)} fusion(bf16[8192,2,3,128]{0,3,2,1:T(8,128)(2,1)S(1)} %copy-done.1, bf16[512,8192]{1,0:T(8,128)(2,1)S(1)} %get-tuple-element.8), kind=kOutput, calls=%fused_computation.26 | convolution fusion | flops 1073741824 | bytes 10747904 | tf_op jit(solution)/shard_map/dot_general | solution.py:80
  177.3 0.0 slice-start.1
  177.3 6.5 %fusion.15 = f32[1,512,128]{1,2,0:T(8,128)S(1)} fusion(bf16[8192,2,3,128]{0,3,2,1:T(8,128)(2,1)S(1)} %copy-done.1, bf16[512,8192]{1,0:T(8,128)(2,1)} %get-tuple-element.10), kind=kOutput, calls=%fused_computation.25 | convolution fusion | flops 1073741824 | bytes 10747904 | tf_op jit(solution)/shard_map/dot_general | solution.py:80
  183.8 3.0 %fusion.12 = f32[1,512,128]{1,2,0:T(8,128)S(1)} fusion(bf16[8192,2,3,128]{0,3,2,1:T(8,128)(2,1)S(1)} %copy-done.1, bf16[512,8192]{1,0:T(8,128)(2,1)S(1)} %bitcast.112), kind=kOutput, calls=%fused_computation.24 | convolution fusion | flops 1073741824 | bytes 10747904 | tf_op jit(solution)/shard_map/dot_general | solution.py:80
  186.9 0.1 fusion.21
  187.0 3.6 %convolution_convert_fusion = bf16[512,3072]{1,0:T(8,128)(2,1)} fusion(bf16[512,384]{0,1:T(8,128)(2,1)S(1)} %bitcast.105, bf16[384,3072]{1,0:T(8,128)(2,1)S(1)} %copy-done), kind=kOutput, calls=%fused_computation.17 | convolution fusion | flops 1209532416 | bytes 5898240 | tf_op jit(solution)/shard_map/dot_general | solution.py:90
  190.5 4.7 %copy.44 = bf16[512,3072]{0,1:T(8,128)(2,1)} copy(bf16[512,3072]{1,0:T(8,128)(2,1)} %convolution_convert_fusion) | data formatting | bytes 6291456
  195.2 0.0 reduce-scatter.4.cloned.1.call-update
  195.2 80.6 %reduce-scatter.4.cloned.1.call-done = bf16[384,512]{1,0:T(8,128)(2,1)} async-done(((bf16[3072,512]{1,0:T(8,128)(2,1)}), bf16[384,512]{1,0:T(8,128)(2,1)}) %reduce-scatter.4.cloned.1.call-update) | async-done | bytes 393232
  275.8 1.2 copy.45
  277.0 0.8 multiply_convert_fusion
  (31 shorter events, 0.1 us)
Async XLA Ops:
  6.5 180.4 %copy-start = (bf16[384,3072]{1,0:T(8,128)(2,1)S(1)}, bf16[384,3072]{1,0:T(8,128)(2,1)}, u32[]{:S(2)}) copy-start(bf16[384,3072]{1,0:T(8,128)(2,1)} %param.12) | copy-start | bytes 7077892
  6.5 5.4 %copy-start.4 = (f32[3072]{0:T(1024)S(1)}, f32[3072]{0:T(1024)}, u32[]{:S(2)}) copy-start(f32[3072]{0:T(1024)} %param.14) | copy-start | bytes 36868
  6.5 109.2 %all-gather.2.cloned.1.call-start = ((), (), s32[]{:S(2)}) async-start(), calls=%async_computation.1 | async-start | bytes 13369344 | tf_op jit(solution)/shard_map/all_gather | solution.py:46
  12.0 10.3 %copy-start.5 = (f32[3072]{0:T(1024)S(1)}, f32[3072]{0:T(1024)}, u32[]{:S(2)}) copy-start(f32[3072]{0:T(1024)} %param.13) | copy-start | bytes 36868
  25.9 7.8 %copy-start.8 = (f32[128]{0:T(128)S(1)}, f32[128]{0:T(128)}, u32[]{:S(2)}) copy-start(f32[128]{0:T(128)} %param.17) | copy-start | bytes 1540
  32.2 1.4 copy-start.2
  32.3 6.0 %copy-start.10 = (s32[16]{0:T(128)S(1)}, s32[16]{0:T(128)}, u32[]{:S(2)}) copy-start(s32[16]{0:T(128)} %param.18) | copy-start | bytes 196
  32.3 6.1 %copy-start.6 = (s32[16,4,4,2]{0,3,2,1:T(2,128)S(1)}, s32[16,4,4,2]{0,3,2,1:T(2,128)}, u32[]{:S(2)}) copy-start(s32[16,4,4,2]{0,3,2,1:T(2,128)} %param.19) | copy-start | bytes 6148
  38.0 237.8 %reduce-scatter.4.cloned.1.call-start = ((), (), s32[]{:S(2)}) async-start(), calls=%async_computation.2 | async-start | bytes 3538944
  45.8 22.8 %copy-start.9 = (f32[128]{0:T(128)S(1)}, f32[128]{0:T(128)}, u32[]{:S(2)}) copy-start(f32[128]{0:T(128)} %param.16) | copy-start | bytes 1540
  152.2 7.9 %copy-start.1 = (bf16[8192,2,3,128]{0,3,2,1:T(8,128)(2,1)S(1)}, bf16[8192,2,3,128]{0,3,2,1:T(8,128)(2,1)}, u32[]{:S(2)}) copy-start(bf16[8192,2,3,128]{0,3,2,1:T(8,128)(2,1)} %reshape_reshape.3) | copy-start | bytes 37748740
  152.2 7.9 %copy-start.3 = (pred[512,8192]{1,0:T(32,128)(4,1)S(1)}, pred[512,8192]{1,0:T(32,128)(4,1)}, u32[]{:S(2)}) copy-start(pred[512,8192]{1,0:T(32,128)(4,1)} %reshape.261) | copy-start | bytes 12582916
  174.3 9.5 %slice-start = ((s8[8388608]{0:T(1024)(128)(4,1)}), s8[4194304]{0:T(1024)(128)(4,1)S(1)}, s32[]{:S(2)}) async-start(s8[8388608]{0:T(1024)(128)(4,1)} %bitcast.111), calls=%async_computation.3 | async-start | bytes 8388608
  177.3 6.5 %slice-start.1 = ((s8[8388608]{0:T(1024)(128)(4,1)}), s8[4194304]{0:T(1024)(128)(4,1)S(1)}, s32[]{:S(2)}) async-start(s8[8388608]{0:T(1024)(128)(4,1)} %bitcast.111), calls=%async_computation.4 | async-start | bytes 8388608
  190.5 86.5 %copy-start.7 = (f32[384]{0:T(512)S(1)}, f32[384]{0:T(512)}, u32[]{:S(2)}) copy-start(f32[384]{0:T(512)} %param.15) | copy-start | bytes 4612
Sparse Core Ops, SparseCore 0:
  38.2 77.5 all-gather.1
  195.4 80.4 reduce-scatter.3
where the time goes:
time: 286 us; the launch traced here: 285 us
  waiting for transfers between devices  127 us (44%)
  local copies, waits for them, and re-layouts  86.8 us (30%)
  matrix products  44.5 us (16%)
  between operations  13.7 us (5%)
  other arithmetic  13 us (5%)
    unnamed x3, waiting for transfers between devices  80.6 us
    all_gather x1, waiting for transfers between devices, shards(): lax.all_gather(packed, ('frame', 'spatial'), axis=0, tiled=True)  45.9 us
    dot_general x3, matrix products, shards(): jnp.einsum('qd,kd->qk', query_heads[head_at], key_parts[:, 0, head_at], p...  22 us
    reshape x1, local copies, waits for them, and re-layouts, shards(): spread.reshape(row_count, piece_rows * half_tok).astype(jnp.float32)  21.5 us
    another operation x1, local copies, waits for them, and re-layouts, shards(): shard_piece.reshape(piece_rows * half_tok, -1)  19.6 us
    unnamed x29, local copies, waits for them, and re-layouts  17.4 us
    all_gather x1, local copies, waits for them, and re-layouts, shards(): lax.all_gather(packed, ('frame', 'spatial'), axis=0, tiled=True)  16.9 us
    dot_general x3, matrix products, shards(): jnp.dot(weights.astype(jnp.bfloat16), key_parts[:, 1, head_at], preferred...  12.5 us
  transfers between devices with their start and end apart: 2, of which 2 were waited for; matrix products, arithmetic and copies ran while one was open for 11% of the time, Pallas kernels for 0%

commit v1 on v0

v1 whole, which is shorter than its diff:
```python
import functools

import jax
import jax.numpy as jnp
from jax import lax
from jax.experimental import pallas as pl
from jax.experimental.pallas import tpu as pltpu
from jax.sharding import PartitionSpec as P

HEAD_DIM = 128
TILE = 128
NORM_EPS = 1e-06
LOG2E = 1.4426950408889634
ANY = pl.BlockSpec(memory_space=pl.ANY)
VMEM = pl.BlockSpec(memory_space=pltpu.VMEM)
SMEM = pl.BlockSpec(memory_space=pltpu.SMEM)
PARAMS = pltpu.CompilerParams(vmem_limit_bytes=56 * 1024 * 1024)
F32 = jnp.float32
BF16 = jnp.bfloat16


def rows_dot(a, b):
    return lax.dot_general(a, b, (((1,), (1,)), ((), ())), preferred_element_type=F32)


def rms_norm(part, gain):
    squares = jnp.mean(part * part, axis=-1, keepdims=True)
    return (part * lax.rsqrt(squares + NORM_EPS) * gain).astype(BF16)


def project_kernel(
    s_ref, x_ref, w_ref, scale_ref, shift_ref, qg_ref, kg_ref,
    ao_ref, am_ref, xkv_ref, ql_ref, qx_ref,
    x_scr, n_scr, w_scr, x_sem, w_sem,
):
    rows, width = n_scr.shape
    chunk = rows // 8
    x_copies = [
        pltpu.make_async_copy(
            x_ref.at[pl.ds(i * chunk, chunk)], x_scr.at[pl.ds(i * chunk, chunk)], x_sem.at[i]
        )
        for i in range(8)
    ]
    w_copies = [pltpu.make_async_copy(w_ref.at[j], w_scr.at[j], w_sem.at[j]) for j in range(3)]
    for copy in x_copies:
        copy.start()
    for j in (1, 2, 0):
        w_copies[j].start()
    gain = 1.0 + scale_ref[...]
    shift = shift_ref[...]
    for i in range(8):
        x_copies[i].wait()

        def one_block(step, carry, base=i * chunk):
            at = pl.ds(pl.multiple_of(base + step * 16, 16), 16)
            x = x_scr[at, :].astype(F32)
            centred = x - jnp.mean(x, axis=1, keepdims=True)
            var = jnp.mean(centred * centred, axis=1, keepdims=True)
            n_scr[at, :] = (centred * lax.rsqrt(var + NORM_EPS) * gain + shift).astype(BF16)
            return carry

        lax.fori_loop(0, chunk // 16, one_block, 0, unroll=True)
    first = s_ref[0] == 0
    kgain = kg_ref[...]
    qgain = qg_ref[...]

    def heads_of(j, gain_row):
        w_copies[j].wait()
        full = jnp.dot(n_scr[...], w_scr[j], preferred_element_type=F32)
        parts = [full[:, h * HEAD_DIM:(h + 1) * HEAD_DIM] for h in range(3)]
        if gain_row is None:
            parts = [part.astype(BF16) for part in parts]
        else:
            parts = [rms_norm(part, gain_row) for part in parts]
        own = jnp.where(first, parts[0], parts[2])
        other = jnp.where(first, parts[2], parts[0])
        shape = (2, rows // 2, HEAD_DIM)
        return own.reshape(shape), parts[1].reshape(shape), other.reshape(shape)

    for j, gain_row, low in ((1, kgain, 0), (2, None, HEAD_DIM)):
        own, mid, other = heads_of(j, gain_row)
        lanes = slice(low, low + HEAD_DIM)
        ao_ref[:, :, lanes] = own
        am_ref[:, :, lanes] = mid
        xkv_ref[:, :, lanes] = other
    own, mid, other = heads_of(0, qgain)
    ql_ref[:, :, :HEAD_DIM] = own
    ql_ref[:, :, HEAD_DIM:] = mid
    qx_ref[:, :, :HEAD_DIM] = other
    qx_ref[:, :, HEAD_DIM:] = mid


def project(s, tokens, w, scale, shift, q_gain, k_gain):
    frames, half_tok, width = tokens.shape
    rows = frames * half_tok
    piece = jax.ShapeDtypeStruct((frames, half_tok, 2 * HEAD_DIM), BF16)
    return pl.pallas_call(
        project_kernel,
        out_shape=[piece] * 5,
        in_specs=[SMEM, ANY, ANY] + [VMEM] * 4,
        out_specs=[VMEM] * 5,
        scratch_shapes=[
            pltpu.VMEM((rows, width), BF16),
            pltpu.VMEM((rows, width), BF16),
            pltpu.VMEM(w.shape, BF16),
            pltpu.SemaphoreType.DMA((8,)),
            pltpu.SemaphoreType.DMA((3,)),
        ],
        compiler_params=PARAMS,
        cost_estimate=pl.CostEstimate(
            flops=2 * rows * width * 9 * HEAD_DIM, bytes_accessed=12_000_000, transcendentals=0
        ),
        name="project",
    )(
        s.reshape(1), tokens.reshape(rows, width), w,
        scale.reshape(1, -1), shift.reshape(1, -1), q_gain.reshape(1, -1), k_gain.reshape(1, -1),
    )


META_BLOCKS = 1
META_FRAME = 9
META_BAND = 10
META_FAR = 12


def attend_kernel(meta_ref, *refs):
    ql_ref, qx_ref = refs[0:2]
    pieces = refs[2:26]
    home_ref, mid_ref, ret_ref = refs[26:29]
    q_scr, kvo, kvm, acc_o, acc_m, sem = refs[29:35]
    n_frames = kvo.shape[0]
    half = ql_ref.shape[1]
    s = meta_ref[0]
    copies = [
        pltpu.make_async_copy(ql_ref, q_scr.at[:, pl.ds(0, half)], sem.at[24]),
        pltpu.make_async_copy(qx_ref, q_scr.at[:, pl.ds(half, half)], sem.at[25]),
    ]
    two = pl.ds(0, 2 * HEAD_DIM)
    for r in range(8):
        frames = pl.ds(2 * meta_ref[META_BLOCKS + r], 2)
        near = pl.ds(pl.multiple_of(s * half, half), half)
        away = pl.ds(pl.multiple_of((1 - s) * half, half), half)
        copies.append(
            pltpu.make_async_copy(pieces[3 * r], kvo.at[frames, near, two], sem.at[3 * r])
        )
        copies.append(
            pltpu.make_async_copy(pieces[3 * r + 1], kvm.at[frames, :, two], sem.at[3 * r + 1])
        )
        copies.append(
            pltpu.make_async_copy(pieces[3 * r + 2], kvo.at[frames, away, two], sem.at[3 * r + 2])
        )
    for copy in copies:
        copy.start()
    ones = slice(2 * HEAD_DIM, 3 * HEAD_DIM)
    kvo[:, :, ones] = jnp.ones((n_frames, 2 * half, HEAD_DIM), BF16)
    kvm[:, :, ones] = jnp.ones((n_frames, half, HEAD_DIM), BF16)
    for copy in copies:
        copy.wait()
    factor = LOG2E * HEAD_DIM ** (-0.5)

    def weights_of(q, keys):
        return jnp.exp2(rows_dot(q, keys) * factor)

    eye = lax.broadcasted_iota(jnp.int32, (TILE, TILE), 0) == lax.broadcasted_iota(
        jnp.int32, (TILE, TILE), 1
    )
    first_frame = meta_ref[META_FRAME]
    for fi in range(2):
        frame = first_frame + fi
        width = meta_ref[META_BAND + fi]
        acc_o[...] = jnp.zeros_like(acc_o)
        acc_m[...] = jnp.zeros_like(acc_m)

        def one_frame(kf, carry, fi=fi):
            keys = kvo[kf]
            weights = weights_of(q_scr[fi, :, :HEAD_DIM], keys[:, :HEAD_DIM]).astype(BF16)
            acc_o[...] += jnp.dot(weights, keys[:, HEAD_DIM:], preferred_element_type=F32)
            keys = kvm[kf]
            weights = weights_of(q_scr[fi, :, HEAD_DIM:], keys[:, :HEAD_DIM]).astype(BF16)
            acc_m[...] += jnp.dot(weights, keys[:, HEAD_DIM:], preferred_element_type=F32)
            return carry

        low = jnp.maximum(frame - width, 0)
        high = jnp.minimum(frame + width, n_frames - 1)
        lax.fori_loop(low, high + 1, one_frame, 0)

        for r in range(2):
            for t in range(2):
                at = slice(r * half + t * TILE, r * half + (t + 1) * TILE)
                tile = 2 * (s ^ r) + t
                base = META_FAR + ((fi * 4 + tile) * 4) * 2
                entries = [(meta_ref[base + 2 * j], meta_ref[base + 2 * j + 1]) for j in range(4)]
                flags = []
                for j in range(4):
                    fresh = jnp.bool_(True)
                    for i in range(j):
                        same = (entries[i][0] == entries[j][0]) & (entries[i][1] == entries[j][1])
                        fresh = fresh & jnp.logical_not(same)
                    flags.append(fresh)
                keys = jnp.concatenate(
                    [kvo[kf, pl.ds(pl.multiple_of(kt * TILE, TILE), TILE), :] for kf, kt in entries],
                    axis=0,
                )
                weights = weights_of(q_scr[fi, at, :HEAD_DIM], keys[:, :HEAD_DIM])
                weights = jnp.concatenate(
                    [
                        weights[:, j * TILE:(j + 1) * TILE] * jnp.where(flags[j], 1.0, 0.0)
                        for j in range(4)
                    ],
                    axis=1,
                ).astype(BF16)
                acc_o[at, :] += jnp.dot(weights, keys[:, HEAD_DIM:], preferred_element_type=F32)
                keys = jnp.concatenate(
                    [
                        kvm[kf, pl.ds(pl.multiple_of((kt % 2) * TILE, TILE), TILE), :]
                        for kf, kt in entries
                    ],
                    axis=0,
                )
                weights = weights_of(q_scr[fi, at, HEAD_DIM:], keys[:, :HEAD_DIM])
                weights = jnp.concatenate(
                    [
                        weights[:, j * TILE:(j + 1) * TILE]
                        * jnp.where(flags[j] & (entries[j][1] // 2 == s), 1.0, 0.0)
                        for j in range(4)
                    ],
                    axis=1,
                ).astype(BF16)
                acc_m[at, :] += jnp.dot(weights, keys[:, HEAD_DIM:], preferred_element_type=F32)

        attended = (acc_o[:, :HEAD_DIM] / acc_o[:, HEAD_DIM:]).astype(BF16)
        home_ref[fi] = attended[:half]
        ret_ref[fi, :half, :HEAD_DIM] = attended[half:]
        mid_ref[fi] = acc_m[:half, :]
        ret_ref[fi, :half, HEAD_DIM:] = acc_m[half:, :HEAD_DIM].astype(BF16)
        dens = []
        for g in range(2):
            den = acc_m[half + g * TILE:half + (g + 1) * TILE, HEAD_DIM:]
            dens.append(jnp.sum(jnp.where(eye, den, 0.0), axis=0, keepdims=True))
        den = jnp.concatenate(dens, axis=0)
        upper = den.astype(BF16).astype(F32)
        block = jnp.concatenate([upper, den - upper, jnp.zeros((12, TILE), F32)], axis=0)
        ret_ref[fi, half:, :HEAD_DIM] = block.astype(BF16)
        ret_ref[fi, half:, HEAD_DIM:] = jnp.zeros((16, HEAD_DIM), BF16)


def attend(meta, q_home, q_away, pieces, n_frames):
    frames, half, _ = q_home.shape
    return pl.pallas_call(
        attend_kernel,
        out_shape=[
            jax.ShapeDtypeStruct((frames, half, HEAD_DIM), BF16),
            jax.ShapeDtypeStruct((frames, half, 2 * HEAD_DIM), F32),
            jax.ShapeDtypeStruct((frames, half + 16, 2 * HEAD_DIM), BF16),
        ],
        in_specs=[SMEM] + [ANY] * (2 + len(pieces)),
        out_specs=[VMEM] * 3,
        scratch_shapes=[
            pltpu.VMEM((frames, 2 * half, 2 * HEAD_DIM), BF16),
            pltpu.VMEM((n_frames, 2 * half, 3 * HEAD_DIM), BF16),
            pltpu.VMEM((n_frames, half, 3 * HEAD_DIM), BF16),
            pltpu.VMEM((2 * half, 2 * HEAD_DIM), F32),
            pltpu.VMEM((2 * half, 2 * HEAD_DIM), F32),
            pltpu.SemaphoreType.DMA((26,)),
        ],
        compiler_params=PARAMS,
        cost_estimate=pl.CostEstimate(
            flops=10_000_000_000, bytes_accessed=8_000_000, transcendentals=5_000_000
        ),
        name="attend",
    )(meta, q_home, q_away, *pieces)


def combine_kernel(s_ref, home_ref, mid_ref, got_ref, out0_ref, out1_ref):
    half = home_ref.shape[1]
    own_lanes = pl.ds(pl.multiple_of(s_ref[0] * 2 * HEAD_DIM, HEAD_DIM), HEAD_DIM)
    other_lanes = pl.ds(pl.multiple_of((1 - s_ref[0]) * 2 * HEAD_DIM, HEAD_DIM), HEAD_DIM)
    eye = lax.broadcasted_iota(jnp.int32, (TILE, TILE), 0) == lax.broadcasted_iota(
        jnp.int32, (TILE, TILE), 1
    )
    ones = jnp.ones((TILE, TILE), BF16)
    for fi, out_ref in enumerate((out0_ref, out1_ref)):
        out_ref[:, own_lanes] = home_ref[fi]
        out_ref[:, other_lanes] = got_ref[fi, :half, :HEAD_DIM]
        tail = got_ref[fi, half:, :HEAD_DIM].astype(F32)
        for g in range(2):
            at = slice(g * TILE, (g + 1) * TILE)
            upper = jnp.where(eye, tail[g:g + 1, :], 0.0).astype(BF16)
            lower = jnp.where(eye, tail[2 + g:3 + g, :], 0.0).astype(BF16)
            den = jnp.dot(upper, ones, preferred_element_type=F32) + jnp.dot(
                lower, ones, preferred_element_type=F32
            )
            num = mid_ref[fi, at, :HEAD_DIM] + got_ref[fi, at, HEAD_DIM:].astype(F32)
            out_ref[at, HEAD_DIM:2 * HEAD_DIM] = (
                num / (mid_ref[fi, at, HEAD_DIM:] + den)
            ).astype(BF16)


def combine(s, home, mid, got):
    half = home.shape[1]
    out = jax.ShapeDtypeStruct((half, 3 * HEAD_DIM), BF16)
    return pl.pallas_call(
        combine_kernel,
        out_shape=[out, out],
        in_specs=[SMEM, VMEM, VMEM, VMEM],
        out_specs=[VMEM, VMEM],
        compiler_params=PARAMS,
        cost_estimate=pl.CostEstimate(
            flops=50_000_000, bytes_accessed=1_500_000, transcendentals=0
        ),
        name="combine",
    )(s.reshape(1), home, mid, got)


def output_kernel(core_ref, *refs):
    mixed = refs[0:16]
    w_near, w_far = refs[16:20], refs[20:24]
    gate_ref, out_ref, h_scr, w_scr, h_sem, w_sem = refs[24:30]
    half, width = mixed[0].shape
    part = w_near[0].shape[1]
    core = core_ref[0]
    copies = []
    for k in range(4):
        for side in range(2):
            base = (side * 4 + k) * width
            for at, (source, which) in enumerate(((w_near, core), (w_far, 1 - core))):
                copies.append(
                    pltpu.make_async_copy(
                        source[k].at[side],
                        w_scr.at[pl.ds(pl.multiple_of(base + which * part, part), part)],
                        w_sem.at[(k * 2 + side) * 2 + at],
                    )
                )
    for fi in range(2):
        for g in range(8):
            copies.append(
                pltpu.make_async_copy(
                    mixed[fi * 8 + g],
                    h_scr.at[pl.ds(fi * half, half), pl.ds(g * width, width)],
                    h_sem.at[fi * 8 + g],
                )
            )
    for copy in copies:
        copy.start()
    for copy in copies:
        copy.wait()
    total = jnp.dot(h_scr[...], w_scr[...], preferred_element_type=F32)
    out_ref[...] = (total * gate_ref[...]).astype(BF16)


def output(core, mixed, w_near, w_far, gate):
    half, width = mixed[0].shape
    cols = w_near[0].shape[2]
    return pl.pallas_call(
        output_kernel,
        out_shape=jax.ShapeDtypeStruct((2 * half, cols), BF16),
        in_specs=[SMEM] + [ANY] * 24 + [VMEM],
        out_specs=VMEM,
        scratch_shapes=[
            pltpu.VMEM((2 * half, 8 * width), BF16),
            pltpu.VMEM((8 * width, cols), BF16),
            pltpu.SemaphoreType.DMA((16,)),
            pltpu.SemaphoreType.DMA((16,)),
        ],
        compiler_params=PARAMS,
        cost_estimate=pl.CostEstimate(
            flops=4 * half * 8 * width * cols, bytes_accessed=6_000_000, transcendentals=0
        ),
        name="output",
    )(core.reshape(1), *mixed, *w_near, *w_far, gate.reshape(1, -1))


def move(axis, to, x):
    count = lax.axis_size(axis)
    return lax.ppermute(x, axis, [(i, to(i)) for i in range(count)])


up_y = functools.partial(move, "frame", lambda i: (i + 2) % 8)
down_y = functools.partial(move, "frame", lambda i: (i + 6) % 8)
swap_core = functools.partial(move, "frame", lambda i: i ^ 1)
swap_half = functools.partial(move, "spatial", lambda i: i ^ 1)
up_z = functools.partial(move, "head", lambda i: i // 4 * 4 + (i + 1) % 4)
down_z = functools.partial(move, "head", lambda i: i // 4 * 4 + (i + 3) % 4)
cross_z = functools.partial(move, "head", lambda i: i // 4 * 4 + (i + 2) % 4)
swap_x = functools.partial(move, "head", lambda i: i ^ 4)


def ring(piece, up, down, by_up):
    before, after = up(piece), down(piece)
    return [piece, before, after, up(before) if by_up else down(after)]


def shards(tokens, w_qkv, w_out, shift, scale, gate, q_gain, k_gain, band, far_tiles):
    frames_dev, half_tok, model_width = tokens.shape
    n_frames = band.shape[0]
    f = lax.axis_index("frame")
    s = lax.axis_index("spatial")
    g = lax.axis_index("head")
    core, y, z, side = f % 2, f // 2, g % 4, g // 4

    part = w_out.shape[0] // 2
    cols = model_width // 8
    kept = lax.dynamic_slice(w_out, (core * part, side * 4 * cols), (part, 4 * cols))
    sent = lax.dynamic_slice(w_out, (core * part, (1 - side) * 4 * cols), (part, 4 * cols))
    both = jnp.stack([kept, swap_x(sent)])

    def w_for(step):
        return lax.dynamic_slice(both, (0, 0, (z + step) % 4 * cols), (2, part, cols))

    w_near = [w_for(0), up_z(w_for(1)), down_z(w_for(3)), cross_z(w_for(2))]
    w_far = [swap_core(w) for w in w_near]

    own, mid, other, q_home, q_send = project(
        s, tokens, jnp.transpose(w_qkv, (1, 0, 2)), scale, shift, q_gain, k_gain
    )
    away = swap_half(other)
    rings = [
        ring(own, up_y, down_y, True),
        ring(mid, up_y, down_y, False),
        ring(away, up_y, down_y, True),
    ]
    q_away = swap_half(q_send)
    pieces = []
    for r in range(4):
        pieces += [one[r] for one in rings]
    for r in range(4):
        pieces += [swap_core(one[r]) for one in rings]
    ys = jnp.stack([y, (y + 3) % 4, (y + 1) % 4, (y + 2) % 4])
    blocks = jnp.concatenate([2 * ys + core, 2 * ys + 1 - core])
    first = f * frames_dev
    meta = jnp.concatenate(
        [
            s.reshape(1),
            blocks,
            first.reshape(1),
            lax.dynamic_slice_in_dim(band, first, frames_dev, 0),
            lax.dynamic_slice_in_dim(far_tiles, first, frames_dev, 0).reshape(-1),
        ]
    ).astype(jnp.int32)
    home, mid_sums, back = attend(meta, q_home, q_away, pieces, n_frames)
    mixed = combine(s, home, mid_sums, swap_half(back))
    gathered = []
    for fi in range(2):
        gathered += ring(mixed[fi], up_z, down_z, fi == 0)
        gathered += ring(swap_x(mixed[fi]), up_z, down_z, fi == 0)
    result = output(core, gathered, w_near, w_far, gate)
    return result.reshape(frames_dev, half_tok, -1)


def solution(mesh):
    return jax.shard_map(
        shards,
        mesh=mesh,
        in_specs=(
            P("frame", "spatial", None),
            P(None, None, "head"),
            P("head", None),
            P(),
            P(),
            P("head"),
            P(),
            P(),
            P(),
            P(),
        ),
        out_specs=P("frame", "spatial", "head"),
        check_vma=False,
    )
```

time: 286 us -> 137 us (0.48)
  local copies, waits for them, and re-layouts: 86.8 us -> 6.13 us
  waiting for transfers between devices: 127 us -> 52.9 us
  starting transfers between devices: 0.22 us -> 47.4 us
  matrix products: 44.5 us -> 0 us
  Pallas kernels: 0 us -> 29.8 us
  between operations: 13.7 us -> 0.58 us
  other arithmetic: 13 us -> 0.2 us
    unnamed x3 -> x0, waiting for transfers between devices: 80.6 us -> none
    ppermute x0 -> x46, waiting for transfers between devices: none -> 52.9 us  [move(): return lax.ppermute(x, axis, [(i, to(i)) for i in range(count)])]
    ppermute x0 -> x46, starting transfers between devices: none -> 47.4 us  [move(): return lax.ppermute(x, axis, [(i, to(i)) for i in range(count)])]
    all_gather x1 -> x0, waiting for transfers between devices: 45.9 us -> none  [shards(): lax.all_gather(packed, ('frame', 'spatial'), axis=0, tiled=True)]
    dot_general x8 -> x0, matrix products: 44.5 us -> none  [the longest x3 22 us: shards(): jnp.einsum('qd,kd->qk', query_heads[head_at], key_parts[:, 0, head_at], p...]
    pallas_call x0 -> x4, Pallas kernels: none -> 29.8 us  [the longest x1 11.1 us: project(): pl.pallas_call(project_kernel, out_shape=[piece] * 5, in_specs=[SMEM, ANY...]
    reshape x3 -> x2, local copies, waits for them, and re-layouts: 25.7 us -> 0.7 us  [the longest x1 0.58 us: output(): gate.reshape(1, -1)]
    another operation x1 -> x0, local copies, waits for them, and re-layouts: 19.6 us -> none  [shards(): shard_piece.reshape(piece_rows * half_tok, -1)]
  transfers between devices with their start and end apart: 2 -> 46, of which waited for: 2 -> 18; matrix products, arithmetic and copies ran while one was open for 11% -> 1% of each run, Pallas kernels for 0% -> 9%
where the time goes in v1:
time: 137 us
  waiting for transfers between devices  52.9 us (39%)
  starting transfers between devices  47.4 us (35%)
  Pallas kernels  29.8 us (22%)
  local copies, waits for them, and re-layouts  6.13 us (4%)
    ppermute x46, waiting for transfers between devices, move(): return lax.ppermute(x, axis, [(i, to(i)) for i in range(count)])  52.9 us
    ppermute x46, starting transfers between devices, move(): return lax.ppermute(x, axis, [(i, to(i)) for i in range(count)])  47.4 us
    pallas_call x1, Pallas kernels, project(): pl.pallas_call(project_kernel, out_shape=[piece] * 5, in_specs=[SMEM, ANY...  11.1 us
    pallas_call x1, Pallas kernels, attend(): pl.pallas_call(attend_kernel, out_shape=[jax.ShapeDtypeStruct((frames, ha...  10.5 us
    pallas_call x1, Pallas kernels, output(): pl.pallas_call(output_kernel, out_shape=jax.ShapeDtypeStruct((2 * half, c...  6.14 us
    unnamed x86, local copies, waits for them, and re-layouts  4.37 us
  transfers between devices with their start and end apart: 46, of which 18 were waited for; matrix products, arithmetic and copies ran while one was open for 1% of the time, Pallas kernels for 9%

profile of v1, /device:TPU:0, one launch (start us, length us, event | category | flops | bytes accessed | tf_op | source)
XLA Modules:
  0.0 137.1 jit_solution(6021097893104366378)
XLA Ops:
  0.0 11.1 %project.1 = (bf16[2,256,256]{2,1,0:T(8,128)(2,1)}, bf16[2,256,256]{2,1,0:T(8,128)(2,1)}, bf16[2,256,256]{2,1,0:T(8,128)(2,1)}, bf16[2,256,256]{2,1,0:T(8,128)(2,1)}, bf16[2,256,256]{2,1,0:T(8,128)(2,1)}) custom-call(s32[1]{0:T(128)} %bitcast.1.s_ref, bf16[512,3072]{1,0:T(8,128)(2,1)} %bitcast.19, bf16[3,3072,384]{2,1,0:T(8,128)(2,1)} %bitcast.18, ...), custom_call_target="tpu_custom_call" | custom-call | flops 3623878656 | bytes 12000000 | tf_op jit(solution)/shard_map/project/pallas_call | solution.py:97
  11.1 1.7 %collective-permute-start = (bf16[2,256,256]{2,1,0:T(8,128)(2,1)}, bf16[2,256,256]{2,1,0:T(8,128)(2,1)S(1)}, u32[]{:S(2)}, u32[]{:S(2)}) collective-permute-start(bf16[2,256,256]{2,1,0:T(8,128)(2,1)} %get-tuple-element.16), channel_id=1, source_target_pairs={{0,8},{8,0},{1,9},{9,1},{2,10},{10,2},{3,11},{11,3},{4,12},{12,4},... | collective-permute-start | bytes 786440 | tf_op jit(solution)/shard_map/ppermute | solution.py:375
  13.2 1.7 %collective-permute-start.2 = (bf16[2,256,256]{2,1,0:T(8,128)(2,1)}, bf16[2,256,256]{2,1,0:T(8,128)(2,1)}, u32[]{:S(2)}, u32[]{:S(2)}) collective-permute-start(bf16[2,256,256]{2,1,0:T(8,128)(2,1)} %get-tuple-element.17.refs_2_), channel_id=1, source_target_pairs={{0,32},{16,48},{32,64},{48,80},{64,96},{80,112},{96,0},{112,16},{1... | collective-permute-start | bytes 786440 | tf_op jit(solution)/shard_map/ppermute | solution.py:375
  14.9 1.6 %collective-permute-start.5 = (bf16[2,256,256]{2,1,0:T(8,128)(2,1)}, bf16[2,256,256]{2,1,0:T(8,128)(2,1)}, u32[]{:S(2)}, u32[]{:S(2)}) collective-permute-start(bf16[2,256,256]{2,1,0:T(8,128)(2,1)} %get-tuple-element.17.refs_2_), channel_id=1, source_target_pairs={{0,96},{16,112},{32,0},{48,16},{64,32},{80,48},{96,64},{112,80},{1... | collective-permute-start | bytes 786440 | tf_op jit(solution)/shard_map/ppermute | solution.py:375
  16.9 3.7 %collective-permute-done.refs_1_ = bf16[2,256,256]{2,1,0:T(8,128)(2,1)S(1)} collective-permute-done((bf16[2,256,256]{2,1,0:T(8,128)(2,1)}, bf16[2,256,256]{2,1,0:T(8,128)(2,1)S(1)}, u32[]{:S(2)}, u32[]{:S(2)}) %collective-permute-start) | collective-permute-done | bytes 262176 | tf_op jit(solution)/shard_map/ppermute | solution.py:375
  20.6 3.1 %collective-permute-start.6 = (bf16[2,256,256]{2,1,0:T(8,128)(2,1)}, bf16[2,256,256]{2,1,0:T(8,128)(2,1)}, u32[]{:S(2)}, u32[]{:S(2)}) collective-permute-start(bf16[2,256,256]{2,1,0:T(8,128)(2,1)} %get-tuple-element.18.refs_3_), channel_id=1, source_target_pairs={{0,96},{16,112},{32,0},{48,16},{64,32},{80,48},{96,64},{112,80},{1... | collective-permute-start | bytes 786440 | tf_op jit(solution)/shard_map/ppermute | solution.py:375
  23.7 1.2 collective-permute-done.1.refs_4_
  24.9 0.7 copy-done.28
  25.7 3.3 %collective-permute-start.38 = (bf16[192,1536]{1,0:T(8,128)(2,1)S(1)}, bf16[192,1536]{1,0:T(8,128)(2,1)S(1)}, u32[]{:S(2)}, u32[]{:S(2)}) collective-permute-start(bf16[192,1536]{1,0:T(8,128)(2,1)S(1)} %get-tuple-element.27), channel_id=1, source_target_pairs={{0,4},{1,5},{2,6},{3,7},{4,0},{5,1},{6,2},{7,3},{8,12},{9,13},{10,... | collective-permute-start | bytes 1769480 | tf_op jit(solution)/shard_map/ppermute | solution.py:375
  29.3 1.6 %collective-permute-start.4 = (bf16[2,256,256]{2,1,0:T(8,128)(2,1)S(1)}, bf16[2,256,256]{2,1,0:T(8,128)(2,1)S(1)}, u32[]{:S(2)}, u32[]{:S(2)}) collective-permute-start(bf16[2,256,256]{2,1,0:T(8,128)(2,1)S(1)} %copy-done.29), channel_id=1, source_target_pairs={{0,32},{16,48},{32,64},{48,80},{64,96},{80,112},{96,0},{112,16},{1... | collective-permute-start | bytes 786440 | tf_op jit(solution)/shard_map/ppermute | solution.py:375
  30.9 1.7 %collective-permute-start.7 = (bf16[2,256,256]{2,1,0:T(8,128)(2,1)S(1)}, bf16[2,256,256]{2,1,0:T(8,128)(2,1)S(1)}, u32[]{:S(2)}, u32[]{:S(2)}) collective-permute-start(bf16[2,256,256]{2,1,0:T(8,128)(2,1)S(1)} %copy-done.29), channel_id=1, source_target_pairs={{0,96},{16,112},{32,0},{48,16},{64,32},{80,48},{96,64},{112,80},{1... | collective-permute-start | bytes 786440 | tf_op jit(solution)/shard_map/ppermute | solution.py:375
  32.9 2.9 %collective-permute-start.9 = (bf16[2,256,256]{2,1,0:T(8,128)(2,1)}, bf16[2,256,256]{2,1,0:T(8,128)(2,1)}, u32[]{:S(2)}, u32[]{:S(2)}) collective-permute-start(bf16[2,256,256]{2,1,0:T(8,128)(2,1)} %collective-permute-done.6.refs_9_), channel_id=1, source_target_pairs={{0,96},{16,112},{32,0},{48,16},{64,32},{80,48},{96,64},{112,80},{1... | collective-permute-start | bytes 786440 | tf_op jit(solution)/shard_map/ppermute | solution.py:375
  35.8 3.8 %collective-permute-done.4.refs_7_ = bf16[2,256,256]{2,1,0:T(8,128)(2,1)S(1)} collective-permute-done((bf16[2,256,256]{2,1,0:T(8,128)(2,1)S(1)}, bf16[2,256,256]{2,1,0:T(8,128)(2,1)S(1)}, u32[]{:S(2)}, u32[]{:S(2)}) %collective-permute-start.4) | collective-permute-done | bytes 262176 | tf_op jit(solution)/shard_map/ppermute | solution.py:375
  40.2 4.5 %collective-permute-done.8.refs_11_ = bf16[2,256,256]{2,1,0:T(8,128)(2,1)S(1)} collective-permute-done((bf16[2,256,256]{2,1,0:T(8,128)(2,1)}, bf16[2,256,256]{2,1,0:T(8,128)(2,1)S(1)}, u32[]{:S(2)}, u32[]{:S(2)}) %collective-permute-start.8) | collective-permute-done | bytes 262176 | tf_op jit(solution)/shard_map/ppermute | solution.py:375
  45.5 1.4 %collective-permute-start.10 = (bf16[2,256,256]{2,1,0:T(8,128)(2,1)S(1)}, bf16[2,256,256]{2,1,0:T(8,128)(2,1)}, u32[]{:S(2)}, u32[]{:S(2)}) collective-permute-start(bf16[2,256,256]{2,1,0:T(8,128)(2,1)S(1)} %collective-permute-done.4.refs_7_), channel_id=1, source_target_pairs={{0,32},{16,48},{32,64},{48,80},{64,96},{80,112},{96,0},{112,16},{1... | collective-permute-start | bytes 786440 | tf_op jit(solution)/shard_map/ppermute | solution.py:375
  47.8 0.8 copy-done.35
  49.1 6.2 %collective-permute-done.10.refs_13_ = bf16[2,256,256]{2,1,0:T(8,128)(2,1)} collective-permute-done((bf16[2,256,256]{2,1,0:T(8,128)(2,1)S(1)}, bf16[2,256,256]{2,1,0:T(8,128)(2,1)}, u32[]{:S(2)}, u32[]{:S(2)}) %collective-permute-start.10) | collective-permute-done | bytes 262176 | tf_op jit(solution)/shard_map/ppermute | solution.py:375
  55.3 1.9 %collective-permute-start.39 = (bf16[2,192,384]{2,1,0:T(8,128)(2,1)S(1)}, bf16[2,192,384]{2,1,0:T(8,128)(2,1)S(1)}, u32[]{:S(2)}, u32[]{:S(2)}) collective-permute-start(bf16[2,192,384]{2,1,0:T(8,128)(2,1)S(1)} %get-tuple-element.31), channel_id=1, source_target_pairs={{0,1},{1,2},{2,3},{3,0},{4,5},{5,6},{6,7},{7,4},{8,9},{9,10},{10,1... | collective-permute-start | bytes 884744 | tf_op jit(solution)/shard_map/ppermute | solution.py:375
  57.2 2.1 %collective-permute-start.40 = (bf16[2,192,384]{2,1,0:T(8,128)(2,1)S(1)}, bf16[2,192,384]{2,1,0:T(8,128)(2,1)S(1)}, u32[]{:S(2)}, u32[]{:S(2)}) collective-permute-start(bf16[2,192,384]{2,1,0:T(8,128)(2,1)S(1)} %get-tuple-element.32), channel_id=1, source_target_pairs={{0,3},{1,0},{2,1},{3,2},{4,7},{5,4},{6,5},{7,6},{8,11},{9,8},{10,9... | collective-permute-start | bytes 884744 | tf_op jit(solution)/shard_map/ppermute | solution.py:375
  59.8 0.6 concatenate.3.meta_ref
  60.5 1.9 %collective-permute-start.41 = (bf16[2,192,384]{2,1,0:T(8,128)(2,1)S(1)}, bf16[2,192,384]{2,1,0:T(8,128)(2,1)S(1)}, u32[]{:S(2)}, u32[]{:S(2)}) collective-permute-start(bf16[2,192,384]{2,1,0:T(8,128)(2,1)S(1)} %get-tuple-element.29), channel_id=1, source_target_pairs={{0,2},{1,3},{2,0},{3,1},{4,6},{5,7},{6,4},{7,5},{8,10},{9,11},{10,... | collective-permute-start | bytes 884744 | tf_op jit(solution)/shard_map/ppermute | solution.py:375
  62.3 0.7 copy-done.40
  63.3 3.1 %collective-permute-done.39.refs_17_ = bf16[2,192,384]{2,1,0:T(8,128)(2,1)S(1)} collective-permute-done((bf16[2,192,384]{2,1,0:T(8,128)(2,1)S(1)}, bf16[2,192,384]{2,1,0:T(8,128)(2,1)S(1)}, u32[]{:S(2)}, u32[]{:S(2)}) %collective-permute-start.39) | collective-permute-done | bytes 294944 | tf_op jit(solution)/shard_map/ppermute | solution.py:375
  66.3 5.2 %collective-permute-done.40.refs_18_ = bf16[2,192,384]{2,1,0:T(8,128)(2,1)S(1)} collective-permute-done((bf16[2,192,384]{2,1,0:T(8,128)(2,1)S(1)}, bf16[2,192,384]{2,1,0:T(8,128)(2,1)S(1)}, u32[]{:S(2)}, u32[]{:S(2)}) %collective-permute-start.40) | collective-permute-done | bytes 294944 | tf_op jit(solution)/shard_map/ppermute | solution.py:375
  71.6 0.7 copy-done.41
  72.3 10.5 %attend.1 = (bf16[2,256,128]{2,1,0:T(8,128)(2,1)}, f32[2,256,256]{2,1,0:T(8,128)}, bf16[2,272,256]{2,1,0:T(8,128)(2,1)}) custom-call(s32[76]{0:T(128)} %concatenate.3.meta_ref, bf16[2,256,256]{2,1,0:T(8,128)(2,1)} %get-tuple-element.15.refs_0_, bf16[2,256,256]{2,1,0:T(8,128)(2,1)} %copy-done.27, bf16[2,256,256]{2,1,0:T(8,128)(2,1)} %get-tuple-element.17.refs_2_, ...), custom_call_target="tpu_custom_call" | custom-call | flops 10000000000 | bytes 8000000 | tf_op jit(solution)/shard_map/attend/pallas_call | solution.py:249
  82.8 0.7 collective-permute-start.23
  83.5 0.8 collective-permute-start.45
  84.2 8.3 %collective-permute-done.23.got_ref = bf16[2,272,256]{2,1,0:T(8,128)(2,1)S(1)} collective-permute-done((bf16[2,272,256]{2,1,0:T(8,128)(2,1)}, bf16[2,272,256]{2,1,0:T(8,128)(2,1)S(1)}, u32[]{:S(2)}, u32[]{:S(2)}) %collective-permute-start.23) | collective-permute-done | bytes 278560 | tf_op jit(solution)/shard_map/ppermute | solution.py:375
  92.5 0.7 copy-done.10
  93.2 2.1 %combine.1 = (bf16[256,384]{1,0:T(8,128)(2,1)}, bf16[256,384]{1,0:T(8,128)(2,1)}) custom-call(s32[1]{0:T(128)} %bitcast.1.s_ref, bf16[2,256,128]{2,1,0:T(8,128)(2,1)} %get-tuple-element.20.home_ref, f32[2,256,256]{2,1,0:T(8,128)} %get-tuple-element.21.mid_ref, bf16[2,272,256]{2,1,0:T(8,128)(2,1)} %copy-done.10), custom_call_target="tpu_custom_call" | custom-call | flops 50000000 | bytes 1500000 | tf_op jit(solution)/shard_map/combine/pallas_call | solution.py:302
  95.4 3.7 %collective-permute-start.25 = (bf16[256,384]{1,0:T(8,128)(2,1)}, bf16[256,384]{1,0:T(8,128)(2,1)S(1)}, u32[]{:S(2)}, u32[]{:S(2)}) collective-permute-start(bf16[256,384]{1,0:T(8,128)(2,1)} %get-tuple-element.23.refs_0_), channel_id=1, source_target_pairs={{0,3},{1,0},{2,1},{3,2},{4,7},{5,4},{6,5},{7,6},{8,11},{9,8},{10,9... | collective-permute-start | bytes 589832 | tf_op jit(solution)/shard_map/ppermute | solution.py:375
  99.1 1.9 %collective-permute-start.27 = (bf16[256,384]{1,0:T(8,128)(2,1)}, bf16[256,384]{1,0:T(8,128)(2,1)S(1)}, u32[]{:S(2)}, u32[]{:S(2)}) collective-permute-start(bf16[256,384]{1,0:T(8,128)(2,1)} %get-tuple-element.23.refs_0_), channel_id=1, source_target_pairs={{0,4},{1,5},{2,6},{3,7},{4,0},{5,1},{6,2},{7,3},{8,12},{9,13},{10,... | collective-permute-start | bytes 589832 | tf_op jit(solution)/shard_map/ppermute | solution.py:375
  100.9 1.7 %collective-permute-start.34 = (bf16[256,384]{1,0:T(8,128)(2,1)}, bf16[256,384]{1,0:T(8,128)(2,1)S(1)}, u32[]{:S(2)}, u32[]{:S(2)}) collective-permute-start(bf16[256,384]{1,0:T(8,128)(2,1)} %get-tuple-element.24.refs_8_), channel_id=1, source_target_pairs={{0,4},{1,5},{2,6},{3,7},{4,0},{5,1},{6,2},{7,3},{8,12},{9,13},{10,... | collective-permute-start | bytes 589832 | tf_op jit(solution)/shard_map/ppermute | solution.py:375
  102.6 1.8 %collective-permute-done.24.refs_1_ = bf16[256,384]{1,0:T(8,128)(2,1)S(1)} collective-permute-done((bf16[256,384]{1,0:T(8,128)(2,1)}, bf16[256,384]{1,0:T(8,128)(2,1)S(1)}, u32[]{:S(2)}, u32[]{:S(2)}) %collective-permute-start.24) | collective-permute-done | bytes 196640 | tf_op jit(solution)/shard_map/ppermute | solution.py:375
  104.4 1.7 %collective-permute-start.32 = (bf16[256,384]{1,0:T(8,128)(2,1)}, bf16[256,384]{1,0:T(8,128)(2,1)S(1)}, u32[]{:S(2)}, u32[]{:S(2)}) collective-permute-start(bf16[256,384]{1,0:T(8,128)(2,1)} %get-tuple-element.24.refs_8_), channel_id=1, source_target_pairs={{0,3},{1,0},{2,1},{3,2},{4,7},{5,4},{6,5},{7,6},{8,11},{9,8},{10,9... | collective-permute-start | bytes 589832 | tf_op jit(solution)/shard_map/ppermute | solution.py:375
  106.4 2.2 %collective-permute-done.27.refs_4_ = bf16[256,384]{1,0:T(8,128)(2,1)S(1)} collective-permute-done((bf16[256,384]{1,0:T(8,128)(2,1)}, bf16[256,384]{1,0:T(8,128)(2,1)S(1)}, u32[]{:S(2)}, u32[]{:S(2)}) %collective-permute-start.27) | collective-permute-done | bytes 196640 | tf_op jit(solution)/shard_map/ppermute | solution.py:375
  108.6 3.1 %collective-permute-done.34.refs_12_ = bf16[256,384]{1,0:T(8,128)(2,1)S(1)} collective-permute-done((bf16[256,384]{1,0:T(8,128)(2,1)}, bf16[256,384]{1,0:T(8,128)(2,1)S(1)}, u32[]{:S(2)}, u32[]{:S(2)}) %collective-permute-start.34) | collective-permute-done | bytes 196640 | tf_op jit(solution)/shard_map/ppermute | solution.py:375
  111.6 1.7 %collective-permute-start.36 = (bf16[256,384]{1,0:T(8,128)(2,1)S(1)}, bf16[256,384]{1,0:T(8,128)(2,1)S(1)}, u32[]{:S(2)}, u32[]{:S(2)}) collective-permute-start(bf16[256,384]{1,0:T(8,128)(2,1)S(1)} %collective-permute-done.34.refs_12_), channel_id=1, source_target_pairs={{0,3},{1,0},{2,1},{3,2},{4,7},{5,4},{6,5},{7,6},{8,11},{9,8},{10,9... | collective-permute-start | bytes 589832 | tf_op jit(solution)/shard_map/ppermute | solution.py:375
  113.7 1.6 %collective-permute-start.35 = (bf16[256,384]{1,0:T(8,128)(2,1)S(1)}, bf16[256,384]{1,0:T(8,128)(2,1)S(1)}, u32[]{:S(2)}, u32[]{:S(2)}) collective-permute-start(bf16[256,384]{1,0:T(8,128)(2,1)S(1)} %collective-permute-done.34.refs_12_), channel_id=1, source_target_pairs={{0,1},{1,2},{2,3},{3,0},{4,5},{5,6},{6,7},{7,4},{8,9},{9,10},{10,1... | collective-permute-start | bytes 589832 | tf_op jit(solution)/shard_map/ppermute | solution.py:375
  115.5 1.5 %collective-permute-start.33 = (bf16[256,384]{1,0:T(8,128)(2,1)S(1)}, bf16[256,384]{1,0:T(8,128)(2,1)S(1)}, u32[]{:S(2)}, u32[]{:S(2)}) collective-permute-start(bf16[256,384]{1,0:T(8,128)(2,1)S(1)} %collective-permute-done.32.refs_10_), channel_id=1, source_target_pairs={{0,3},{1,0},{2,1},{3,2},{4,7},{5,4},{6,5},{7,6},{8,11},{9,8},{10,9... | collective-permute-start | bytes 589832 | tf_op jit(solution)/shard_map/ppermute | solution.py:375
  117.0 2.7 %collective-permute-done.28.refs_5_ = bf16[256,384]{1,0:T(8,128)(2,1)S(1)} collective-permute-done((bf16[256,384]{1,0:T(8,128)(2,1)S(1)}, bf16[256,384]{1,0:T(8,128)(2,1)S(1)}, u32[]{:S(2)}, u32[]{:S(2)}) %collective-permute-start.28) | collective-permute-done | bytes 196640 | tf_op jit(solution)/shard_map/ppermute | solution.py:375
  119.7 3.2 %collective-permute-start.37 = (bf16[256,384]{1,0:T(8,128)(2,1)S(1)}, bf16[256,384]{1,0:T(8,128)(2,1)S(1)}, u32[]{:S(2)}, u32[]{:S(2)}) collective-permute-start(bf16[256,384]{1,0:T(8,128)(2,1)S(1)} %collective-permute-done.36.refs_14_), channel_id=1, source_target_pairs={{0,3},{1,0},{2,1},{3,2},{4,7},{5,4},{6,5},{7,6},{8,11},{9,8},{10,9... | collective-permute-start | bytes 589832 | tf_op jit(solution)/shard_map/ppermute | solution.py:375
  122.9 0.6 reshape.44.refs_24_
  123.7 4.2 %collective-permute-done.33.refs_11_ = bf16[256,384]{1,0:T(8,128)(2,1)S(1)} collective-permute-done((bf16[256,384]{1,0:T(8,128)(2,1)S(1)}, bf16[256,384]{1,0:T(8,128)(2,1)S(1)}, u32[]{:S(2)}, u32[]{:S(2)}) %collective-permute-start.33) | collective-permute-done | bytes 196640 | tf_op jit(solution)/shard_map/ppermute | solution.py:375
  127.9 2.1 %collective-permute-done.37.refs_15_ = bf16[256,384]{1,0:T(8,128)(2,1)S(1)} collective-permute-done((bf16[256,384]{1,0:T(8,128)(2,1)S(1)}, bf16[256,384]{1,0:T(8,128)(2,1)S(1)}, u32[]{:S(2)}, u32[]{:S(2)}) %collective-permute-start.37) | collective-permute-done | bytes 196640 | tf_op jit(solution)/shard_map/ppermute | solution.py:375
  130.2 0.5 copy-done.24
  130.8 6.1 %output.1 = bf16[512,384]{1,0:T(8,128)(2,1)} custom-call(s32[1]{0:T(128)} %bitcast.core_ref, bf16[256,384]{1,0:T(8,128)(2,1)} %get-tuple-element.23.refs_0_, bf16[256,384]{1,0:T(8,128)(2,1)} %copy-done.11, bf16[256,384]{1,0:T(8,128)(2,1)} %copy-done.12, bf16[256,384]{1,0:T(8,128)(2,1)} %copy-done.17, bf16[256,384]{1,0:T(8,128)(2,1)} %copy-done.13, ...), custom_call_target="tpu_custom_call" | custom-call | flops 1207959552 | bytes 6000000 | tf_op jit(solution)/shard_map/output/pallas_call | solution.py:354
  (144 shorter events, 6.1 us)
Async XLA Ops:
  0.0 47.5 %copy-start = (s32[16,4,4,2]{0,3,2,1:T(2,128)S(1)}, s32[16,4,4,2]{0,3,2,1:T(2,128)}, u32[]{:S(2)}) copy-start(s32[16,4,4,2]{0,3,2,1:T(2,128)} %param.19) | copy-start | bytes 6148
  11.1 9.5 %collective-permute-start = (bf16[2,256,256]{2,1,0:T(8,128)(2,1)}, bf16[2,256,256]{2,1,0:T(8,128)(2,1)S(1)}, u32[]{:S(2)}, u32[]{:S(2)}) collective-permute-start(bf16[2,256,256]{2,1,0:T(8,128)(2,1)} %get-tuple-element.16), channel_id=1, source_target_pairs={{0,8},{8,0},{1,9},{9,1},{2,10},{10,2},{3,11},{11,3},{4,12},{12,4},... | collective-permute-start | bytes 786440 | tf_op jit(solution)/shard_map/ppermute | solution.py:375
  12.8 12.1 %collective-permute-start.1 = (bf16[2,256,256]{2,1,0:T(8,128)(2,1)}, bf16[2,256,256]{2,1,0:T(8,128)(2,1)S(1)}, u32[]{:S(2)}, u32[]{:S(2)}) collective-permute-start(bf16[2,256,256]{2,1,0:T(8,128)(2,1)} %get-tuple-element.19), channel_id=1, source_target_pairs={{0,8},{8,0},{1,9},{9,1},{2,10},{10,2},{3,11},{11,3},{4,12},{12,4},... | collective-permute-start | bytes 786440 | tf_op jit(solution)/shard_map/ppermute | solution.py:375
  13.2 12.5 %collective-permute-start.2 = (bf16[2,256,256]{2,1,0:T(8,128)(2,1)}, bf16[2,256,256]{2,1,0:T(8,128)(2,1)}, u32[]{:S(2)}, u32[]{:S(2)}) collective-permute-start(bf16[2,256,256]{2,1,0:T(8,128)(2,1)} %get-tuple-element.17.refs_2_), channel_id=1, source_target_pairs={{0,32},{16,48},{32,64},{48,80},{64,96},{80,112},{96,0},{112,16},{1... | collective-permute-start | bytes 786440 | tf_op jit(solution)/shard_map/ppermute | solution.py:375
  14.9 14.4 %collective-permute-start.5 = (bf16[2,256,256]{2,1,0:T(8,128)(2,1)}, bf16[2,256,256]{2,1,0:T(8,128)(2,1)}, u32[]{:S(2)}, u32[]{:S(2)}) collective-permute-start(bf16[2,256,256]{2,1,0:T(8,128)(2,1)} %get-tuple-element.17.refs_2_), channel_id=1, source_target_pairs={{0,96},{16,112},{32,0},{48,16},{64,32},{80,48},{96,64},{112,80},{1... | collective-permute-start | bytes 786440 | tf_op jit(solution)/shard_map/ppermute | solution.py:375
  16.5 12.6 %collective-permute-start.3 = (bf16[2,256,256]{2,1,0:T(8,128)(2,1)}, bf16[2,256,256]{2,1,0:T(8,128)(2,1)}, u32[]{:S(2)}, u32[]{:S(2)}) collective-permute-start(bf16[2,256,256]{2,1,0:T(8,128)(2,1)} %get-tuple-element.18.refs_3_), channel_id=1, source_target_pairs={{0,32},{16,48},{32,64},{48,80},{64,96},{80,112},{96,0},{112,16},{1... | collective-permute-start | bytes 786440 | tf_op jit(solution)/shard_map/ppermute | solution.py:375
  20.6 10.3 %collective-permute-start.6 = (bf16[2,256,256]{2,1,0:T(8,128)(2,1)}, bf16[2,256,256]{2,1,0:T(8,128)(2,1)}, u32[]{:S(2)}, u32[]{:S(2)}) collective-permute-start(bf16[2,256,256]{2,1,0:T(8,128)(2,1)} %get-tuple-element.18.refs_3_), channel_id=1, source_target_pairs={{0,96},{16,112},{32,0},{48,16},{64,32},{80,48},{96,64},{112,80},{1... | collective-permute-start | bytes 786440 | tf_op jit(solution)/shard_map/ppermute | solution.py:375
  25.6 6.9 %collective-permute-start.11 = (bf16[2,256,256]{2,1,0:T(8,128)(2,1)}, bf16[2,256,256]{2,1,0:T(8,128)(2,1)S(1)}, u32[]{:S(2)}, u32[]{:S(2)}) collective-permute-start(bf16[2,256,256]{2,1,0:T(8,128)(2,1)} %get-tuple-element.17.refs_2_), channel_id=1, source_target_pairs={{0,16},{16,0},{32,48},{48,32},{64,80},{80,64},{96,112},{112,96},{1... | collective-permute-start | bytes 786440 | tf_op jit(solution)/shard_map/ppermute | solution.py:375
  25.7 21.2 %collective-permute-start.38 = (bf16[192,1536]{1,0:T(8,128)(2,1)S(1)}, bf16[192,1536]{1,0:T(8,128)(2,1)S(1)}, u32[]{:S(2)}, u32[]{:S(2)}) collective-permute-start(bf16[192,1536]{1,0:T(8,128)(2,1)S(1)} %get-tuple-element.27), channel_id=1, source_target_pairs={{0,4},{1,5},{2,6},{3,7},{4,0},{5,1},{6,2},{7,3},{8,12},{9,13},{10,... | collective-permute-start | bytes 1769480 | tf_op jit(solution)/shard_map/ppermute | solution.py:375
  29.1 3.8 %collective-permute-start.12 = (bf16[2,256,256]{2,1,0:T(8,128)(2,1)S(1)}, bf16[2,256,256]{2,1,0:T(8,128)(2,1)S(1)}, u32[]{:S(2)}, u32[]{:S(2)}) collective-permute-start(bf16[2,256,256]{2,1,0:T(8,128)(2,1)S(1)} %copy-done.26), channel_id=1, source_target_pairs={{0,16},{16,0},{32,48},{48,32},{64,80},{80,64},{96,112},{112,96},{1... | collective-permute-start | bytes 786440 | tf_op jit(solution)/shard_map/ppermute | solution.py:375
  29.3 10.3 %collective-permute-start.4 = (bf16[2,256,256]{2,1,0:T(8,128)(2,1)S(1)}, bf16[2,256,256]{2,1,0:T(8,128)(2,1)S(1)}, u32[]{:S(2)}, u32[]{:S(2)}) collective-permute-start(bf16[2,256,256]{2,1,0:T(8,128)(2,1)S(1)} %copy-done.29), channel_id=1, source_target_pairs={{0,32},{16,48},{32,64},{48,80},{64,96},{80,112},{96,0},{112,16},{1... | collective-permute-start | bytes 786440 | tf_op jit(solution)/shard_map/ppermute | solution.py:375
  30.9 9.2 %collective-permute-start.7 = (bf16[2,256,256]{2,1,0:T(8,128)(2,1)S(1)}, bf16[2,256,256]{2,1,0:T(8,128)(2,1)S(1)}, u32[]{:S(2)}, u32[]{:S(2)}) collective-permute-start(bf16[2,256,256]{2,1,0:T(8,128)(2,1)S(1)} %copy-done.29), channel_id=1, source_target_pairs={{0,96},{16,112},{32,0},{48,16},{64,32},{80,48},{96,64},{112,80},{1... | collective-permute-start | bytes 786440 | tf_op jit(solution)/shard_map/ppermute | solution.py:375
  32.6 12.2 %collective-permute-start.8 = (bf16[2,256,256]{2,1,0:T(8,128)(2,1)}, bf16[2,256,256]{2,1,0:T(8,128)(2,1)S(1)}, u32[]{:S(2)}, u32[]{:S(2)}) collective-permute-start(bf16[2,256,256]{2,1,0:T(8,128)(2,1)} %collective-permute-done.2.refs_5_), channel_id=1, source_target_pairs={{0,32},{16,48},{32,64},{48,80},{64,96},{80,112},{96,0},{112,16},{1... | collective-permute-start | bytes 786440 | tf_op jit(solution)/shard_map/ppermute | solution.py:375
  32.9 11.9 %collective-permute-start.9 = (bf16[2,256,256]{2,1,0:T(8,128)(2,1)}, bf16[2,256,256]{2,1,0:T(8,128)(2,1)}, u32[]{:S(2)}, u32[]{:S(2)}) collective-permute-start(bf16[2,256,256]{2,1,0:T(8,128)(2,1)} %collective-permute-done.6.refs_9_), channel_id=1, source_target_pairs={{0,96},{16,112},{32,0},{48,16},{64,32},{80,48},{96,64},{112,80},{1... | collective-permute-start | bytes 786440 | tf_op jit(solution)/shard_map/ppermute | solution.py:375
  39.7 5.6 %collective-permute-start.13 = (bf16[2,256,256]{2,1,0:T(8,128)(2,1)S(1)}, bf16[2,256,256]{2,1,0:T(8,128)(2,1)S(1)}, u32[]{:S(2)}, u32[]{:S(2)}) collective-permute-start(bf16[2,256,256]{2,1,0:T(8,128)(2,1)S(1)} %copy-done.29), channel_id=1, source_target_pairs={{0,16},{16,0},{32,48},{48,32},{64,80},{80,64},{96,112},{112,96},{1... | collective-permute-start | bytes 786440 | tf_op jit(solution)/shard_map/ppermute | solution.py:375
  40.1 5.4 %collective-permute-start.14 = (bf16[2,256,256]{2,1,0:T(8,128)(2,1)}, bf16[2,256,256]{2,1,0:T(8,128)(2,1)S(1)}, u32[]{:S(2)}, u32[]{:S(2)}) collective-permute-start(bf16[2,256,256]{2,1,0:T(8,128)(2,1)} %collective-permute-done.2.refs_5_), channel_id=1, source_target_pairs={{0,16},{16,0},{32,48},{48,32},{64,80},{80,64},{96,112},{112,96},{1... | collective-permute-start | bytes 786440 | tf_op jit(solution)/shard_map/ppermute | solution.py:375
  44.7 2.2 %collective-permute-start.15 = (bf16[2,256,256]{2,1,0:T(8,128)(2,1)}, bf16[2,256,256]{2,1,0:T(8,128)(2,1)S(1)}, u32[]{:S(2)}, u32[]{:S(2)}) collective-permute-start(bf16[2,256,256]{2,1,0:T(8,128)(2,1)} %collective-permute-done.3.refs_6_), channel_id=1, source_target_pairs={{0,16},{16,0},{32,48},{48,32},{64,80},{80,64},{96,112},{112,96},{1... | collective-permute-start | bytes 786440 | tf_op jit(solution)/shard_map/ppermute | solution.py:375
  44.8 3.0 %collective-permute-start.17 = (bf16[2,256,256]{2,1,0:T(8,128)(2,1)}, bf16[2,256,256]{2,1,0:T(8,128)(2,1)}, u32[]{:S(2)}, u32[]{:S(2)}) collective-permute-start(bf16[2,256,256]{2,1,0:T(8,128)(2,1)} %collective-permute-done.5.refs_8_), channel_id=1, source_target_pairs={{0,16},{16,0},{32,48},{48,32},{64,80},{80,64},{96,112},{112,96},{1... | collective-permute-start | bytes 786440 | tf_op jit(solution)/shard_map/ppermute | solution.py:375
  45.2 3.5 %collective-permute-start.18 = (bf16[2,256,256]{2,1,0:T(8,128)(2,1)}, bf16[2,256,256]{2,1,0:T(8,128)(2,1)}, u32[]{:S(2)}, u32[]{:S(2)}) collective-permute-start(bf16[2,256,256]{2,1,0:T(8,128)(2,1)} %collective-permute-done.6.refs_9_), channel_id=1, source_target_pairs={{0,16},{16,0},{32,48},{48,32},{64,80},{80,64},{96,112},{112,96},{1... | collective-permute-start | bytes 786440 | tf_op jit(solution)/shard_map/ppermute | solution.py:375
  45.5 9.8 %collective-permute-start.10 = (bf16[2,256,256]{2,1,0:T(8,128)(2,1)S(1)}, bf16[2,256,256]{2,1,0:T(8,128)(2,1)}, u32[]{:S(2)}, u32[]{:S(2)}) collective-permute-start(bf16[2,256,256]{2,1,0:T(8,128)(2,1)S(1)} %collective-permute-done.4.refs_7_), channel_id=1, source_target_pairs={{0,32},{16,48},{32,64},{48,80},{64,96},{80,112},{96,0},{112,16},{1... | collective-permute-start | bytes 786440 | tf_op jit(solution)/shard_map/ppermute | solution.py:375
  47.0 10.2 %collective-permute-start.16 = (bf16[2,256,256]{2,1,0:T(8,128)(2,1)S(1)}, bf16[2,256,256]{2,1,0:T(8,128)(2,1)}, u32[]{:S(2)}, u32[]{:S(2)}) collective-permute-start(bf16[2,256,256]{2,1,0:T(8,128)(2,1)S(1)} %collective-permute-done.4.refs_7_), channel_id=1, source_target_pairs={{0,16},{16,0},{32,48},{48,32},{64,80},{80,64},{96,112},{112,96},{1... | collective-permute-start | bytes 786440 | tf_op jit(solution)/shard_map/ppermute | solution.py:375
  47.0 12.3 %collective-permute-start.19 = (bf16[2,256,256]{2,1,0:T(8,128)(2,1)S(1)}, bf16[2,256,256]{2,1,0:T(8,128)(2,1)}, u32[]{:S(2)}, u32[]{:S(2)}) collective-permute-start(bf16[2,256,256]{2,1,0:T(8,128)(2,1)S(1)} %collective-permute-done.7.refs_10_), channel_id=1, source_target_pairs={{0,16},{16,0},{32,48},{48,32},{64,80},{80,64},{96,112},{112,96},{1... | collective-permute-start | bytes 786440 | tf_op jit(solution)/shard_map/ppermute | solution.py:375
  48.6 11.8 %collective-permute-start.20 = (bf16[2,256,256]{2,1,0:T(8,128)(2,1)S(1)}, bf16[2,256,256]{2,1,0:T(8,128)(2,1)S(1)}, u32[]{:S(2)}, u32[]{:S(2)}) collective-permute-start(bf16[2,256,256]{2,1,0:T(8,128)(2,1)S(1)} %copy-done.35), channel_id=1, source_target_pairs={{0,16},{16,0},{32,48},{48,32},{64,80},{80,64},{96,112},{112,96},{1... | collective-permute-start | bytes 786440 | tf_op jit(solution)/shard_map/ppermute | solution.py:375
  48.7 13.6 %collective-permute-start.21 = (bf16[2,256,256]{2,1,0:T(8,128)(2,1)}, bf16[2,256,256]{2,1,0:T(8,128)(2,1)S(1)}, u32[]{:S(2)}, u32[]{:S(2)}) collective-permute-start(bf16[2,256,256]{2,1,0:T(8,128)(2,1)} %collective-permute-done.9.refs_12_), channel_id=1, source_target_pairs={{0,16},{16,0},{32,48},{48,32},{64,80},{80,64},{96,112},{112,96},{1... | collective-permute-start | bytes 786440 | tf_op jit(solution)/shard_map/ppermute | solution.py:375
  55.3 11.1 %collective-permute-start.39 = (bf16[2,192,384]{2,1,0:T(8,128)(2,1)S(1)}, bf16[2,192,384]{2,1,0:T(8,128)(2,1)S(1)}, u32[]{:S(2)}, u32[]{:S(2)}) collective-permute-start(bf16[2,192,384]{2,1,0:T(8,128)(2,1)S(1)} %get-tuple-element.31), channel_id=1, source_target_pairs={{0,1},{1,2},{2,3},{3,0},{4,5},{5,6},{6,7},{7,4},{8,9},{9,10},{10,1... | collective-permute-start | bytes 884744 | tf_op jit(solution)/shard_map/ppermute | solution.py:375
  57.2 14.3 %collective-permute-start.40 = (bf16[2,192,384]{2,1,0:T(8,128)(2,1)S(1)}, bf16[2,192,384]{2,1,0:T(8,128)(2,1)S(1)}, u32[]{:S(2)}, u32[]{:S(2)}) collective-permute-start(bf16[2,192,384]{2,1,0:T(8,128)(2,1)S(1)} %get-tuple-element.32), channel_id=1, source_target_pairs={{0,3},{1,0},{2,1},{3,2},{4,7},{5,4},{6,5},{7,6},{8,11},{9,8},{10,9... | collective-permute-start | bytes 884744 | tf_op jit(solution)/shard_map/ppermute | solution.py:375
  59.3 12.2 %collective-permute-start.22 = (bf16[2,256,256]{2,1,0:T(8,128)(2,1)}, bf16[2,256,256]{2,1,0:T(8,128)(2,1)S(1)}, u32[]{:S(2)}, u32[]{:S(2)}) collective-permute-start(bf16[2,256,256]{2,1,0:T(8,128)(2,1)} %collective-permute-done.10.refs_13_), channel_id=1, source_target_pairs={{0,16},{16,0},{32,48},{48,32},{64,80},{80,64},{96,112},{112,96},{1... | collective-permute-start | bytes 786440 | tf_op jit(solution)/shard_map/ppermute | solution.py:375
  60.5 23.0 %collective-permute-start.41 = (bf16[2,192,384]{2,1,0:T(8,128)(2,1)S(1)}, bf16[2,192,384]{2,1,0:T(8,128)(2,1)S(1)}, u32[]{:S(2)}, u32[]{:S(2)}) collective-permute-start(bf16[2,192,384]{2,1,0:T(8,128)(2,1)S(1)} %get-tuple-element.29), channel_id=1, source_target_pairs={{0,2},{1,3},{2,0},{3,1},{4,6},{5,7},{6,4},{7,5},{8,10},{9,11},{10,... | collective-permute-start | bytes 884744 | tf_op jit(solution)/shard_map/ppermute | solution.py:375
  63.0 32.3 %collective-permute-start.42 = (bf16[2,192,384]{2,1,0:T(8,128)(2,1)S(1)}, bf16[2,192,384]{2,1,0:T(8,128)(2,1)S(1)}, u32[]{:S(2)}, u32[]{:S(2)}) collective-permute-start(bf16[2,192,384]{2,1,0:T(8,128)(2,1)S(1)} %get-tuple-element.30.refs_16_), channel_id=1, source_target_pairs={{0,16},{16,0},{32,48},{48,32},{64,80},{80,64},{96,112},{112,96},{1... | collective-permute-start | bytes 884744 | tf_op jit(solution)/shard_map/ppermute | solution.py:375
  66.3 32.7 %collective-permute-start.43 = (bf16[2,192,384]{2,1,0:T(8,128)(2,1)S(1)}, bf16[2,192,384]{2,1,0:T(8,128)(2,1)S(1)}, u32[]{:S(2)}, u32[]{:S(2)}) collective-permute-start(bf16[2,192,384]{2,1,0:T(8,128)(2,1)S(1)} %collective-permute-done.39.refs_17_), channel_id=1, source_target_pairs={{0,16},{16,0},{32,48},{48,32},{64,80},{80,64},{96,112},{112,96},{1... | collective-permute-start | bytes 884744 | tf_op jit(solution)/shard_map/ppermute | solution.py:375
  71.5 29.4 %collective-permute-start.44 = (bf16[2,192,384]{2,1,0:T(8,128)(2,1)S(1)}, bf16[2,192,384]{2,1,0:T(8,128)(2,1)S(1)}, u32[]{:S(2)}, u32[]{:S(2)}) collective-permute-start(bf16[2,192,384]{2,1,0:T(8,128)(2,1)S(1)} %collective-permute-done.40.refs_18_), channel_id=1, source_target_pairs={{0,16},{16,0},{32,48},{48,32},{64,80},{80,64},{96,112},{112,96},{1... | collective-permute-start | bytes 884744 | tf_op jit(solution)/shard_map/ppermute | solution.py:375
  72.3 50.7 %copy-start.25 = (f32[384]{0:T(512)S(1)}, f32[384]{0:T(512)}, u32[]{:S(2)}) copy-start(f32[384]{0:T(512)} %param.15) | copy-start | bytes 4612
  82.8 9.7 %collective-permute-start.23 = (bf16[2,272,256]{2,1,0:T(8,128)(2,1)}, bf16[2,272,256]{2,1,0:T(8,128)(2,1)S(1)}, u32[]{:S(2)}, u32[]{:S(2)}) collective-permute-start(bf16[2,272,256]{2,1,0:T(8,128)(2,1)} %get-tuple-element.22), channel_id=1, source_target_pairs={{0,8},{8,0},{1,9},{9,1},{2,10},{10,2},{3,11},{11,3},{4,12},{12,4},... | collective-permute-start | bytes 835592 | tf_op jit(solution)/shard_map/ppermute | solution.py:375
  83.5 19.1 %collective-permute-start.45 = (bf16[2,192,384]{2,1,0:T(8,128)(2,1)S(1)}, bf16[2,192,384]{2,1,0:T(8,128)(2,1)S(1)}, u32[]{:S(2)}, u32[]{:S(2)}) collective-permute-start(bf16[2,192,384]{2,1,0:T(8,128)(2,1)S(1)} %collective-permute-done.41.refs_19_), channel_id=1, source_target_pairs={{0,16},{16,0},{32,48},{48,32},{64,80},{80,64},{96,112},{112,96},{1... | collective-permute-start | bytes 884744 | tf_op jit(solution)/shard_map/ppermute | solution.py:375
  95.3 9.1 %collective-permute-start.24 = (bf16[256,384]{1,0:T(8,128)(2,1)}, bf16[256,384]{1,0:T(8,128)(2,1)S(1)}, u32[]{:S(2)}, u32[]{:S(2)}) collective-permute-start(bf16[256,384]{1,0:T(8,128)(2,1)} %get-tuple-element.23.refs_0_), channel_id=1, source_target_pairs={{0,1},{1,2},{2,3},{3,0},{4,5},{5,6},{6,7},{7,4},{8,9},{9,10},{10,1... | collective-permute-start | bytes 589832 | tf_op jit(solution)/shard_map/ppermute | solution.py:375
  95.4 10.7 %collective-permute-start.25 = (bf16[256,384]{1,0:T(8,128)(2,1)}, bf16[256,384]{1,0:T(8,128)(2,1)S(1)}, u32[]{:S(2)}, u32[]{:S(2)}) collective-permute-start(bf16[256,384]{1,0:T(8,128)(2,1)} %get-tuple-element.23.refs_0_), channel_id=1, source_target_pairs={{0,3},{1,0},{2,1},{3,2},{4,7},{5,4},{6,5},{7,6},{8,11},{9,8},{10,9... | collective-permute-start | bytes 589832 | tf_op jit(solution)/shard_map/ppermute | solution.py:375
  99.1 9.5 %collective-permute-start.27 = (bf16[256,384]{1,0:T(8,128)(2,1)}, bf16[256,384]{1,0:T(8,128)(2,1)S(1)}, u32[]{:S(2)}, u32[]{:S(2)}) collective-permute-start(bf16[256,384]{1,0:T(8,128)(2,1)} %get-tuple-element.23.refs_0_), channel_id=1, source_target_pairs={{0,4},{1,5},{2,6},{3,7},{4,0},{5,1},{6,2},{7,3},{8,12},{9,13},{10,... | collective-permute-start | bytes 589832 | tf_op jit(solution)/shard_map/ppermute | solution.py:375
  100.9 10.7 %collective-permute-start.34 = (bf16[256,384]{1,0:T(8,128)(2,1)}, bf16[256,384]{1,0:T(8,128)(2,1)S(1)}, u32[]{:S(2)}, u32[]{:S(2)}) collective-permute-start(bf16[256,384]{1,0:T(8,128)(2,1)} %get-tuple-element.24.refs_8_), channel_id=1, source_target_pairs={{0,4},{1,5},{2,6},{3,7},{4,0},{5,1},{6,2},{7,3},{8,12},{9,13},{10,... | collective-permute-start | bytes 589832 | tf_op jit(solution)/shard_map/ppermute | solution.py:375
  102.6 10.7 %collective-permute-start.31 = (bf16[256,384]{1,0:T(8,128)(2,1)}, bf16[256,384]{1,0:T(8,128)(2,1)S(1)}, u32[]{:S(2)}, u32[]{:S(2)}) collective-permute-start(bf16[256,384]{1,0:T(8,128)(2,1)} %get-tuple-element.24.refs_8_), channel_id=1, source_target_pairs={{0,1},{1,2},{2,3},{3,0},{4,5},{5,6},{6,7},{7,4},{8,9},{9,10},{10,1... | collective-permute-start | bytes 589832 | tf_op jit(solution)/shard_map/ppermute | solution.py:375
  104.4 9.3 %collective-permute-start.32 = (bf16[256,384]{1,0:T(8,128)(2,1)}, bf16[256,384]{1,0:T(8,128)(2,1)S(1)}, u32[]{:S(2)}, u32[]{:S(2)}) collective-permute-start(bf16[256,384]{1,0:T(8,128)(2,1)} %get-tuple-element.24.refs_8_), channel_id=1, source_target_pairs={{0,3},{1,0},{2,1},{3,2},{4,7},{5,4},{6,5},{7,6},{8,11},{9,8},{10,9... | collective-permute-start | bytes 589832 | tf_op jit(solution)/shard_map/ppermute | solution.py:375
  106.1 9.3 %collective-permute-start.26 = (bf16[256,384]{1,0:T(8,128)(2,1)S(1)}, bf16[256,384]{1,0:T(8,128)(2,1)S(1)}, u32[]{:S(2)}, u32[]{:S(2)}) collective-permute-start(bf16[256,384]{1,0:T(8,128)(2,1)S(1)} %collective-permute-done.24.refs_1_), channel_id=1, source_target_pairs={{0,1},{1,2},{2,3},{3,0},{4,5},{5,6},{6,7},{7,4},{8,9},{9,10},{10,1... | collective-permute-start | bytes 589832 | tf_op jit(solution)/shard_map/ppermute | solution.py:375
  108.6 11.1 %collective-permute-start.28 = (bf16[256,384]{1,0:T(8,128)(2,1)S(1)}, bf16[256,384]{1,0:T(8,128)(2,1)S(1)}, u32[]{:S(2)}, u32[]{:S(2)}) collective-permute-start(bf16[256,384]{1,0:T(8,128)(2,1)S(1)} %collective-permute-done.27.refs_4_), channel_id=1, source_target_pairs={{0,1},{1,2},{2,3},{3,0},{4,5},{5,6},{6,7},{7,4},{8,9},{9,10},{10,1... | collective-permute-start | bytes 589832 | tf_op jit(solution)/shard_map/ppermute | solution.py:375
  111.6 8.0 %collective-permute-start.36 = (bf16[256,384]{1,0:T(8,128)(2,1)S(1)}, bf16[256,384]{1,0:T(8,128)(2,1)S(1)}, u32[]{:S(2)}, u32[]{:S(2)}) collective-permute-start(bf16[256,384]{1,0:T(8,128)(2,1)S(1)} %collective-permute-done.34.refs_12_), channel_id=1, source_target_pairs={{0,3},{1,0},{2,1},{3,2},{4,7},{5,4},{6,5},{7,6},{8,11},{9,8},{10,9... | collective-permute-start | bytes 589832 | tf_op jit(solution)/shard_map/ppermute | solution.py:375
  113.3 10.4 %collective-permute-start.29 = (bf16[256,384]{1,0:T(8,128)(2,1)S(1)}, bf16[256,384]{1,0:T(8,128)(2,1)S(1)}, u32[]{:S(2)}, u32[]{:S(2)}) collective-permute-start(bf16[256,384]{1,0:T(8,128)(2,1)S(1)} %collective-permute-done.27.refs_4_), channel_id=1, source_target_pairs={{0,3},{1,0},{2,1},{3,2},{4,7},{5,4},{6,5},{7,6},{8,11},{9,8},{10,9... | collective-permute-start | bytes 589832 | tf_op jit(solution)/shard_map/ppermute | solution.py:375
  113.7 14.2 %collective-permute-start.35 = (bf16[256,384]{1,0:T(8,128)(2,1)S(1)}, bf16[256,384]{1,0:T(8,128)(2,1)S(1)}, u32[]{:S(2)}, u32[]{:S(2)}) collective-permute-start(bf16[256,384]{1,0:T(8,128)(2,1)S(1)} %collective-permute-done.34.refs_12_), channel_id=1, source_target_pairs={{0,1},{1,2},{2,3},{3,0},{4,5},{5,6},{6,7},{7,4},{8,9},{9,10},{10,1... | collective-permute-start | bytes 589832 | tf_op jit(solution)/shard_map/ppermute | solution.py:375
  115.5 12.4 %collective-permute-start.33 = (bf16[256,384]{1,0:T(8,128)(2,1)S(1)}, bf16[256,384]{1,0:T(8,128)(2,1)S(1)}, u32[]{:S(2)}, u32[]{:S(2)}) collective-permute-start(bf16[256,384]{1,0:T(8,128)(2,1)S(1)} %collective-permute-done.32.refs_10_), channel_id=1, source_target_pairs={{0,3},{1,0},{2,1},{3,2},{4,7},{5,4},{6,5},{7,6},{8,11},{9,8},{10,9... | collective-permute-start | bytes 589832 | tf_op jit(solution)/shard_map/ppermute | solution.py:375
  119.7 8.2 %collective-permute-start.30 = (bf16[256,384]{1,0:T(8,128)(2,1)S(1)}, bf16[256,384]{1,0:T(8,128)(2,1)S(1)}, u32[]{:S(2)}, u32[]{:S(2)}) collective-permute-start(bf16[256,384]{1,0:T(8,128)(2,1)S(1)} %collective-permute-done.28.refs_5_), channel_id=1, source_target_pairs={{0,1},{1,2},{2,3},{3,0},{4,5},{5,6},{6,7},{7,4},{8,9},{9,10},{10,1... | collective-permute-start | bytes 589832 | tf_op jit(solution)/shard_map/ppermute | solution.py:375
  119.7 10.3 %collective-permute-start.37 = (bf16[256,384]{1,0:T(8,128)(2,1)S(1)}, bf16[256,384]{1,0:T(8,128)(2,1)S(1)}, u32[]{:S(2)}, u32[]{:S(2)}) collective-permute-start(bf16[256,384]{1,0:T(8,128)(2,1)S(1)} %collective-permute-done.36.refs_14_), channel_id=1, source_target_pairs={{0,3},{1,0},{2,1},{3,2},{4,7},{5,4},{6,5},{7,6},{8,11},{9,8},{10,9... | collective-permute-start | bytes 589832 | tf_op jit(solution)/shard_map/ppermute | solution.py:375
  (41 other events, 530.4 us)

commit v2 on v1

v2 whole, which is shorter than its diff:
```python
import functools

import jax
import jax.numpy as jnp
from jax import lax
from jax.experimental import pallas as pl
from jax.experimental.pallas import tpu as pltpu
from jax.sharding import PartitionSpec as P

HEAD_DIM = 128
TILE = 128
NORM_EPS = 1e-06
LOG2E = 1.4426950408889634
ANY = pl.BlockSpec(memory_space=pl.ANY)
VMEM = pl.BlockSpec(memory_space=pltpu.VMEM)
SMEM = pl.BlockSpec(memory_space=pltpu.SMEM)
PARAMS = pltpu.CompilerParams(vmem_limit_bytes=56 * 1024 * 1024)
F32 = jnp.float32
BF16 = jnp.bfloat16


def rows_dot(a, b):
    return lax.dot_general(a, b, (((1,), (1,)), ((), ())), preferred_element_type=F32)


def rms_norm(part, gain):
    squares = jnp.mean(part * part, axis=-1, keepdims=True)
    return (part * lax.rsqrt(squares + NORM_EPS) * gain).astype(BF16)


def split_heads(full, gain_row, first):
    parts = [full[:, h * HEAD_DIM:(h + 1) * HEAD_DIM] for h in range(3)]
    if gain_row is None:
        parts = [part.astype(BF16) for part in parts]
    else:
        parts = [rms_norm(part, gain_row) for part in parts]
    own = jnp.where(first, parts[0], parts[2])
    other = jnp.where(first, parts[2], parts[0])
    shape = (2, full.shape[0] // 2, HEAD_DIM)
    return own.reshape(shape), parts[1].reshape(shape), other.reshape(shape)


def project_kernel(
    place_ref, x_ref, w_ref, w_out_ref, scale_ref, shift_ref, qg_ref, kg_ref,
    kept_ref, sent_ref, home_ref, q_sent_ref, ahead_ref, apart_ref,
    n_scr, x_scr, w_scr, o_scr, x_sem, w_sem, o_sem,
):
    rows, width = x_scr.shape
    chunk = rows // 8
    x_copies = [
        pltpu.make_async_copy(
            x_ref.at[pl.ds(i * chunk, chunk)], x_scr.at[pl.ds(i * chunk, chunk)], x_sem.at[i]
        )
        for i in range(8)
    ]
    w_copies = [pltpu.make_async_copy(w_ref.at[j], w_scr.at[j], w_sem.at[j]) for j in range(3)]
    o_load = pltpu.make_async_copy(w_out_ref, o_scr, o_sem.at[0])
    for copy in x_copies + [w_copies[1], w_copies[2], w_copies[0], o_load]:
        copy.start()
    gain = 1.0 + scale_ref[...]
    shift = shift_ref[...]
    for i in range(8):
        x_copies[i].wait()

        def one_block(step, carry, base=i * chunk):
            at = pl.ds(pl.multiple_of(base + step * 16, 16), 16)
            x = x_scr[at, :].astype(F32)
            centred = x - jnp.mean(x, axis=1, keepdims=True)
            var = jnp.mean(centred * centred, axis=1, keepdims=True)
            n_scr[at, :] = (centred * lax.rsqrt(var + NORM_EPS) * gain + shift).astype(BF16)
            return carry

        lax.fori_loop(0, chunk // 16, one_block, 0, unroll=True)
    first = place_ref[0] == 0
    lanes = (slice(0, HEAD_DIM), slice(HEAD_DIM, 2 * HEAD_DIM), slice(2 * HEAD_DIM, 3 * HEAD_DIM),
             slice(3 * HEAD_DIM, 4 * HEAD_DIM))
    o_copies = []
    for j, gain_row in ((1, kg_ref[...]), (2, None), (0, qg_ref[...])):
        w_copies[j].wait()
        full = jnp.dot(n_scr[...], w_scr[j], preferred_element_type=F32)
        own, mid, other = split_heads(full, gain_row, first)
        if j == 0:
            home_ref[:, :, lanes[0]] = own
            home_ref[:, :, lanes[1]] = mid
            q_sent_ref[:, :, lanes[0]] = other
            q_sent_ref[:, :, lanes[1]] = mid
        else:
            kept_ref[:, :, lanes[j - 1]] = own
            kept_ref[:, :, lanes[j + 1]] = mid
            sent_ref[:, :, lanes[j - 1]] = other
        if j == 1:
            o_load.wait()
            cols, part = ahead_ref.shape[1] // 2, apart_ref.shape[0]
            for k in range(2):
                ahead = pl.ds(pl.multiple_of(place_ref[2 + k] * cols, TILE), cols)
                apart = pl.ds(pl.multiple_of(place_ref[4 + k] * cols, TILE), cols)
                half = pl.ds(pl.multiple_of(place_ref[1] * part, 16), part)
                to = pl.ds(k * cols, cols)
                o_copies += [
                    pltpu.make_async_copy(
                        o_scr.at[:, ahead], ahead_ref.at[:, to], o_sem.at[1 + 2 * k]
                    ),
                    pltpu.make_async_copy(
                        o_scr.at[half, apart], apart_ref.at[:, to], o_sem.at[2 + 2 * k]
                    ),
                ]
            for copy in o_copies:
                copy.start()
    for copy in o_copies:
        copy.wait()


def project(place, tokens, w, w_out, scale, shift, q_gain, k_gain):
    frames, half_tok, width = tokens.shape
    rows = frames * half_tok
    depth, cols = w_out.shape[0], w_out.shape[1] // 4
    piece = jax.ShapeDtypeStruct((frames, half_tok, 2 * HEAD_DIM), BF16)
    return pl.pallas_call(
        project_kernel,
        out_shape=[
            jax.ShapeDtypeStruct((frames, half_tok, 4 * HEAD_DIM), BF16),
            piece, piece, piece,
            jax.ShapeDtypeStruct((depth, cols), BF16),
            jax.ShapeDtypeStruct((depth // 2, cols), BF16),
        ],
        in_specs=[SMEM, ANY, ANY, ANY] + [VMEM] * 4,
        out_specs=[VMEM] * 4 + [ANY] * 2,
        scratch_shapes=[
            pltpu.VMEM((rows, width), BF16),
            pltpu.VMEM((rows, width), BF16),
            pltpu.VMEM(w.shape, BF16),
            pltpu.VMEM(w_out.shape, BF16),
            pltpu.SemaphoreType.DMA((8,)),
            pltpu.SemaphoreType.DMA((3,)),
            pltpu.SemaphoreType.DMA((5,)),
        ],
        compiler_params=PARAMS,
        cost_estimate=pl.CostEstimate(
            flops=2 * rows * width * 9 * HEAD_DIM, bytes_accessed=16_000_000, transcendentals=0
        ),
        name="project",
    )(
        place, tokens.reshape(rows, width), w, w_out,
        scale.reshape(1, -1), shift.reshape(1, -1), q_gain.reshape(1, -1), k_gain.reshape(1, -1),
    )


META_BLOCKS = 1
META_FRAME = 9
META_BAND = 10
META_FAR = 12
ONES = slice(2 * HEAD_DIM, 3 * HEAD_DIM)
FACTOR = LOG2E * HEAD_DIM ** (-0.5)


def weights_of(q, keys):
    return jnp.exp2(rows_dot(q, keys) * FACTOR)


def key_copies(meta_ref, blocks, pieces, kvo, kvm, sem):
    half = kvm.shape[1]
    s = meta_ref[0]
    near = pl.ds(pl.multiple_of(s * half, half), half)
    away = pl.ds(pl.multiple_of((1 - s) * half, half), half)
    two = pl.ds(0, 2 * HEAD_DIM)
    copies = []
    for at, block in enumerate(blocks):
        frames = pl.ds(2 * block, 2)
        kept, received = pieces[2 * at], pieces[2 * at + 1]
        copies += [
            pltpu.make_async_copy(kept.at[:, :, two], kvo.at[frames, near, two], sem.at[3 * at]),
            pltpu.make_async_copy(
                kept.at[:, :, pl.ds(2 * HEAD_DIM, 2 * HEAD_DIM)],
                kvm.at[frames, :, two],
                sem.at[3 * at + 1],
            ),
            pltpu.make_async_copy(received, kvo.at[frames, away, two], sem.at[3 * at + 2]),
        ]
    return copies


def query_copies(home_ref, away_ref, q_scr, sem, base):
    half = home_ref.shape[1]
    return [
        pltpu.make_async_copy(home_ref, q_scr.at[:, pl.ds(0, half)], sem.at[base]),
        pltpu.make_async_copy(away_ref, q_scr.at[:, pl.ds(half, half)], sem.at[base + 1]),
    ]


def add_frame(fi, at, q_scr, kvo, kvm, acc_o, acc_m):
    for lanes, kv, acc in (
        (slice(0, HEAD_DIM), kvo, acc_o),
        (slice(HEAD_DIM, 2 * HEAD_DIM), kvm, acc_m),
    ):
        keys = kv[at]
        weights = weights_of(q_scr[fi, :, lanes], keys[:, :HEAD_DIM]).astype(BF16)
        acc[fi] += jnp.dot(weights, keys[:, HEAD_DIM:], preferred_element_type=F32)


def near_kernel(meta_ref, home_ref, away_ref, *refs):
    pieces = refs[0:4]
    acc_o, acc_m, _, q_scr, kvo, kvm, sem = refs[5:12]
    local, half = kvm.shape[0], kvm.shape[1]
    start = meta_ref[META_FRAME] // local * local
    core = meta_ref[META_BLOCKS] % 2
    copies = query_copies(home_ref, away_ref, q_scr, sem, 6)
    copies += key_copies(meta_ref, [core, 1 - core], pieces, kvo, kvm, sem)
    for copy in copies:
        copy.start()
    kvo[:, :, ONES] = jnp.ones((local, 2 * half, HEAD_DIM), BF16)
    kvm[:, :, ONES] = jnp.ones((local, half, HEAD_DIM), BF16)
    acc_o[...] = jnp.zeros_like(acc_o)
    acc_m[...] = jnp.zeros_like(acc_m)
    for copy in copies:
        copy.wait()
    for fi in range(2):
        frame = meta_ref[META_FRAME] + fi - start
        width = meta_ref[META_BAND + fi]

        def one_frame(kf, carry, fi=fi):
            add_frame(fi, kf, q_scr, kvo, kvm, acc_o, acc_m)
            return carry

        lax.fori_loop(
            jnp.maximum(frame - width, 0), jnp.minimum(frame + width, local - 1) + 1, one_frame, 0
        )


def attend_near(meta, q_home, q_away, pieces, later):
    frames, half, _ = q_home.shape
    sums = jax.ShapeDtypeStruct((frames, 2 * half, 2 * HEAD_DIM), F32)
    return pl.pallas_call(
        near_kernel,
        out_shape=[sums, sums, jax.ShapeDtypeStruct(later.shape, later.dtype)],
        in_specs=[SMEM] + [ANY] * (3 + len(pieces)),
        out_specs=[VMEM] * 2 + [ANY],
        input_output_aliases={3 + len(pieces): 2},
        scratch_shapes=[
            pltpu.VMEM((frames, 2 * half, 2 * HEAD_DIM), BF16),
            pltpu.VMEM((2 * frames, 2 * half, 3 * HEAD_DIM), BF16),
            pltpu.VMEM((2 * frames, half, 3 * HEAD_DIM), BF16),
            pltpu.SemaphoreType.DMA((8,)),
        ],
        compiler_params=PARAMS,
        cost_estimate=pl.CostEstimate(
            flops=4_000_000_000, bytes_accessed=5_000_000, transcendentals=2_500_000
        ),
        name="attend_near",
    )(meta, q_home, q_away, *pieces, later)


def far_kernel(meta_ref, home_ref, away_ref, sums_o_ref, sums_m_ref, *refs):
    pieces = refs[0:12]
    out_ref, mid_ref, ret_ref = refs[16:19]
    q_scr, kvo, kvm, acc_o, acc_m, sem = refs[19:25]
    n_frames, half = kvm.shape[0], kvm.shape[1]
    s = meta_ref[0]
    copies = query_copies(home_ref, away_ref, q_scr, sem, 18)
    copies += [
        pltpu.make_async_copy(sums_o_ref, acc_o, sem.at[20]),
        pltpu.make_async_copy(sums_m_ref, acc_m, sem.at[21]),
    ]
    blocks = [meta_ref[META_BLOCKS + r] for r in range(2, 8)]
    copies += key_copies(meta_ref, blocks, pieces, kvo, kvm, sem)
    for copy in copies:
        copy.start()
    kvo[:, :, ONES] = jnp.ones((n_frames, 2 * half, HEAD_DIM), BF16)
    kvm[:, :, ONES] = jnp.ones((n_frames, half, HEAD_DIM), BF16)
    for copy in copies:
        copy.wait()
    eye = lax.broadcasted_iota(jnp.int32, (TILE, TILE), 0) == lax.broadcasted_iota(
        jnp.int32, (TILE, TILE), 1
    )
    start = meta_ref[META_FRAME] // 4 * 4
    for fi in range(2):
        frame = meta_ref[META_FRAME] + fi
        width = meta_ref[META_BAND + fi]

        def one_frame(kf, carry, fi=fi):
            add_frame(fi, kf, q_scr, kvo, kvm, acc_o, acc_m)
            return carry

        lax.fori_loop(jnp.maximum(frame - width, 0), start, one_frame, 0)
        lax.fori_loop(start + 4, jnp.minimum(frame + width, n_frames - 1) + 1, one_frame, 0)

        for r in range(2):
            for t in range(2):
                at = slice(r * half + t * TILE, r * half + (t + 1) * TILE)
                tile = 2 * (s ^ r) + t
                base = META_FAR + ((fi * 4 + tile) * 4) * 2
                entries = [(meta_ref[base + 2 * j], meta_ref[base + 2 * j + 1]) for j in range(4)]
                flags = []
                for j in range(4):
                    fresh = jnp.bool_(True)
                    for i in range(j):
                        same = (entries[i][0] == entries[j][0]) & (entries[i][1] == entries[j][1])
                        fresh = fresh & jnp.logical_not(same)
                    flags.append(fresh)
                mid_flags = [fresh & (entry[1] // 2 == s) for fresh, entry in zip(flags, entries)]
                for lanes, kv, acc, shown, tiles in (
                    (slice(0, HEAD_DIM), kvo, acc_o, flags, 4),
                    (slice(HEAD_DIM, 2 * HEAD_DIM), kvm, acc_m, mid_flags, 2),
                ):
                    keys = jnp.concatenate(
                        [
                            kv[kf, pl.ds(pl.multiple_of((kt % tiles) * TILE, TILE), TILE), :]
                            for kf, kt in entries
                        ],
                        axis=0,
                    )
                    weights = weights_of(q_scr[fi, at, lanes], keys[:, :HEAD_DIM])
                    weights = jnp.concatenate(
                        [
                            weights[:, j * TILE:(j + 1) * TILE] * jnp.where(shown[j], 1.0, 0.0)
                            for j in range(4)
                        ],
                        axis=1,
                    ).astype(BF16)
                    acc[fi, at, :] += jnp.dot(
                        weights, keys[:, HEAD_DIM:], preferred_element_type=F32
                    )

        attended = (acc_o[fi, :, :HEAD_DIM] / acc_o[fi, :, HEAD_DIM:]).astype(BF16)
        out_ref[fi] = attended[:half]
        ret_ref[fi, :half, :HEAD_DIM] = attended[half:]
        mid_ref[fi] = acc_m[fi, :half, :]
        ret_ref[fi, :half, HEAD_DIM:] = acc_m[fi, half:, :HEAD_DIM].astype(BF16)
        dens = []
        for g in range(2):
            den = acc_m[fi, half + g * TILE:half + (g + 1) * TILE, HEAD_DIM:]
            dens.append(jnp.sum(jnp.where(eye, den, 0.0), axis=0, keepdims=True))
        den = jnp.concatenate(dens, axis=0)
        upper = den.astype(BF16).astype(F32)
        block = jnp.concatenate([upper, den - upper, jnp.zeros((12, TILE), F32)], axis=0)
        ret_ref[fi, half:, :HEAD_DIM] = block.astype(BF16)
        ret_ref[fi, half:, HEAD_DIM:] = jnp.zeros((16, HEAD_DIM), BF16)


def attend_far(meta, q_home, q_away, sums, pieces, waited, n_frames):
    frames, half, _ = q_home.shape
    return pl.pallas_call(
        far_kernel,
        out_shape=[
            jax.ShapeDtypeStruct((frames, half, HEAD_DIM), BF16),
            jax.ShapeDtypeStruct((frames, half, 2 * HEAD_DIM), F32),
            jax.ShapeDtypeStruct((frames, half + 16, 2 * HEAD_DIM), BF16),
        ],
        in_specs=[SMEM] + [ANY] * (4 + len(pieces) + len(waited)),
        out_specs=[VMEM] * 3,
        scratch_shapes=[
            pltpu.VMEM((frames, 2 * half, 2 * HEAD_DIM), BF16),
            pltpu.VMEM((n_frames, 2 * half, 3 * HEAD_DIM), BF16),
            pltpu.VMEM((n_frames, half, 3 * HEAD_DIM), BF16),
            pltpu.VMEM((frames, 2 * half, 2 * HEAD_DIM), F32),
            pltpu.VMEM((frames, 2 * half, 2 * HEAD_DIM), F32),
            pltpu.SemaphoreType.DMA((22,)),
        ],
        compiler_params=PARAMS,
        cost_estimate=pl.CostEstimate(
            flops=5_000_000_000, bytes_accessed=10_000_000, transcendentals=2_500_000
        ),
        name="attend_far",
    )(meta, q_home, q_away, *sums, *pieces, *waited)


def combine_kernel(s_ref, home_ref, mid_ref, got_ref, out_ref):
    half = home_ref.shape[1]
    own_lanes = pl.ds(pl.multiple_of(s_ref[0] * 2 * HEAD_DIM, HEAD_DIM), HEAD_DIM)
    other_lanes = pl.ds(pl.multiple_of((1 - s_ref[0]) * 2 * HEAD_DIM, HEAD_DIM), HEAD_DIM)
    eye = lax.broadcasted_iota(jnp.int32, (TILE, TILE), 0) == lax.broadcasted_iota(
        jnp.int32, (TILE, TILE), 1
    )
    ones = jnp.ones((TILE, TILE), BF16)
    for fi in range(2):
        rows = pl.ds(fi * half, half)
        out_ref[rows, own_lanes] = home_ref[fi]
        out_ref[rows, other_lanes] = got_ref[fi, :half, :HEAD_DIM]
        tail = got_ref[fi, half:, :HEAD_DIM].astype(F32)
        for g in range(2):
            at = slice(g * TILE, (g + 1) * TILE)
            upper = jnp.where(eye, tail[g:g + 1, :], 0.0).astype(BF16)
            lower = jnp.where(eye, tail[2 + g:3 + g, :], 0.0).astype(BF16)
            den = jnp.dot(upper, ones, preferred_element_type=F32) + jnp.dot(
                lower, ones, preferred_element_type=F32
            )
            num = mid_ref[fi, at, :HEAD_DIM] + got_ref[fi, at, HEAD_DIM:].astype(F32)
            to = slice(fi * half + g * TILE, fi * half + (g + 1) * TILE)
            out_ref[to, HEAD_DIM:2 * HEAD_DIM] = (
                num / (mid_ref[fi, at, HEAD_DIM:] + den)
            ).astype(BF16)


def combine(s, home, mid, got):
    frames, half, _ = home.shape
    return pl.pallas_call(
        combine_kernel,
        out_shape=jax.ShapeDtypeStruct((frames * half, 3 * HEAD_DIM), BF16),
        in_specs=[SMEM, VMEM, VMEM, VMEM],
        out_specs=VMEM,
        compiler_params=PARAMS,
        cost_estimate=pl.CostEstimate(
            flops=50_000_000, bytes_accessed=1_500_000, transcendentals=0
        ),
        name="combine",
    )(s.reshape(1), home, mid, got)


def output_kernel(place_ref, *refs):
    mixed, (w_out_ref, ahead_ref, behind_ref, apart_ref, swapped_ref) = refs[0:4], refs[4:9]
    kept_ref, sent_ref, h_scr, w_scr, h_sem, w_sem = refs[9:15]
    width = mixed[0].shape[1]
    cols = kept_ref.shape[1]
    part = apart_ref.shape[0]
    core = place_ref[1]
    copies = []
    for k in range(4):
        at = pl.ds(k * width, width)
        copies.append(pltpu.make_async_copy(mixed[k], h_scr.at[:, at], h_sem.at[k]))
    for k in range(2):
        block = pl.ds(pl.multiple_of(place_ref[6 + k] * cols, TILE), cols)
        copies.append(
            pltpu.make_async_copy(
                w_out_ref.at[:, block],
                w_scr.at[pl.ds(0, width), pl.ds(k * cols, cols)],
                w_sem.at[k],
            )
        )
    for k, (source, base) in enumerate(
        (
            (ahead_ref, width),
            (behind_ref, 2 * width),
            (apart_ref, 3 * width + core * part),
            (swapped_ref, 3 * width + (1 - core) * part),
        )
    ):
        at = pl.ds(pl.multiple_of(base, 16), source.shape[0])
        copies.append(pltpu.make_async_copy(source, w_scr.at[at], w_sem.at[2 + k]))
    for copy in copies:
        copy.start()
    for copy in copies:
        copy.wait()
    sent_ref[...] = jnp.dot(
        h_scr[...], w_scr[:, cols:], preferred_element_type=F32
    ).astype(BF16)
    kept_ref[...] = jnp.dot(h_scr[...], w_scr[:, :cols], preferred_element_type=F32)


def output(place, mixed, w_out, weights):
    rows, width = mixed[0].shape
    cols = weights[0].shape[1] // 2
    return pl.pallas_call(
        output_kernel,
        out_shape=[
            jax.ShapeDtypeStruct((rows, cols), F32),
            jax.ShapeDtypeStruct((rows, cols), BF16),
        ],
        in_specs=[SMEM] + [ANY] * 9,
        out_specs=[VMEM] * 2,
        scratch_shapes=[
            pltpu.VMEM((rows, 4 * width), BF16),
            pltpu.VMEM((4 * width, 2 * cols), BF16),
            pltpu.SemaphoreType.DMA((4,)),
            pltpu.SemaphoreType.DMA((6,)),
        ],
        compiler_params=PARAMS,
        cost_estimate=pl.CostEstimate(
            flops=16 * rows * width * cols, bytes_accessed=6_000_000, transcendentals=0
        ),
        name="output",
    )(place, *mixed, w_out, *weights)


def move(axis, to, x):
    axes = axis if isinstance(axis, tuple) else (axis,)
    count = 1
    for name in axes:
        count *= lax.axis_size(name)
    return lax.ppermute(x, axis, [(i, to(i)) for i in range(count)])


def z_step(head, step):
    return head // 4 * 4 + (head + step) % 4


def z_by_core(step, i):
    frame, head = i // 8, i % 8
    return frame * 8 + z_step(head, step if frame % 2 == 0 else 4 - step)


swap_core = functools.partial(move, "frame", lambda i: i ^ 1)
out_y = functools.partial(move, "frame", lambda i: (i + (2 if i % 2 == 0 else 6)) % 8)
swap_half = functools.partial(move, "spatial", lambda i: i ^ 1)
cross_z = functools.partial(move, "head", lambda i: z_step(i, 2))
out_z = functools.partial(move, ("frame", "head"), functools.partial(z_by_core, 1))
in_z = functools.partial(move, ("frame", "head"), functools.partial(z_by_core, 3))
swap_x = functools.partial(move, "head", lambda i: i ^ 4)


def shards(tokens, w_qkv, w_out, shift, scale, gate, q_gain, k_gain, band, far_tiles):
    frames_dev, half_tok, model_width = tokens.shape
    n_frames = band.shape[0]
    f = lax.axis_index("frame")
    s = lax.axis_index("spatial")
    g = lax.axis_index("head")
    core, y, z, side = f % 2, f // 2, g % 4, g // 4

    step = jnp.where(core == 0, 1, 3)
    w = jnp.transpose(w_qkv, (1, 0, 2))
    columns = [(z + by) % 4 + 4 * to for by in (step, 2, 0) for to in (side, 1 - side)]
    place = jnp.stack([s, core] + columns)
    kept, sent, q_home, q_send, w_ahead, w_apart = project(
        place, tokens, w, w_out, scale, shift, q_gain, k_gain
    )
    q_away = swap_half(q_send)
    away = swap_half(sent)
    kept_other = swap_core(kept)
    kept_first, kept_second = out_y(kept), out_y(kept_other)
    away_other = swap_core(away)
    away_first, away_second = out_y(away), out_y(away_other)
    w_ahead, w_apart = out_z(w_ahead), cross_z(w_apart)
    w_parts = [w_ahead, swap_core(w_ahead), w_apart, swap_core(w_apart)]
    kept_across = out_y(kept_first)
    near_pieces = [kept, away, kept_other, away_other]
    ahead = (y + jnp.where(core == 0, 3, 1)) % 4
    behind = (y + jnp.where(core == 0, 1, 3)) % 4
    apart = (y + 2) % 4
    blocks = jnp.stack(
        [
            2 * y + core, 2 * y + 1 - core,
            2 * ahead + core, 2 * ahead + 1 - core,
            2 * behind + 1 - core, 2 * behind + core,
            2 * apart + core, 2 * apart + 1 - core,
        ]
    )
    start = f * frames_dev
    meta = jnp.concatenate(
        [
            s.reshape(1),
            blocks,
            start.reshape(1),
            lax.dynamic_slice_in_dim(band, start, frames_dev, 0),
            lax.dynamic_slice_in_dim(far_tiles, start, frames_dev, 0).reshape(-1),
        ]
    ).astype(jnp.int32)
    *sums, away_first = attend_near(meta, q_home, q_away, near_pieces, away_first)
    away_across = out_y(away_first)
    far = [
        (first, second, swap_core(first), swap_core(second), across, swap_core(across))
        for first, second, across in (
            (kept_first, kept_second, kept_across),
            (away_first, away_second, away_across),
        )
    ]
    far_pieces = [one[r] for r in range(6) for one in far]
    home, mid_sums, back = attend_far(
        meta, q_home, q_away, sums, far_pieces, w_parts, n_frames
    )
    mixed = combine(s, home, mid_sums, swap_half(back))
    ahead_z = out_z(mixed)
    gathered = [mixed, ahead_z, in_z(mixed), out_z(ahead_z)]
    kept_part, sent_part = output(place, gathered, w_out, w_parts)
    total = kept_part + swap_x(sent_part).astype(F32)
    return (total * gate).astype(BF16).reshape(frames_dev, half_tok, -1)


def solution(mesh):
    return jax.shard_map(
        shards,
        mesh=mesh,
        in_specs=(
            P("frame", "spatial", None),
            P(None, None, "head"),
            P("head", None),
            P(),
            P(),
            P("head"),
            P(),
            P(),
            P(),
            P(),
        ),
        out_specs=P("frame", "spatial", "head"),
        check_vma=False,
    )
```

time: 137 us -> 118 us (0.86)
  starting transfers between devices: 47.4 us -> 27 us
  Pallas kernels: 29.8 us -> 32.4 us
  waiting for transfers between devices: 52.9 us -> 50.7 us
  other arithmetic: 0.2 us -> 1.98 us
    ppermute x46 -> x25, starting transfers between devices: 47.4 us -> 27 us  [move(): return lax.ppermute(x, axis, [(i, to(i)) for i in range(count)])]
    pallas_call x4 -> x5, Pallas kernels: 29.8 us -> 32.4 us  [the longest x1 11.3 us: project(): pl.pallas_call(project_kernel, out_shape=[jax.ShapeDtypeStruct((frames, h...]
    ppermute x46 -> x25, waiting for transfers between devices: 52.9 us -> 50.7 us  [move(): return lax.ppermute(x, axis, [(i, to(i)) for i in range(count)])]
    convert_element_type x0 -> x1, other arithmetic: none -> 1.98 us  [shards(): return (total * gate).astype(BF16).reshape(frames_dev, half_tok, -1)]
    unnamed x86 -> x54, local copies, waits for them, and re-layouts: 4.37 us -> 3.49 us
  transfers between devices with their start and end apart: 46 -> 25, of which waited for: 18 -> 9; matrix products, arithmetic and copies ran while one was open for 1% -> 1% of each run, Pallas kernels for 9% -> 6%
where the time goes in v2:
time: 118 us
  waiting for transfers between devices  50.7 us (43%)
  Pallas kernels  32.4 us (27%)
  starting transfers between devices  27 us (23%)
  local copies, waits for them, and re-layouts  5.14 us (4%)
  other arithmetic  1.98 us (2%)
    ppermute x25, waiting for transfers between devices, move(): return lax.ppermute(x, axis, [(i, to(i)) for i in range(count)])  50.7 us
    ppermute x25, starting transfers between devices, move(): return lax.ppermute(x, axis, [(i, to(i)) for i in range(count)])  27 us
    pallas_call x1, Pallas kernels, project(): pl.pallas_call(project_kernel, out_shape=[jax.ShapeDtypeStruct((frames, h...  11.3 us
    pallas_call x1, Pallas kernels, attend_near(): pl.pallas_call(near_kernel, out_shape=[sums, sums, jax.ShapeDtypeStruct(l...  7.07 us
    pallas_call x1, Pallas kernels, attend_far(): pl.pallas_call(far_kernel, out_shape=[jax.ShapeDtypeStruct((frames, half,...  6.38 us
    pallas_call x1, Pallas kernels, output(): pl.pallas_call(output_kernel, out_shape=[jax.ShapeDtypeStruct((rows, cols...  5.51 us
    unnamed x54, local copies, waits for them, and re-layouts  3.49 us
  transfers between devices with their start and end apart: 25, of which 9 were waited for; matrix products, arithmetic and copies ran while one was open for 1% of the time, Pallas kernels for 6%

profile of v2, /device:TPU:0, one launch (start us, length us, event | category | flops | bytes accessed | tf_op | source)
XLA Modules:
  0.0 117.5 jit_solution(14699519884811855327)
XLA Ops:
  0.0 0.6 stack.59.place_ref
  0.6 11.3 %project.1 = (bf16[2,256,512]{2,1,0:T(8,128)(2,1)}, bf16[2,256,256]{2,1,0:T(8,128)(2,1)}, bf16[2,256,256]{2,1,0:T(8,128)(2,1)}, bf16[2,256,256]{2,1,0:T(8,128)(2...) custom-call(s32[8]{0:T(128)} %stack.59.place_ref, bf16[512,3072]{1,0:T(8,128)(2,1)} %bitcast.25, ...), custom_call_target="tpu_custom_call" | custom-call | flops 3623878656 | bytes 16000000 | tf_op jit(solution)/shard_map/project/pallas_call | solution.py:118
  11.9 1.7 %collective-permute-start.1 = (bf16[2,256,256]{2,1,0:T(8,128)(2,1)}, bf16[2,256,256]{2,1,0:T(8,128)(2,1)S(1)}, u32[]{:S(2)}, u32[]{:S(2)}) collective-permute-start(bf16[2,256,256]{2,1,0:T(8,128)(2,1)} %get-tuple-element.22), channel_id=1, source_target_pairs={{0,8},{8,0},{1,9},{9,1},{2,10},{10,2},{3,11},{11,3},{4,12},{12,4},... | collective-permute-start | bytes 786440 | tf_op jit(solution)/shard_map/ppermute | solution.py:478
  13.6 1.6 %collective-permute-start.5 = (bf16[2,256,512]{2,1,0:T(8,128)(2,1)}, bf16[2,256,512]{2,1,0:T(8,128)(2,1)S(1)}, u32[]{:S(2)}, u32[]{:S(2)}) collective-permute-start(bf16[2,256,512]{2,1,0:T(8,128)(2,1)} %get-tuple-element.21.refs_0_), channel_id=1, source_target_pairs={{0,32},{16,112},{32,64},{48,16},{64,96},{80,48},{96,0},{112,80},{1... | collective-permute-start | bytes 1572872 | tf_op jit(solution)/shard_map/ppermute | solution.py:478
  15.1 0.5 collective-permute-start
  15.7 3.9 %collective-permute-start.18 = (bf16[192,768]{1,0:T(8,128)(2,1)}, bf16[192,768]{1,0:T(8,128)(2,1)S(1)}, u32[]{:S(2)}, u32[]{:S(2)}) collective-permute-start(bf16[192,768]{1,0:T(8,128)(2,1)} %get-tuple-element.27), channel_id=1, source_target_pairs={{0,2},{1,3},{2,0},{3,1},{4,6},{5,7},{6,4},{7,5},{8,10},{9,11},{10,... | collective-permute-start | bytes 884744 | tf_op jit(solution)/shard_map/ppermute | solution.py:478
  19.6 1.0 collective-permute-done.1.refs_1_
  20.6 0.1 collective-permute-start.3
  20.7 5.0 %collective-permute-done.away_ref = bf16[2,256,256]{2,1,0:T(8,128)(2,1)S(1)} collective-permute-done((bf16[2,256,256]{2,1,0:T(8,128)(2,1)}, bf16[2,256,256]{2,1,0:T(8,128)(2,1)S(1)}, u32[]{:S(2)}, u32[]{:S(2)}) %collective-permute-start) | collective-permute-done | bytes 262176 | tf_op jit(solution)/shard_map/ppermute | solution.py:478
  25.7 1.8 %collective-permute-start.4 = (bf16[2,256,256]{2,1,0:T(8,128)(2,1)S(1)}, bf16[2,256,256]{2,1,0:T(8,128)(2,1)S(1)}, u32[]{:S(2)}, u32[]{:S(2)}) collective-permute-start(bf16[2,256,256]{2,1,0:T(8,128)(2,1)S(1)} %collective-permute-done.1.refs_1_), channel_id=1, source_target_pairs={{0,32},{16,112},{32,64},{48,16},{64,96},{80,48},{96,0},{112,80},{1... | collective-permute-start | bytes 786440 | tf_op jit(solution)/shard_map/ppermute | solution.py:478
  27.5 1.9 %collective-permute-start.16 = (bf16[384,768]{1,0:T(8,128)(2,1)}, bf16[384,768]{1,0:T(8,128)(2,1)S(1)}, u32[]{:S(2)}, u32[]{:S(2)}) collective-permute-start(bf16[384,768]{1,0:T(8,128)(2,1)} %get-tuple-element.26), channel_id=1, source_target_pairs={{0,1},{1,2},{2,3},{3,0},{4,5},{5,6},{6,7},{7,4},{16,19},{17,16},{1... | collective-permute-start | bytes 1769480 | tf_op jit(solution)/shard_map/ppermute | solution.py:478
  29.5 0.1 constant_dynamic-slice_fusion
  29.5 0.2 copy.13
  29.7 0.1 reshape.28
  29.9 0.1 dynamic_slice.6
  29.9 0.6 concatenate.3.meta_ref
  30.6 2.0 %collective-permute-start.19 = (bf16[192,768]{1,0:T(8,128)(2,1)S(1)}, bf16[192,768]{1,0:T(8,128)(2,1)S(1)}, u32[]{:S(2)}, u32[]{:S(2)}) collective-permute-start(bf16[192,768]{1,0:T(8,128)(2,1)S(1)} %collective-permute-done.18.refs_14_.refs_7_), channel_id=1, source_target_pairs={{0,16},{16,0},{32,48},{48,32},{64,80},{80,64},{96,112},{112,96},{1... | collective-permute-start | bytes 884744 | tf_op jit(solution)/shard_map/ppermute | solution.py:478
  32.5 1.0 collective-permute-start.12
  33.5 0.7 copy-done.20
  34.2 7.1 %attend_near.1 = (f32[2,512,256]{2,1,0:T(8,128)}, f32[2,512,256]{2,1,0:T(8,128)}, bf16[2,256,256]{2,1,0:T(8,128)(2,1)}) custom-call(s32[76]{0:T(128)} %concatenate.3.meta_ref, bf16[2,256,256]{2,1,0:T(8,128)(2,1)} %get-tuple-element.19.home_ref, bf16[2,256,256]{2,1,0:T(8,128)(2,1)} %copy-done.17, ...), custom_call_target="tpu_custom_call", output_to_operand_aliasing={{2}: (7, {})} | custom-call | flops 4000000000 | bytes 5000000 | tf_op jit(solution)/shard_map/attend_near/pallas_call | solution.py:232
  41.3 1.2 %collective-permute-start.13 = (bf16[2,256,256]{2,1,0:T(8,128)(2,1)}, bf16[2,256,256]{2,1,0:T(8,128)(2,1)S(1)}, u32[]{:S(2)}, u32[]{:S(2)}) collective-permute-start(bf16[2,256,256]{2,1,0:T(8,128)(2,1)} %get-tuple-element.25.refs_1_), channel_id=1, source_target_pairs={{0,32},{16,112},{32,64},{48,16},{64,96},{80,48},{96,0},{112,80},{1... | collective-permute-start | bytes 786440 | tf_op jit(solution)/shard_map/ppermute | solution.py:478
  42.6 2.0 %collective-permute-start.7 = (bf16[2,256,256]{2,1,0:T(8,128)(2,1)}, bf16[2,256,256]{2,1,0:T(8,128)(2,1)S(1)}, u32[]{:S(2)}, u32[]{:S(2)}) collective-permute-start(bf16[2,256,256]{2,1,0:T(8,128)(2,1)} %copy-done.18), channel_id=1, source_target_pairs={{0,32},{16,112},{32,64},{48,16},{64,96},{80,48},{96,0},{112,80},{1... | collective-permute-start | bytes 786440 | tf_op jit(solution)/shard_map/ppermute | solution.py:478
  44.6 6.8 %collective-permute-done.13.refs_9_ = bf16[2,256,256]{2,1,0:T(8,128)(2,1)S(1)} collective-permute-done((bf16[2,256,256]{2,1,0:T(8,128)(2,1)}, bf16[2,256,256]{2,1,0:T(8,128)(2,1)S(1)}, u32[]{:S(2)}, u32[]{:S(2)}) %collective-permute-start.13) | collective-permute-done | bytes 262176 | tf_op jit(solution)/shard_map/ppermute | solution.py:478
  51.4 0.5 collective-permute-start.15
  51.9 2.3 %collective-permute-done.7.refs_3_ = bf16[2,256,256]{2,1,0:T(8,128)(2,1)S(1)} collective-permute-done((bf16[2,256,256]{2,1,0:T(8,128)(2,1)}, bf16[2,256,256]{2,1,0:T(8,128)(2,1)S(1)}, u32[]{:S(2)}, u32[]{:S(2)}) %collective-permute-start.7) | collective-permute-done | bytes 262176 | tf_op jit(solution)/shard_map/ppermute | solution.py:478
  54.2 0.5 collective-permute-start.10
  54.7 0.1 collective-permute-start.14
  54.8 0.4 collective-permute-start.11
  55.2 2.7 %collective-permute-done.11.refs_7_ = bf16[2,256,256]{2,1,0:T(8,128)(2,1)S(1)} collective-permute-done((bf16[2,256,256]{2,1,0:T(8,128)(2,1)S(1)}, bf16[2,256,256]{2,1,0:T(8,128)(2,1)S(1)}, u32[]{:S(2)}, u32[]{:S(2)}) %collective-permute-start.11) | collective-permute-done | bytes 262176 | tf_op jit(solution)/shard_map/ppermute | solution.py:478
  58.1 0.5 copy-done.25
  58.6 0.2 copy-done.14
  58.8 0.2 copy-done.2
  59.0 0.2 copy-done.15
  59.2 0.1 copy-done.16
  59.4 6.4 %attend_far.1 = (bf16[2,256,128]{2,1,0:T(8,128)(2,1)}, f32[2,256,256]{2,1,0:T(8,128)}, bf16[2,272,256]{2,1,0:T(8,128)(2,1)}) custom-call(s32[76]{0:T(128)} %concatenate.3.meta_ref, bf16[2,256,256]{2,1,0:T(8,128)(2,1)} %get-tuple-element.19.home_ref, bf16[2,256,256]{2,1,0:T(8,128)(2,1)} %copy-done.17, f32[2,512,256]{2,1,0:T(8,128)} %get-tuple-element.23.sums_o_ref, ...), custom_call_target="tpu_custom_call" | custom-call | flops 5000000000 | bytes 10000000 | tf_op jit(solution)/shard_map/attend_far/pallas_call | solution.py:341
  65.8 1.6 %collective-permute-start.20 = (bf16[2,272,256]{2,1,0:T(8,128)(2,1)}, bf16[2,272,256]{2,1,0:T(8,128)(2,1)S(1)}, u32[]{:S(2)}, u32[]{:S(2)}) collective-permute-start(bf16[2,272,256]{2,1,0:T(8,128)(2,1)} %get-tuple-element.30), channel_id=1, source_target_pairs={{0,8},{8,0},{1,9},{9,1},{2,10},{10,2},{3,11},{11,3},{4,12},{12,4},... | collective-permute-start | bytes 835592 | tf_op jit(solution)/shard_map/ppermute | solution.py:478
  67.3 7.9 %collective-permute-done.20.got_ref = bf16[2,272,256]{2,1,0:T(8,128)(2,1)S(1)} collective-permute-done((bf16[2,272,256]{2,1,0:T(8,128)(2,1)}, bf16[2,272,256]{2,1,0:T(8,128)(2,1)S(1)}, u32[]{:S(2)}, u32[]{:S(2)}) %collective-permute-start.20) | collective-permute-done | bytes 278560 | tf_op jit(solution)/shard_map/ppermute | solution.py:478
  75.2 0.7 copy-done.8
  75.9 2.1 %combine.1.refs_0_ = bf16[512,384]{1,0:T(8,128)(2,1)} custom-call(s32[1]{0:T(128)} %bitcast.s_ref, bf16[2,256,128]{2,1,0:T(8,128)(2,1)} %get-tuple-element.28.home_ref, f32[2,256,256]{2,1,0:T(8,128)} %get-tuple-element.29.mid_ref, bf16[2,272,256]{2,1,0:T(8,128)(2,1)} %copy-done.8), custom_call_target="tpu_custom_call" | custom-call | flops 50000000 | bytes 1500000 | tf_op jit(solution)/shard_map/combine/pallas_call | solution.py:395
  78.1 0.0 collective-permute-start.21
  78.1 3.2 %collective-permute-start.22 = (bf16[512,384]{1,0:T(8,128)(2,1)}, bf16[512,384]{1,0:T(8,128)(2,1)S(1)}, u32[]{:S(2)}, u32[]{:S(2)}) collective-permute-start(bf16[512,384]{1,0:T(8,128)(2,1)} %combine.1.refs_0_), channel_id=1, source_target_pairs={{0,3},{1,0},{2,1},{3,2},{4,7},{5,4},{6,5},{7,6},{16,17},{17,18},{1... | collective-permute-start | bytes 1179656 | tf_op jit(solution)/shard_map/ppermute | solution.py:478
  81.3 9.4 %collective-permute-done.21.refs_1_ = bf16[512,384]{1,0:T(8,128)(2,1)S(1)} collective-permute-done((bf16[512,384]{1,0:T(8,128)(2,1)}, bf16[512,384]{1,0:T(8,128)(2,1)S(1)}, u32[]{:S(2)}, u32[]{:S(2)}) %collective-permute-start.21) | collective-permute-done | bytes 393248 | tf_op jit(solution)/shard_map/ppermute | solution.py:478
  90.8 9.0 %collective-permute-done.23.refs_3_ = bf16[512,384]{1,0:T(8,128)(2,1)S(1)} collective-permute-done((bf16[512,384]{1,0:T(8,128)(2,1)S(1)}, bf16[512,384]{1,0:T(8,128)(2,1)S(1)}, u32[]{:S(2)}, u32[]{:S(2)}) %collective-permute-start.23) | collective-permute-done | bytes 393248 | tf_op jit(solution)/shard_map/ppermute | solution.py:478
  99.7 0.7 copy-done.5
  100.5 5.5 %output.1 = (f32[512,384]{1,0:T(8,128)}, bf16[512,384]{1,0:T(8,128)(2,1)}) custom-call(s32[8]{0:T(128)} %stack.59.place_ref, bf16[512,384]{1,0:T(8,128)(2,1)} %combine.1.refs_0_, bf16[512,384]{1,0:T(8,128)(2,1)} %copy-done.3, bf16[512,384]{1,0:T(8,128)(2,1)} %copy-done.4, bf16[512,384]{1,0:T(8,128)(2,1)} %copy-done.5, bf16[384,3072]{1,0:T(8,128)(2,1)} %refs_4_.1, ...), custom_call_target="tpu_custom_call" | custom-call | flops 1207959552 | bytes 6000000 | tf_op jit(solution)/shard_map/output/pallas_call | solution.py:451
  106.0 3.1 %collective-permute-start.24 = (bf16[512,384]{1,0:T(8,128)(2,1)}, bf16[512,384]{1,0:T(8,128)(2,1)S(1)}, u32[]{:S(2)}, u32[]{:S(2)}) collective-permute-start(bf16[512,384]{1,0:T(8,128)(2,1)} %get-tuple-element.32), channel_id=1, source_target_pairs={{0,4},{1,5},{2,6},{3,7},{4,0},{5,1},{6,2},{7,3},{8,12},{9,13},{10,... | collective-permute-start | bytes 1179656 | tf_op jit(solution)/shard_map/ppermute | solution.py:478
  109.1 6.5 %collective-permute-done.24 = bf16[512,384]{1,0:T(8,128)(2,1)S(1)} collective-permute-done((bf16[512,384]{1,0:T(8,128)(2,1)}, bf16[512,384]{1,0:T(8,128)(2,1)S(1)}, u32[]{:S(2)}, u32[]{:S(2)}) %collective-permute-start.24) | collective-permute-done | bytes 393248 | tf_op jit(solution)/shard_map/ppermute | solution.py:478
  115.6 2.0 %multiply_convert_fusion = bf16[512,384]{1,0:T(8,128)(2,1)} fusion(f32[512,384]{1,0:T(8,128)} %get-tuple-element.31, bf16[512,384]{1,0:T(8,128)(2,1)S(1)} %collective-permute-done.24, f32[384]{0:T(512)S(1)} %copy-done.9), kind=kLoop, calls=%fused_computation | loop fusion | flops 786432 | bytes 1574400 | tf_op jit(solution)/shard_map/convert_element_type | solution.py:563
  (68 shorter events, 0.1 us)
Async XLA Ops:
  0.0 29.5 %copy-start = (s32[16,4,4,2]{0,3,2,1:T(2,128)S(1)}, s32[16,4,4,2]{0,3,2,1:T(2,128)}, u32[]{:S(2)}) copy-start(s32[16,4,4,2]{0,3,2,1:T(2,128)} %param.19) | copy-start | bytes 6148
  0.6 29.3 %copy-start.26 = (s32[16]{0:T(128)S(1)}, s32[16]{0:T(128)}, u32[]{:S(2)}) copy-start(s32[16]{0:T(128)} %param.18) | copy-start | bytes 196
  11.9 8.7 %collective-permute-start.1 = (bf16[2,256,256]{2,1,0:T(8,128)(2,1)}, bf16[2,256,256]{2,1,0:T(8,128)(2,1)S(1)}, u32[]{:S(2)}, u32[]{:S(2)}) collective-permute-start(bf16[2,256,256]{2,1,0:T(8,128)(2,1)} %get-tuple-element.22), channel_id=1, source_target_pairs={{0,8},{8,0},{1,9},{9,1},{2,10},{10,2},{3,11},{11,3},{4,12},{12,4},... | collective-permute-start | bytes 786440 | tf_op jit(solution)/shard_map/ppermute | solution.py:478
  13.6 19.0 %collective-permute-start.2 = (bf16[2,256,512]{2,1,0:T(8,128)(2,1)}, bf16[2,256,512]{2,1,0:T(8,128)(2,1)S(1)}, u32[]{:S(2)}, u32[]{:S(2)}) collective-permute-start(bf16[2,256,512]{2,1,0:T(8,128)(2,1)} %get-tuple-element.21.refs_0_), channel_id=1, source_target_pairs={{0,16},{16,0},{32,48},{48,32},{64,80},{80,64},{96,112},{112,96},{1... | collective-permute-start | bytes 1572872 | tf_op jit(solution)/shard_map/ppermute | solution.py:478
  13.6 19.0 %collective-permute-start.5 = (bf16[2,256,512]{2,1,0:T(8,128)(2,1)}, bf16[2,256,512]{2,1,0:T(8,128)(2,1)S(1)}, u32[]{:S(2)}, u32[]{:S(2)}) collective-permute-start(bf16[2,256,512]{2,1,0:T(8,128)(2,1)} %get-tuple-element.21.refs_0_), channel_id=1, source_target_pairs={{0,32},{16,112},{32,64},{48,16},{64,96},{80,48},{96,0},{112,80},{1... | collective-permute-start | bytes 1572872 | tf_op jit(solution)/shard_map/ppermute | solution.py:478
  15.1 10.6 %collective-permute-start = (bf16[2,256,256]{2,1,0:T(8,128)(2,1)}, bf16[2,256,256]{2,1,0:T(8,128)(2,1)S(1)}, u32[]{:S(2)}, u32[]{:S(2)}) collective-permute-start(bf16[2,256,256]{2,1,0:T(8,128)(2,1)} %get-tuple-element.20), channel_id=1, source_target_pairs={{0,8},{8,0},{1,9},{9,1},{2,10},{10,2},{3,11},{11,3},{4,12},{12,4},... | collective-permute-start | bytes 786440 | tf_op jit(solution)/shard_map/ppermute | solution.py:478
  15.7 11.9 %collective-permute-start.18 = (bf16[192,768]{1,0:T(8,128)(2,1)}, bf16[192,768]{1,0:T(8,128)(2,1)S(1)}, u32[]{:S(2)}, u32[]{:S(2)}) collective-permute-start(bf16[192,768]{1,0:T(8,128)(2,1)} %get-tuple-element.27), channel_id=1, source_target_pairs={{0,2},{1,3},{2,0},{3,1},{4,6},{5,7},{6,4},{7,5},{8,10},{9,11},{10,... | collective-permute-start | bytes 884744 | tf_op jit(solution)/shard_map/ppermute | solution.py:478
  20.6 12.9 %copy-start.19 = (bf16[2,256,256]{2,1,0:T(8,128)(2,1)}, bf16[2,256,256]{2,1,0:T(8,128)(2,1)S(1)}, u32[]{:S(2)}) copy-start(bf16[2,256,256]{2,1,0:T(8,128)(2,1)S(1)} %collective-permute-done.1.refs_1_) | copy-start | bytes 786436
  20.6 10.0 %collective-permute-start.3 = (bf16[2,256,256]{2,1,0:T(8,128)(2,1)S(1)}, bf16[2,256,256]{2,1,0:T(8,128)(2,1)S(1)}, u32[]{:S(2)}, u32[]{:S(2)}) collective-permute-start(bf16[2,256,256]{2,1,0:T(8,128)(2,1)S(1)} %collective-permute-done.1.refs_1_), channel_id=1, source_target_pairs={{0,16},{16,0},{32,48},{48,32},{64,80},{80,64},{96,112},{112,96},{1... | collective-permute-start | bytes 786440 | tf_op jit(solution)/shard_map/ppermute | solution.py:478
  25.7 7.8 %copy-start.17 = (bf16[2,256,256]{2,1,0:T(8,128)(2,1)}, bf16[2,256,256]{2,1,0:T(8,128)(2,1)S(1)}, u32[]{:S(2)}) copy-start(bf16[2,256,256]{2,1,0:T(8,128)(2,1)S(1)} %collective-permute-done.away_ref) | copy-start | bytes 786436
  25.7 7.8 %collective-permute-start.4 = (bf16[2,256,256]{2,1,0:T(8,128)(2,1)S(1)}, bf16[2,256,256]{2,1,0:T(8,128)(2,1)S(1)}, u32[]{:S(2)}, u32[]{:S(2)}) collective-permute-start(bf16[2,256,256]{2,1,0:T(8,128)(2,1)S(1)} %collective-permute-done.1.refs_1_), channel_id=1, source_target_pairs={{0,32},{16,112},{32,64},{48,16},{64,96},{80,48},{96,0},{112,80},{1... | collective-permute-start | bytes 786440 | tf_op jit(solution)/shard_map/ppermute | solution.py:478
  27.5 13.8 %copy-start.6 = (bf16[192,768]{1,0:T(8,128)(2,1)}, bf16[192,768]{1,0:T(8,128)(2,1)S(1)}, u32[]{:S(2)}) copy-start(bf16[192,768]{1,0:T(8,128)(2,1)S(1)} %collective-permute-done.18.refs_14_.refs_7_) | copy-start | bytes 884740
  27.5 15.0 %collective-permute-start.16 = (bf16[384,768]{1,0:T(8,128)(2,1)}, bf16[384,768]{1,0:T(8,128)(2,1)S(1)}, u32[]{:S(2)}, u32[]{:S(2)}) collective-permute-start(bf16[384,768]{1,0:T(8,128)(2,1)} %get-tuple-element.26), channel_id=1, source_target_pairs={{0,1},{1,2},{2,3},{3,0},{4,5},{5,6},{6,7},{7,4},{16,19},{17,16},{1... | collective-permute-start | bytes 1769480 | tf_op jit(solution)/shard_map/ppermute | solution.py:478
  30.6 3.0 %copy-start.18 = (bf16[2,256,256]{2,1,0:T(8,128)(2,1)}, bf16[2,256,256]{2,1,0:T(8,128)(2,1)S(1)}, u32[]{:S(2)}) copy-start(bf16[2,256,256]{2,1,0:T(8,128)(2,1)S(1)} %collective-permute-done.3.refs_3_) | copy-start | bytes 786436
  30.6 12.0 %collective-permute-start.19 = (bf16[192,768]{1,0:T(8,128)(2,1)S(1)}, bf16[192,768]{1,0:T(8,128)(2,1)S(1)}, u32[]{:S(2)}, u32[]{:S(2)}) collective-permute-start(bf16[192,768]{1,0:T(8,128)(2,1)S(1)} %collective-permute-done.18.refs_14_.refs_7_), channel_id=1, source_target_pairs={{0,16},{16,0},{32,48},{48,32},{64,80},{80,64},{96,112},{112,96},{1... | collective-permute-start | bytes 884744 | tf_op jit(solution)/shard_map/ppermute | solution.py:478
  32.5 1.0 copy-start.11
  32.5 21.6 %collective-permute-start.6 = (bf16[2,256,512]{2,1,0:T(8,128)(2,1)S(1)}, bf16[2,256,512]{2,1,0:T(8,128)(2,1)S(1)}, u32[]{:S(2)}, u32[]{:S(2)}) collective-permute-start(bf16[2,256,512]{2,1,0:T(8,128)(2,1)S(1)} %collective-permute-done.2.refs_2_), channel_id=1, source_target_pairs={{0,32},{16,112},{32,64},{48,16},{64,96},{80,48},{96,0},{112,80},{1... | collective-permute-start | bytes 1572872 | tf_op jit(solution)/shard_map/ppermute | solution.py:478
  32.5 21.6 %copy-start.10 = (bf16[2,256,512]{2,1,0:T(8,128)(2,1)}, bf16[2,256,512]{2,1,0:T(8,128)(2,1)S(1)}, u32[]{:S(2)}) copy-start(bf16[2,256,512]{2,1,0:T(8,128)(2,1)S(1)} %collective-permute-done.5.refs_0_) | copy-start | bytes 1572868
  32.5 22.1 %collective-permute-start.12 = (bf16[2,256,512]{2,1,0:T(8,128)(2,1)S(1)}, bf16[2,256,512]{2,1,0:T(8,128)(2,1)S(1)}, u32[]{:S(2)}, u32[]{:S(2)}) collective-permute-start(bf16[2,256,512]{2,1,0:T(8,128)(2,1)S(1)} %collective-permute-done.5.refs_0_), channel_id=1, source_target_pairs={{0,32},{16,112},{32,64},{48,16},{64,96},{80,48},{96,0},{112,80},{1... | collective-permute-start | bytes 1572872 | tf_op jit(solution)/shard_map/ppermute | solution.py:478
  41.3 10.0 %collective-permute-start.13 = (bf16[2,256,256]{2,1,0:T(8,128)(2,1)}, bf16[2,256,256]{2,1,0:T(8,128)(2,1)S(1)}, u32[]{:S(2)}, u32[]{:S(2)}) collective-permute-start(bf16[2,256,256]{2,1,0:T(8,128)(2,1)} %get-tuple-element.25.refs_1_), channel_id=1, source_target_pairs={{0,32},{16,112},{32,64},{48,16},{64,96},{80,48},{96,0},{112,80},{1... | collective-permute-start | bytes 786440 | tf_op jit(solution)/shard_map/ppermute | solution.py:478
  42.6 15.4 %copy-start.1 = (bf16[384,768]{1,0:T(8,128)(2,1)}, bf16[384,768]{1,0:T(8,128)(2,1)S(1)}, u32[]{:S(2)}) copy-start(bf16[384,768]{1,0:T(8,128)(2,1)S(1)} %collective-permute-done.16.refs_12_.refs_5_) | copy-start | bytes 1769476
  42.6 8.8 %collective-permute-start.9 = (bf16[2,256,256]{2,1,0:T(8,128)(2,1)}, bf16[2,256,256]{2,1,0:T(8,128)(2,1)S(1)}, u32[]{:S(2)}, u32[]{:S(2)}) collective-permute-start(bf16[2,256,256]{2,1,0:T(8,128)(2,1)} %get-tuple-element.25.refs_1_), channel_id=1, source_target_pairs={{0,16},{16,0},{32,48},{48,32},{64,80},{80,64},{96,112},{112,96},{1... | collective-permute-start | bytes 786440 | tf_op jit(solution)/shard_map/ppermute | solution.py:478
  42.6 15.4 %copy-start.7 = (bf16[192,768]{1,0:T(8,128)(2,1)}, bf16[192,768]{1,0:T(8,128)(2,1)S(1)}, u32[]{:S(2)}) copy-start(bf16[192,768]{1,0:T(8,128)(2,1)S(1)} %collective-permute-done.19.refs_15_.refs_8_) | copy-start | bytes 884740
  42.6 11.6 %collective-permute-start.7 = (bf16[2,256,256]{2,1,0:T(8,128)(2,1)}, bf16[2,256,256]{2,1,0:T(8,128)(2,1)S(1)}, u32[]{:S(2)}, u32[]{:S(2)}) collective-permute-start(bf16[2,256,256]{2,1,0:T(8,128)(2,1)} %copy-done.18), channel_id=1, source_target_pairs={{0,32},{16,112},{32,64},{48,16},{64,96},{80,48},{96,0},{112,80},{1... | collective-permute-start | bytes 786440 | tf_op jit(solution)/shard_map/ppermute | solution.py:478
  51.3 6.7 %copy-start.21 = (bf16[2,256,256]{2,1,0:T(8,128)(2,1)}, bf16[2,256,256]{2,1,0:T(8,128)(2,1)S(1)}, u32[]{:S(2)}) copy-start(bf16[2,256,256]{2,1,0:T(8,128)(2,1)S(1)} %collective-permute-done.13.refs_9_) | copy-start | bytes 786436
  51.3 6.6 %collective-permute-start.17 = (bf16[384,768]{1,0:T(8,128)(2,1)S(1)}, bf16[384,768]{1,0:T(8,128)(2,1)S(1)}, u32[]{:S(2)}, u32[]{:S(2)}) collective-permute-start(bf16[384,768]{1,0:T(8,128)(2,1)S(1)} %collective-permute-done.16.refs_12_.refs_5_), channel_id=1, source_target_pairs={{0,16},{16,0},{32,48},{48,32},{64,80},{80,64},{96,112},{112,96},{1... | collective-permute-start | bytes 1769480 | tf_op jit(solution)/shard_map/ppermute | solution.py:478
  51.3 6.7 %copy-start.22 = (bf16[2,256,256]{2,1,0:T(8,128)(2,1)}, bf16[2,256,256]{2,1,0:T(8,128)(2,1)S(1)}, u32[]{:S(2)}) copy-start(bf16[2,256,256]{2,1,0:T(8,128)(2,1)S(1)} %collective-permute-done.9.refs_5_) | copy-start | bytes 786436
  51.4 3.4 %collective-permute-start.15 = (bf16[2,256,256]{2,1,0:T(8,128)(2,1)S(1)}, bf16[2,256,256]{2,1,0:T(8,128)(2,1)S(1)}, u32[]{:S(2)}, u32[]{:S(2)}) collective-permute-start(bf16[2,256,256]{2,1,0:T(8,128)(2,1)S(1)} %collective-permute-done.13.refs_9_), channel_id=1, source_target_pairs={{0,16},{16,0},{32,48},{48,32},{64,80},{80,64},{96,112},{112,96},{1... | collective-permute-start | bytes 786440 | tf_op jit(solution)/shard_map/ppermute | solution.py:478
  54.1 3.9 %copy-start.23 = (bf16[2,256,256]{2,1,0:T(8,128)(2,1)}, bf16[2,256,256]{2,1,0:T(8,128)(2,1)S(1)}, u32[]{:S(2)}) copy-start(bf16[2,256,256]{2,1,0:T(8,128)(2,1)S(1)} %collective-permute-done.7.refs_3_) | copy-start | bytes 786436
  54.1 3.8 %collective-permute-start.8 = (bf16[2,256,512]{2,1,0:T(8,128)(2,1)S(1)}, bf16[2,256,512]{2,1,0:T(8,128)(2,1)S(1)}, u32[]{:S(2)}, u32[]{:S(2)}) collective-permute-start(bf16[2,256,512]{2,1,0:T(8,128)(2,1)S(1)} %collective-permute-done.5.refs_0_), channel_id=1, source_target_pairs={{0,16},{16,0},{32,48},{48,32},{64,80},{80,64},{96,112},{112,96},{1... | collective-permute-start | bytes 1572872 | tf_op jit(solution)/shard_map/ppermute | solution.py:478
  54.2 3.9 %copy-start.12 = (bf16[2,256,512]{2,1,0:T(8,128)(2,1)}, bf16[2,256,512]{2,1,0:T(8,128)(2,1)S(1)}, u32[]{:S(2)}) copy-start(bf16[2,256,512]{2,1,0:T(8,128)(2,1)S(1)} %collective-permute-done.6.refs_2_) | copy-start | bytes 1572868
  54.2 3.8 %collective-permute-start.10 = (bf16[2,256,512]{2,1,0:T(8,128)(2,1)S(1)}, bf16[2,256,512]{2,1,0:T(8,128)(2,1)S(1)}, u32[]{:S(2)}, u32[]{:S(2)}) collective-permute-start(bf16[2,256,512]{2,1,0:T(8,128)(2,1)S(1)} %collective-permute-done.6.refs_2_), channel_id=1, source_target_pairs={{0,16},{16,0},{32,48},{48,32},{64,80},{80,64},{96,112},{112,96},{1... | collective-permute-start | bytes 1572872 | tf_op jit(solution)/shard_map/ppermute | solution.py:478
  54.7 3.4 %copy-start.13 = (bf16[2,256,512]{2,1,0:T(8,128)(2,1)}, bf16[2,256,512]{2,1,0:T(8,128)(2,1)S(1)}, u32[]{:S(2)}) copy-start(bf16[2,256,512]{2,1,0:T(8,128)(2,1)S(1)} %collective-permute-done.12.refs_8_) | copy-start | bytes 1572868
  54.7 3.3 %collective-permute-start.14 = (bf16[2,256,512]{2,1,0:T(8,128)(2,1)S(1)}, bf16[2,256,512]{2,1,0:T(8,128)(2,1)S(1)}, u32[]{:S(2)}, u32[]{:S(2)}) collective-permute-start(bf16[2,256,512]{2,1,0:T(8,128)(2,1)S(1)} %collective-permute-done.12.refs_8_), channel_id=1, source_target_pairs={{0,16},{16,0},{32,48},{48,32},{64,80},{80,64},{96,112},{112,96},{1... | collective-permute-start | bytes 1572872 | tf_op jit(solution)/shard_map/ppermute | solution.py:478
  54.8 3.3 %copy-start.24 = (bf16[2,256,256]{2,1,0:T(8,128)(2,1)}, bf16[2,256,256]{2,1,0:T(8,128)(2,1)S(1)}, u32[]{:S(2)}) copy-start(bf16[2,256,256]{2,1,0:T(8,128)(2,1)S(1)} %collective-permute-done.15.refs_11_) | copy-start | bytes 786436
  54.8 3.2 %collective-permute-start.11 = (bf16[2,256,256]{2,1,0:T(8,128)(2,1)S(1)}, bf16[2,256,256]{2,1,0:T(8,128)(2,1)S(1)}, u32[]{:S(2)}, u32[]{:S(2)}) collective-permute-start(bf16[2,256,256]{2,1,0:T(8,128)(2,1)S(1)} %collective-permute-done.7.refs_3_), channel_id=1, source_target_pairs={{0,16},{16,0},{32,48},{48,32},{64,80},{80,64},{96,112},{112,96},{1... | collective-permute-start | bytes 786440 | tf_op jit(solution)/shard_map/ppermute | solution.py:478
  57.9 0.9 copy-start.14
  57.9 1.1 copy-start.2
  58.0 1.3 %copy-start.15 = (bf16[2,256,512]{2,1,0:T(8,128)(2,1)}, bf16[2,256,512]{2,1,0:T(8,128)(2,1)S(1)}, u32[]{:S(2)}) copy-start(bf16[2,256,512]{2,1,0:T(8,128)(2,1)S(1)} %collective-permute-done.10.refs_6_) | copy-start | bytes 1572868
  58.0 1.4 %copy-start.16 = (bf16[2,256,512]{2,1,0:T(8,128)(2,1)}, bf16[2,256,512]{2,1,0:T(8,128)(2,1)S(1)}, u32[]{:S(2)}) copy-start(bf16[2,256,512]{2,1,0:T(8,128)(2,1)S(1)} %collective-permute-done.14.refs_10_) | copy-start | bytes 1572868
  65.8 9.5 %collective-permute-start.20 = (bf16[2,272,256]{2,1,0:T(8,128)(2,1)}, bf16[2,272,256]{2,1,0:T(8,128)(2,1)S(1)}, u32[]{:S(2)}, u32[]{:S(2)}) collective-permute-start(bf16[2,272,256]{2,1,0:T(8,128)(2,1)} %get-tuple-element.30), channel_id=1, source_target_pairs={{0,8},{8,0},{1,9},{9,1},{2,10},{10,2},{3,11},{11,3},{4,12},{12,4},... | collective-permute-start | bytes 835592 | tf_op jit(solution)/shard_map/ppermute | solution.py:478
  78.1 37.5 %copy-start.9 = (f32[384]{0:T(512)S(1)}, f32[384]{0:T(512)}, u32[]{:S(2)}) copy-start(f32[384]{0:T(512)} %param.15) | copy-start | bytes 4612
  78.1 12.7 %collective-permute-start.21 = (bf16[512,384]{1,0:T(8,128)(2,1)}, bf16[512,384]{1,0:T(8,128)(2,1)S(1)}, u32[]{:S(2)}, u32[]{:S(2)}) collective-permute-start(bf16[512,384]{1,0:T(8,128)(2,1)} %combine.1.refs_0_), channel_id=1, source_target_pairs={{0,1},{1,2},{2,3},{3,0},{4,5},{5,6},{6,7},{7,4},{16,19},{17,16},{1... | collective-permute-start | bytes 1179656 | tf_op jit(solution)/shard_map/ppermute | solution.py:478
  78.1 12.6 %collective-permute-start.22 = (bf16[512,384]{1,0:T(8,128)(2,1)}, bf16[512,384]{1,0:T(8,128)(2,1)S(1)}, u32[]{:S(2)}, u32[]{:S(2)}) collective-permute-start(bf16[512,384]{1,0:T(8,128)(2,1)} %combine.1.refs_0_), channel_id=1, source_target_pairs={{0,3},{1,0},{2,1},{3,2},{4,7},{5,4},{6,5},{7,6},{16,17},{17,18},{1... | collective-permute-start | bytes 1179656 | tf_op jit(solution)/shard_map/ppermute | solution.py:478
  90.7 9.0 %copy-start.3 = (bf16[512,384]{1,0:T(8,128)(2,1)}, bf16[512,384]{1,0:T(8,128)(2,1)S(1)}, u32[]{:S(2)}) copy-start(bf16[512,384]{1,0:T(8,128)(2,1)S(1)} %collective-permute-done.21.refs_1_) | copy-start | bytes 1179652
  90.7 9.0 %collective-permute-start.23 = (bf16[512,384]{1,0:T(8,128)(2,1)S(1)}, bf16[512,384]{1,0:T(8,128)(2,1)S(1)}, u32[]{:S(2)}, u32[]{:S(2)}) collective-permute-start(bf16[512,384]{1,0:T(8,128)(2,1)S(1)} %collective-permute-done.21.refs_1_), channel_id=1, source_target_pairs={{0,1},{1,2},{2,3},{3,0},{4,5},{5,6},{6,7},{7,4},{16,19},{17,16},{1... | collective-permute-start | bytes 1179656 | tf_op jit(solution)/shard_map/ppermute | solution.py:478
  90.7 9.0 %copy-start.4 = (bf16[512,384]{1,0:T(8,128)(2,1)}, bf16[512,384]{1,0:T(8,128)(2,1)S(1)}, u32[]{:S(2)}) copy-start(bf16[512,384]{1,0:T(8,128)(2,1)S(1)} %collective-permute-done.22.refs_2_) | copy-start | bytes 1179652
  106.0 9.6 %collective-permute-start.24 = (bf16[512,384]{1,0:T(8,128)(2,1)}, bf16[512,384]{1,0:T(8,128)(2,1)S(1)}, u32[]{:S(2)}, u32[]{:S(2)}) collective-permute-start(bf16[512,384]{1,0:T(8,128)(2,1)} %get-tuple-element.32), channel_id=1, source_target_pairs={{0,4},{1,5},{2,6},{3,7},{4,0},{5,1},{6,2},{7,3},{8,12},{9,13},{10,... | collective-permute-start | bytes 1179656 | tf_op jit(solution)/shard_map/ppermute | solution.py:478
  (4 other events, 2.8 us)

commit v3 on v2

v3 whole, which is shorter than its diff:
```python
import functools

import jax
import jax.numpy as jnp
from jax import lax
from jax.experimental import pallas as pl
from jax.experimental.pallas import tpu as pltpu
from jax.sharding import PartitionSpec as P

HEAD_DIM = 128
TILE = 128
NORM_EPS = 1e-06
LOG2E = 1.4426950408889634
ANY = pl.BlockSpec(memory_space=pl.ANY)
HBM = pl.BlockSpec(memory_space=pltpu.HBM)
VMEM = pl.BlockSpec(memory_space=pltpu.VMEM)
SMEM = pl.BlockSpec(memory_space=pltpu.SMEM)
F32 = jnp.float32
BF16 = jnp.bfloat16


def vmem(mib):
    return pltpu.CompilerParams(vmem_limit_bytes=mib * 1024 * 1024)


def rows_dot(a, b):
    return lax.dot_general(a, b, (((1,), (1,)), ((), ())), preferred_element_type=F32)


def rms_norm(part, gain):
    squares = jnp.mean(part * part, axis=-1, keepdims=True)
    return (part * lax.rsqrt(squares + NORM_EPS) * gain).astype(BF16)


def split_heads(full, gain_row, first):
    parts = [full[:, h * HEAD_DIM:(h + 1) * HEAD_DIM] for h in range(3)]
    if gain_row is None:
        parts = [part.astype(BF16) for part in parts]
    else:
        parts = [rms_norm(part, gain_row) for part in parts]
    return jnp.where(first, parts[0], parts[2]), parts[1], jnp.where(first, parts[2], parts[0])


LANES = tuple(slice(k * HEAD_DIM, (k + 1) * HEAD_DIM) for k in range(4))
CHUNKS = 4


def project_kernel(
    place_ref, x_ref, w_ref, w_out_ref, scale_ref, shift_ref, qg_ref, kg_ref,
    kept_ref, sent_ref, home_ref, q_sent_ref, ahead_ref, apart_ref,
    n_scr, x_scr, w_scr, o_scr, kept_scr, sent_scr, home_scr, q_sent_scr,
    x_sem, w_sem, o_sem, out_sem,
):
    rows, width = x_scr.shape
    chunk = rows // CHUNKS
    wide = w_ref.shape[2]
    x_copies = [
        pltpu.make_async_copy(
            x_ref.at[pl.ds(i * chunk, chunk)], x_scr.at[pl.ds(i * chunk, chunk)], x_sem.at[i]
        )
        for i in range(CHUNKS)
    ]
    w_copies = [
        pltpu.make_async_copy(w_ref.at[j], w_scr.at[:, pl.ds(at * wide, wide)], w_sem.at[at])
        for at, j in enumerate((1, 2, 0))
    ]
    o_load = pltpu.make_async_copy(w_out_ref, o_scr, o_sem.at[0])
    for copy in x_copies + w_copies + [o_load]:
        copy.start()
    gain = 1.0 + scale_ref[...]
    shift = shift_ref[...]
    first = place_ref[0] == 0
    spans = [slice(i * chunk, (i + 1) * chunk) for i in range(CHUNKS)]

    def normalise(i):
        x_copies[i].wait()

        def one_block(step, carry):
            at = pl.ds(pl.multiple_of(i * chunk + step * 16, 16), 16)
            x = x_scr[at, :].astype(F32)
            centred = x - jnp.mean(x, axis=1, keepdims=True)
            var = jnp.mean(centred * centred, axis=1, keepdims=True)
            n_scr[at, :] = (centred * lax.rsqrt(var + NORM_EPS) * gain + shift).astype(BF16)
            return carry

        lax.fori_loop(0, chunk // 16, one_block, 0, unroll=True)

    normalise(0)
    w_copies[0].wait()
    w_copies[1].wait()
    for i, at in enumerate(spans):
        if i + 1 < CHUNKS:
            normalise(i + 1)
        full = jnp.dot(n_scr[at, :], w_scr[:, :2 * wide], preferred_element_type=F32)
        for j, gain_row in ((0, kg_ref[...]), (1, None)):
            own, mid, other = split_heads(full[:, j * wide:(j + 1) * wide], gain_row, first)
            kept_scr[at, LANES[j]] = own
            kept_scr[at, LANES[2 + j]] = mid
            sent_scr[at, LANES[j]] = other
    out_copies = [
        pltpu.make_async_copy(sent_scr, sent_ref, out_sem.at[0]),
        pltpu.make_async_copy(kept_scr, kept_ref, out_sem.at[1]),
        pltpu.make_async_copy(home_scr, home_ref, out_sem.at[2]),
        pltpu.make_async_copy(q_sent_scr, q_sent_ref, out_sem.at[3]),
    ]
    out_copies[0].start()
    out_copies[1].start()
    o_load.wait()
    cols, part = ahead_ref.shape[1] // 2, apart_ref.shape[0]
    half = pl.ds(pl.multiple_of(place_ref[1] * part, 16), part)
    o_copies = []
    for j in range(2):
        ahead = pl.ds(pl.multiple_of(place_ref[2 + j] * cols, TILE), cols)
        apart = pl.ds(pl.multiple_of(place_ref[4 + j] * cols, TILE), cols)
        to = pl.ds(j * cols, cols)
        o_copies += [
            pltpu.make_async_copy(o_scr.at[:, ahead], ahead_ref.at[:, to], o_sem.at[1 + 2 * j]),
            pltpu.make_async_copy(o_scr.at[half, apart], apart_ref.at[:, to], o_sem.at[2 + 2 * j]),
        ]
    for copy in o_copies:
        copy.start()
    w_copies[2].wait()
    for at in spans:
        full = jnp.dot(n_scr[at, :], w_scr[:, 2 * wide:], preferred_element_type=F32)
        own, mid, other = split_heads(full, qg_ref[...], first)
        home_scr[at, LANES[0]] = own
        home_scr[at, LANES[1]] = mid
        q_sent_scr[at, LANES[0]] = other
        q_sent_scr[at, LANES[1]] = mid
    out_copies[2].start()
    out_copies[3].start()
    for copy in out_copies + o_copies:
        copy.wait()


def project(place, tokens, w, w_out, scale, shift, q_gain, k_gain):
    frames, half_tok, width = tokens.shape
    rows = frames * half_tok
    shapes = [(rows, 4 * HEAD_DIM)] + [(rows, 2 * HEAD_DIM)] * 3
    depth, cols = w_out.shape[0], w_out.shape[1] // 4
    blocks = [(depth, cols), (depth // 2, cols)]
    pieces = pl.pallas_call(
        project_kernel,
        out_shape=[jax.ShapeDtypeStruct(shape, BF16) for shape in shapes + blocks],
        in_specs=[SMEM, ANY, ANY, ANY] + [VMEM] * 4,
        out_specs=[ANY] * 6,
        scratch_shapes=[
            pltpu.VMEM((rows, width), BF16),
            pltpu.VMEM((rows, width), BF16),
            pltpu.VMEM((width, 9 * HEAD_DIM), BF16),
            pltpu.VMEM(w_out.shape, BF16),
        ]
        + [pltpu.VMEM(shape, BF16) for shape in shapes]
        + [
            pltpu.SemaphoreType.DMA((CHUNKS,)),
            pltpu.SemaphoreType.DMA((3,)),
            pltpu.SemaphoreType.DMA((5,)),
            pltpu.SemaphoreType.DMA((4,)),
        ],
        compiler_params=vmem(56),
        cost_estimate=pl.CostEstimate(
            flops=2 * rows * width * 9 * HEAD_DIM, bytes_accessed=12_000_000, transcendentals=0
        ),
        name="project",
    )(
        place, tokens.reshape(rows, width), w, w_out,
        scale.reshape(1, -1), shift.reshape(1, -1), q_gain.reshape(1, -1), k_gain.reshape(1, -1),
    )
    return [piece.reshape(frames, half_tok, -1) for piece in pieces[:4]] + list(pieces[4:])


META_BLOCKS = 1
META_FRAME = 9
META_BAND = 10
META_FAR = 12
ONES = slice(2 * HEAD_DIM, 3 * HEAD_DIM)
FACTOR = LOG2E * HEAD_DIM ** (-0.5)


def weights_of(q, keys):
    return jnp.exp2(rows_dot(q, keys) * FACTOR)


def key_copies(meta_ref, blocks, pieces, kvo, kvm, sem):
    half = kvm.shape[1]
    s = meta_ref[0]
    near = pl.ds(pl.multiple_of(s * half, half), half)
    away = pl.ds(pl.multiple_of((1 - s) * half, half), half)
    two = pl.ds(0, 2 * HEAD_DIM)
    copies = []
    for at, block in enumerate(blocks):
        frames = pl.ds(2 * block, 2)
        kept, received = pieces[2 * at], pieces[2 * at + 1]
        copies += [
            pltpu.make_async_copy(kept.at[:, :, two], kvo.at[frames, near, two], sem.at[3 * at]),
            pltpu.make_async_copy(
                kept.at[:, :, pl.ds(2 * HEAD_DIM, 2 * HEAD_DIM)],
                kvm.at[frames, :, two],
                sem.at[3 * at + 1],
            ),
            pltpu.make_async_copy(received, kvo.at[frames, away, two], sem.at[3 * at + 2]),
        ]
    return copies


def query_copies(home_ref, away_ref, q_scr, sem, base):
    half = home_ref.shape[1]
    return [
        pltpu.make_async_copy(home_ref, q_scr.at[:, pl.ds(0, half)], sem.at[base]),
        pltpu.make_async_copy(away_ref, q_scr.at[:, pl.ds(half, half)], sem.at[base + 1]),
    ]


def add_frame(fi, at, q_scr, kvo, kvm, acc_o, acc_m):
    for lanes, kv, acc in (
        (slice(0, HEAD_DIM), kvo, acc_o),
        (slice(HEAD_DIM, 2 * HEAD_DIM), kvm, acc_m),
    ):
        keys = kv[at]
        weights = weights_of(q_scr[fi, :, lanes], keys[:, :HEAD_DIM]).astype(BF16)
        acc[fi] += jnp.dot(weights, keys[:, HEAD_DIM:], preferred_element_type=F32)


def attend_kernel(meta_ref, home_ref, away_ref, *refs):
    pieces = refs[0:16]
    out_ref, mid_ref, ret_ref = refs[18:21]
    q_scr, kvo, kvm, acc_o, acc_m, sem = refs[21:27]
    n_frames, half = kvm.shape[0], kvm.shape[1]
    s = meta_ref[0]
    moves = key_copies(
        meta_ref, [meta_ref[META_BLOCKS + r] for r in range(8)], pieces, kvo, kvm, sem
    )
    near = query_copies(home_ref, away_ref, q_scr, sem, 24) + moves[:6]
    band = moves[15:18]
    rest = moves[6:15] + moves[18:]
    for copy in near + band + rest:
        copy.start()
    kvo[:, :, ONES] = jnp.ones((n_frames, 2 * half, HEAD_DIM), BF16)
    kvm[:, :, ONES] = jnp.ones((n_frames, half, HEAD_DIM), BF16)
    acc_o[...] = jnp.zeros_like(acc_o)
    acc_m[...] = jnp.zeros_like(acc_m)
    eye = lax.broadcasted_iota(jnp.int32, (TILE, TILE), 0) == lax.broadcasted_iota(
        jnp.int32, (TILE, TILE), 1
    )
    start = meta_ref[META_FRAME] // 4 * 4

    def add_frames(fi, low, high):
        def one_frame(kf, carry):
            add_frame(fi, kf, q_scr, kvo, kvm, acc_o, acc_m)
            return carry

        lax.fori_loop(low, high + 1, one_frame, 0)

    spans = []
    for fi in range(2):
        frame = meta_ref[META_FRAME] + fi
        width = meta_ref[META_BAND + fi]
        spans.append((jnp.maximum(frame - width, 0), jnp.minimum(frame + width, n_frames - 1)))
    for copy in near:
        copy.wait()
    for fi, (low, high) in enumerate(spans):
        add_frames(fi, jnp.maximum(low, start), jnp.minimum(high, start + 3))
    for copy in band:
        copy.wait()
    for fi, (low, high) in enumerate(spans):
        add_frames(fi, low, start - 1)
        add_frames(fi, start + 4, high)
    for copy in rest:
        copy.wait()
    for fi in range(2):
        for r in range(2):
            for t in range(2):
                at = slice(r * half + t * TILE, r * half + (t + 1) * TILE)
                tile = 2 * (s ^ r) + t
                base = META_FAR + ((fi * 4 + tile) * 4) * 2
                entries = [(meta_ref[base + 2 * j], meta_ref[base + 2 * j + 1]) for j in range(4)]
                flags = []
                for j in range(4):
                    fresh = jnp.bool_(True)
                    for i in range(j):
                        same = (entries[i][0] == entries[j][0]) & (entries[i][1] == entries[j][1])
                        fresh = fresh & jnp.logical_not(same)
                    flags.append(fresh)
                mid_flags = [fresh & (entry[1] // 2 == s) for fresh, entry in zip(flags, entries)]
                for lanes, kv, acc, shown, tiles in (
                    (slice(0, HEAD_DIM), kvo, acc_o, flags, 4),
                    (slice(HEAD_DIM, 2 * HEAD_DIM), kvm, acc_m, mid_flags, 2),
                ):
                    keys = jnp.concatenate(
                        [
                            kv[kf, pl.ds(pl.multiple_of((kt % tiles) * TILE, TILE), TILE), :]
                            for kf, kt in entries
                        ],
                        axis=0,
                    )
                    weights = weights_of(q_scr[fi, at, lanes], keys[:, :HEAD_DIM])
                    weights = jnp.concatenate(
                        [
                            weights[:, j * TILE:(j + 1) * TILE] * jnp.where(shown[j], 1.0, 0.0)
                            for j in range(4)
                        ],
                        axis=1,
                    ).astype(BF16)
                    acc[fi, at, :] += jnp.dot(
                        weights, keys[:, HEAD_DIM:], preferred_element_type=F32
                    )

        attended = (acc_o[fi, :, :HEAD_DIM] / acc_o[fi, :, HEAD_DIM:]).astype(BF16)
        out_ref[fi * half:(fi + 1) * half, :] = attended[:half]
        ret_ref[fi, :half, :HEAD_DIM] = attended[half:]
        mid_ref[fi] = acc_m[fi, :half, :]
        ret_ref[fi, :half, HEAD_DIM:] = acc_m[fi, half:, :HEAD_DIM].astype(BF16)
        dens = []
        for g in range(2):
            den = acc_m[fi, half + g * TILE:half + (g + 1) * TILE, HEAD_DIM:]
            dens.append(jnp.sum(jnp.where(eye, den, 0.0), axis=0, keepdims=True))
        den = jnp.concatenate(dens, axis=0)
        upper = den.astype(BF16).astype(F32)
        block = jnp.concatenate([upper, den - upper, jnp.zeros((12, TILE), F32)], axis=0)
        ret_ref[fi, half:, :HEAD_DIM] = block.astype(BF16)
        ret_ref[fi, half:, HEAD_DIM:] = jnp.zeros((16, HEAD_DIM), BF16)


def attend(meta, q_home, q_away, pieces, waited, n_frames):
    frames, half, _ = q_home.shape
    return pl.pallas_call(
        attend_kernel,
        out_shape=[
            jax.ShapeDtypeStruct((frames * half, HEAD_DIM), BF16),
            jax.ShapeDtypeStruct((frames, half, 2 * HEAD_DIM), F32),
            jax.ShapeDtypeStruct((frames, half + 16, 2 * HEAD_DIM), BF16),
        ],
        in_specs=[SMEM, HBM, HBM]
        + [HBM if at in (0, 1, 3, 13, 15) else ANY for at in range(len(pieces))]
        + [ANY] * len(waited),
        out_specs=[VMEM] * 3,
        scratch_shapes=[
            pltpu.VMEM((frames, 2 * half, 2 * HEAD_DIM), BF16),
            pltpu.VMEM((n_frames, 2 * half, 3 * HEAD_DIM), BF16),
            pltpu.VMEM((n_frames, half, 3 * HEAD_DIM), BF16),
            pltpu.VMEM((frames, 2 * half, 2 * HEAD_DIM), F32),
            pltpu.VMEM((frames, 2 * half, 2 * HEAD_DIM), F32),
            pltpu.SemaphoreType.DMA((26,)),
        ],
        compiler_params=vmem(58),
        cost_estimate=pl.CostEstimate(
            flops=9_000_000_000, bytes_accessed=8_000_000, transcendentals=5_000_000
        ),
        name="attend",
    )(meta, q_home, q_away, *pieces, *waited)


def combine_kernel(place_ref, home_ref, mid_ref, got_ref, out0_ref, out1_ref, home, mid, got, sem):
    half = mid.shape[1]
    copies = [
        pltpu.make_async_copy(source, target, sem.at[k])
        for k, (source, target) in enumerate(
            ((got_ref, got), (mid_ref, mid), (home_ref, home))
        )
    ]
    for copy in copies:
        copy.start()
    s = place_ref[0]
    own_lanes = pl.ds(pl.multiple_of(s * 2 * HEAD_DIM, HEAD_DIM), HEAD_DIM)
    other_lanes = pl.ds(pl.multiple_of((1 - s) * 2 * HEAD_DIM, HEAD_DIM), HEAD_DIM)
    eye = lax.broadcasted_iota(jnp.int32, (TILE, TILE), 0) == lax.broadcasted_iota(
        jnp.int32, (TILE, TILE), 1
    )
    ones = jnp.ones((TILE, TILE), BF16)
    for copy in copies:
        copy.wait()
    for fi, out_ref in enumerate((out0_ref, out1_ref)):
        out_ref[:, own_lanes] = home[fi * half:(fi + 1) * half, :]
        out_ref[:, other_lanes] = got[fi, :half, :HEAD_DIM]
        tail = got[fi, half:, :HEAD_DIM].astype(F32)
        for g in range(2):
            at = slice(g * TILE, (g + 1) * TILE)
            upper = jnp.where(eye, tail[g:g + 1, :], 0.0).astype(BF16)
            lower = jnp.where(eye, tail[2 + g:3 + g, :], 0.0).astype(BF16)
            den = jnp.dot(upper, ones, preferred_element_type=F32) + jnp.dot(
                lower, ones, preferred_element_type=F32
            )
            num = mid[fi, at, :HEAD_DIM] + got[fi, at, HEAD_DIM:].astype(F32)
            out_ref[at, HEAD_DIM:2 * HEAD_DIM] = (num / (mid[fi, at, HEAD_DIM:] + den)).astype(BF16)


def combine(place, home, mid, got):
    frames, half, _ = mid.shape
    return pl.pallas_call(
        combine_kernel,
        out_shape=[jax.ShapeDtypeStruct((half, 3 * HEAD_DIM), BF16)] * frames,
        in_specs=[SMEM, ANY, ANY, ANY],
        out_specs=[VMEM] * frames,
        scratch_shapes=[
            pltpu.VMEM(home.shape, home.dtype),
            pltpu.VMEM(mid.shape, mid.dtype),
            pltpu.VMEM(got.shape, got.dtype),
            pltpu.SemaphoreType.DMA((3,)),
        ],
        compiler_params=vmem(6),
        cost_estimate=pl.CostEstimate(
            flops=50_000_000, bytes_accessed=1_500_000, transcendentals=0
        ),
        name="combine",
    )(place, home, mid, got)


def after_kernel(*refs):
    pass


def after(x, *waited):
    return pl.pallas_call(
        after_kernel,
        out_shape=jax.ShapeDtypeStruct(x.shape, x.dtype),
        in_specs=[ANY] * (1 + len(waited)),
        out_specs=ANY,
        input_output_aliases={0: 0},
        compiler_params=vmem(2),
        name="after",
    )(x, *waited)


def output_kernel(place_ref, *refs):
    mixed, w_out_ref = refs[0:4], refs[4]
    ahead_ref, behind_ref, apart_ref, swapped_ref = refs[5:9]
    kept_ref, sent_ref, h_scr, w_scr, h_sem, w_sem = refs[9:15]
    cols = kept_ref.shape[1]
    core = place_ref[1]
    width = mixed[0].shape[1]
    copies = [
        pltpu.make_async_copy(mixed[k], h_scr.at[:, pl.ds(k * width, width)], h_sem.at[k])
        for k in range(4)
    ]
    depth, part = ahead_ref.shape[0], apart_ref.shape[0]
    for j in range(2):
        block = pl.ds(pl.multiple_of(place_ref[6 + j] * cols, TILE), cols)
        copies.append(
            pltpu.make_async_copy(
                w_out_ref.at[:, block],
                w_scr.at[pl.ds(0, depth), pl.ds(j * cols, cols)],
                w_sem.at[j],
            )
        )
    for k, (source, base) in enumerate(
        (
            (ahead_ref, depth),
            (behind_ref, 2 * depth),
            (apart_ref, 3 * depth + core * part),
            (swapped_ref, 3 * depth + (1 - core) * part),
        )
    ):
        at = pl.ds(pl.multiple_of(base, 16), source.shape[0])
        copies.append(pltpu.make_async_copy(source, w_scr.at[at], w_sem.at[2 + k]))
    for copy in copies:
        copy.start()
    for copy in copies:
        copy.wait()
    sent_ref[...] = jnp.dot(
        h_scr[...], w_scr[:, cols:], preferred_element_type=F32
    ).astype(BF16)
    kept_ref[...] = jnp.dot(h_scr[...], w_scr[:, :cols], preferred_element_type=F32)


def output(place, mixed, w_out, w_parts):
    rows, width = mixed[0].shape
    cols = w_parts[0].shape[1] // 2
    return pl.pallas_call(
        output_kernel,
        out_shape=[
            jax.ShapeDtypeStruct((rows, cols), F32),
            jax.ShapeDtypeStruct((rows, cols), BF16),
        ],
        in_specs=[SMEM] + [ANY] * 9,
        out_specs=[VMEM] * 2,
        scratch_shapes=[
            pltpu.VMEM((rows, 4 * width), BF16),
            pltpu.VMEM((4 * width, 2 * cols), BF16),
            pltpu.SemaphoreType.DMA((4,)),
            pltpu.SemaphoreType.DMA((6,)),
        ],
        compiler_params=vmem(10),
        cost_estimate=pl.CostEstimate(
            flops=16 * rows * width * cols, bytes_accessed=4_000_000, transcendentals=0
        ),
        name="output",
    )(place, *mixed, w_out, *w_parts)


def move(axis, to, x):
    axes = axis if isinstance(axis, tuple) else (axis,)
    count = 1
    for name in axes:
        count *= lax.axis_size(name)
    return lax.ppermute(x, axis, [(i, to(i)) for i in range(count)])


def z_step(head, step):
    return head // 4 * 4 + (head + step) % 4


def z_by_core(step, i):
    frame, head = i // 8, i % 8
    return frame * 8 + z_step(head, step if frame % 2 == 0 else 4 - step)


swap_core = functools.partial(move, "frame", lambda i: i ^ 1)
out_y = functools.partial(move, "frame", lambda i: (i + (2 if i % 2 == 0 else 6)) % 8)
in_y = functools.partial(move, "frame", lambda i: (i + (6 if i % 2 == 0 else 2)) % 8)
cross_y = functools.partial(move, "frame", lambda i: (i + 4) % 8)
swap_half = functools.partial(move, "spatial", lambda i: i ^ 1)
cross_z = functools.partial(move, "head", lambda i: z_step(i, 2))
out_z = functools.partial(move, ("frame", "head"), functools.partial(z_by_core, 1))
in_z = functools.partial(move, ("frame", "head"), functools.partial(z_by_core, 3))
swap_x = functools.partial(move, "head", lambda i: i ^ 4)


def gather_z(x):
    return [x, out_z(x), in_z(x), cross_z(x)]


def shards(tokens, w_qkv, w_out, shift, scale, gate, q_gain, k_gain, band, far_tiles):
    frames_dev, half_tok, model_width = tokens.shape
    n_frames = band.shape[0]
    f = lax.axis_index("frame")
    s = lax.axis_index("spatial")
    g = lax.axis_index("head")
    core, y, z, side = f % 2, f // 2, g % 4, g // 4

    step = jnp.where(core == 0, 1, 3)
    w = jnp.transpose(w_qkv, (1, 0, 2))
    blocks_of_w = [(z + by) % 4 + 4 * to for by in (step, 2, 0) for to in (side, 1 - side)]
    place = jnp.stack([s, core] + blocks_of_w)
    kept, sent, q_home, q_send, w_ahead, w_apart = project(
        place, tokens, w, w_out, scale, shift, q_gain, k_gain
    )
    away = swap_half(sent)
    q_away = swap_half(q_send)
    kept_other, kept_first, kept_second = swap_core(kept), out_y(kept), in_y(kept)
    away_other, away_first, away_second = swap_core(away), out_y(away), in_y(away)
    away_across = cross_y(away)
    ahead = (y + jnp.where(core == 0, 3, 1)) % 4
    behind = (y + jnp.where(core == 0, 1, 3)) % 4
    apart = (y + 2) % 4
    blocks = jnp.stack(
        [
            2 * y + core, 2 * y + 1 - core,
            2 * ahead + core, 2 * behind + core,
            2 * behind + 1 - core, 2 * ahead + 1 - core,
            2 * apart + core, 2 * apart + 1 - core,
        ]
    )
    start = f * frames_dev
    meta = jnp.concatenate(
        [
            s.reshape(1),
            blocks,
            start.reshape(1),
            lax.dynamic_slice_in_dim(band, start, frames_dev, 0),
            lax.dynamic_slice_in_dim(far_tiles, start, frames_dev, 0).reshape(-1),
        ]
    ).astype(jnp.int32)
    kept_first = after(kept_first, kept_second)
    kept_across = out_y(kept_first)
    w_ahead, w_apart = out_z(w_ahead), cross_z(w_apart)
    pieces = [kept, away, kept_other, away_other]
    for kept_piece, away_piece in (
        (kept_first, away_first),
        (kept_second, away_second),
    ):
        pieces += [kept_piece, away_piece]
    for kept_piece, away_piece in (
        (kept_first, away_first),
        (kept_second, away_second),
    ):
        pieces += [swap_core(kept_piece), swap_core(away_piece)]
    pieces += [kept_across, away_across, swap_core(kept_across), swap_core(away_across)]
    home, mid_sums, back = attend(
        meta, q_home, q_away, pieces, [w_ahead, w_apart], n_frames
    )
    w_parts = [w_ahead, swap_core(w_ahead), w_apart, swap_core(w_apart)]
    totals = []
    for mixed in combine(place, home, mid_sums, swap_half(back)):
        kept_part, sent_part = output(place, gather_z(mixed), w_out, w_parts)
        totals.append(kept_part + swap_x(sent_part).astype(F32))
    return jnp.stack([(total * gate).astype(BF16) for total in totals])


def solution(mesh):
    return jax.shard_map(
        shards,
        mesh=mesh,
        in_specs=(
            P("frame", "spatial", None),
            P(None, None, "head"),
            P("head", None),
            P(),
            P(),
            P("head"),
            P(),
            P(),
            P(),
            P(),
        ),
        out_specs=P("frame", "spatial", "head"),
        check_vma=False,
    )
```

time: 118 us -> 106 us (0.90)
  waiting for transfers between devices: 50.7 us -> 30.1 us
  starting transfers between devices: 27 us -> 44.4 us
  Pallas kernels: 32.4 us -> 23.9 us
  local copies, waits for them, and re-layouts: 5.14 us -> 6.5 us
    ppermute x25 -> x29, waiting for transfers between devices: 50.7 us -> 30.1 us  [move(): return lax.ppermute(x, axis, [(i, to(i)) for i in range(count)])]
    ppermute x25 -> x29, starting transfers between devices: 27 us -> 44.4 us  [move(): return lax.ppermute(x, axis, [(i, to(i)) for i in range(count)])]
    pallas_call x4, Pallas kernels: 26.9 us -> 19.6 us  [the longest x1 10.9 us: project(): pl.pallas_call(project_kernel, out_shape=[jax.ShapeDtypeStruct(shape, BF1...]
    convert_element_type x1 -> x0, other arithmetic: 1.98 us -> none  [shards(): return (total * gate).astype(BF16).reshape(frames_dev, half_tok, -1)]
    unnamed x54 -> x40, local copies, waits for them, and re-layouts: 3.49 us -> 4.8 us
    pallas_call x1 -> x2, Pallas kernels: 5.51 us -> 4.32 us  [output(): pl.pallas_call(output_kernel, out_shape=[jax.ShapeDtypeStruct((rows, cols...]
  transfers between devices with their start and end apart: 25 -> 29, of which waited for: 9 -> 9; matrix products, arithmetic and copies ran while one was open for 1% -> 1% of each run, Pallas kernels for 6% -> 12%
where the time goes in v3:
time: 106 us
  starting transfers between devices  44.4 us (42%)
  waiting for transfers between devices  30.1 us (28%)
  Pallas kernels  23.9 us (23%)
  local copies, waits for them, and re-layouts  6.5 us (6%)
    ppermute x29, starting transfers between devices, move(): return lax.ppermute(x, axis, [(i, to(i)) for i in range(count)])  44.4 us
    ppermute x29, waiting for transfers between devices, move(): return lax.ppermute(x, axis, [(i, to(i)) for i in range(count)])  30.1 us
    pallas_call x1, Pallas kernels, project(): pl.pallas_call(project_kernel, out_shape=[jax.ShapeDtypeStruct(shape, BF1...  10.9 us
    pallas_call x1, Pallas kernels, attend(): pl.pallas_call(attend_kernel, out_shape=[jax.ShapeDtypeStruct((frames * h...  7.65 us
    unnamed x40, local copies, waits for them, and re-layouts  4.8 us
    pallas_call x2, Pallas kernels, output(): pl.pallas_call(output_kernel, out_shape=[jax.ShapeDtypeStruct((rows, cols...  4.32 us
  transfers between devices with their start and end apart: 29, of which 9 were waited for; matrix products, arithmetic and copies ran while one was open for 1% of the time, Pallas kernels for 12%

profile of v3, /device:TPU:0, one launch (start us, length us, event | category | flops | bytes accessed | tf_op | source)
XLA Modules:
  0.0 106.1 jit_solution(6605699583765774156)
XLA Ops:
  0.0 0.6 stack.68.place_ref
  0.6 10.9 %project.1 = (bf16[512,512]{1,0:T(8,128)(2,1)}, bf16[512,256]{1,0:T(8,128)(2,1)}, bf16[512,256]{1,0:T(8,128)(2,1)}, bf16[512,256]{1,0:T(8,128)(2,1)}, bf16[384,7...) custom-call(s32[8]{0:T(128)} %stack.68.place_ref, bf16[512,3072]{1,0:T(8,128)(2,1)} %bitcast.32, bf16[3,3072,384]{2,1,0:T(8,128)(2,1)} %bitcast.31, ...), custom_call_target="tpu_custom_call" | custom-call | flops 3623878656 | bytes 12000000 | tf_op jit(solution)/shard_map/project/pallas_call | solution.py:142
  11.5 1.7 %collective-permute-start.4 = (bf16[2,256,512]{2,1,0:T(8,128)(2,1)}, bf16[2,256,512]{2,1,0:T(8,128)(2,1)S(1)}, u32[]{:S(2)}, u32[]{:S(2)}) collective-permute-start(bf16[2,256,512]{2,1,0:T(8,128)(2,1)} %bitcast.33), channel_id=1, source_target_pairs={{0,32},{16,112},{32,64},{48,16},{64,96},{80,48},{96,0},{112,80},{1... | collective-permute-start | bytes 1572872 | tf_op jit(solution)/shard_map/ppermute | solution.py:495
  13.2 1.6 %collective-permute-start.5 = (bf16[2,256,512]{2,1,0:T(8,128)(2,1)}, bf16[2,256,512]{2,1,0:T(8,128)(2,1)S(1)}, u32[]{:S(2)}, u32[]{:S(2)}) collective-permute-start(bf16[2,256,512]{2,1,0:T(8,128)(2,1)} %bitcast.34), channel_id=1, source_target_pairs={{0,96},{16,48},{32,0},{48,80},{64,32},{80,112},{96,64},{112,16},{1... | collective-permute-start | bytes 1572872 | tf_op jit(solution)/shard_map/ppermute | solution.py:495
  14.8 1.6 %collective-permute-start.1 = (bf16[2,256,256]{2,1,0:T(8,128)(2,1)}, bf16[2,256,256]{2,1,0:T(8,128)(2,1)S(1)}, u32[]{:S(2)}, u32[]{:S(2)}) collective-permute-start(bf16[2,256,256]{2,1,0:T(8,128)(2,1)} %bitcast.38), channel_id=1, source_target_pairs={{0,8},{8,0},{1,9},{9,1},{2,10},{10,2},{3,11},{11,3},{4,12},{12,4},... | collective-permute-start | bytes 786440 | tf_op jit(solution)/shard_map/ppermute | solution.py:495
  16.4 0.5 collective-permute-start
  16.8 4.0 %collective-permute-start.17 = (bf16[192,768]{1,0:T(8,128)(2,1)}, bf16[192,768]{1,0:T(8,128)(2,1)S(1)}, u32[]{:S(2)}, u32[]{:S(2)}) collective-permute-start(bf16[192,768]{1,0:T(8,128)(2,1)} %get-tuple-element.25), channel_id=1, source_target_pairs={{0,2},{1,3},{2,0},{3,1},{4,6},{5,7},{6,4},{7,5},{8,10},{9,11},{10,... | collective-permute-start | bytes 884744 | tf_op jit(solution)/shard_map/ppermute | solution.py:495
  20.8 3.5 %collective-permute-done.1.refs_1_ = bf16[2,256,256]{2,1,0:T(8,128)(2,1)S(1)} collective-permute-done((bf16[2,256,256]{2,1,0:T(8,128)(2,1)}, bf16[2,256,256]{2,1,0:T(8,128)(2,1)S(1)}, u32[]{:S(2)}, u32[]{:S(2)}) %collective-permute-start.1) | collective-permute-done | bytes 262176 | tf_op jit(solution)/shard_map/ppermute | solution.py:495
  24.3 1.8 %collective-permute-start.7 = (bf16[2,256,256]{2,1,0:T(8,128)(2,1)S(1)}, bf16[2,256,256]{2,1,0:T(8,128)(2,1)S(1)}, u32[]{:S(2)}, u32[]{:S(2)}) collective-permute-start(bf16[2,256,256]{2,1,0:T(8,128)(2,1)S(1)} %collective-permute-done.1.refs_1_), channel_id=1, source_target_pairs={{0,96},{16,48},{32,0},{48,80},{64,32},{80,112},{96,64},{112,16},{1... | collective-permute-start | bytes 786440 | tf_op jit(solution)/shard_map/ppermute | solution.py:495
  26.0 3.8 %collective-permute-start.13 = (bf16[2,256,256]{2,1,0:T(8,128)(2,1)S(1)}, bf16[2,256,256]{2,1,0:T(8,128)(2,1)S(1)}, u32[]{:S(2)}, u32[]{:S(2)}) collective-permute-start(bf16[2,256,256]{2,1,0:T(8,128)(2,1)S(1)} %collective-permute-done.1.refs_1_), channel_id=1, source_target_pairs={{0,64},{16,80},{32,96},{48,112},{64,0},{80,16},{96,32},{112,48},{1... | collective-permute-start | bytes 786440 | tf_op jit(solution)/shard_map/ppermute | solution.py:495
  29.9 0.7 collective-permute-start.12
  30.7 1.9 %collective-permute-start.16 = (bf16[384,768]{1,0:T(8,128)(2,1)}, bf16[384,768]{1,0:T(8,128)(2,1)S(1)}, u32[]{:S(2)}, u32[]{:S(2)}) collective-permute-start(bf16[384,768]{1,0:T(8,128)(2,1)} %get-tuple-element.24), channel_id=1, source_target_pairs={{0,1},{1,2},{2,3},{3,0},{4,5},{5,6},{6,7},{7,4},{16,19},{17,16},{1... | collective-permute-start | bytes 1769480 | tf_op jit(solution)/shard_map/ppermute | solution.py:495
  32.6 1.6 %collective-permute-done.7.refs_7_ = bf16[2,256,256]{2,1,0:T(8,128)(2,1)S(1)} collective-permute-done((bf16[2,256,256]{2,1,0:T(8,128)(2,1)S(1)}, bf16[2,256,256]{2,1,0:T(8,128)(2,1)S(1)}, u32[]{:S(2)}, u32[]{:S(2)}) %collective-permute-start.7) | collective-permute-done | bytes 262176 | tf_op jit(solution)/shard_map/ppermute | solution.py:495
  34.2 2.8 %collective-permute-done.13.refs_13_ = bf16[2,256,256]{2,1,0:T(8,128)(2,1)S(1)} collective-permute-done((bf16[2,256,256]{2,1,0:T(8,128)(2,1)S(1)}, bf16[2,256,256]{2,1,0:T(8,128)(2,1)S(1)}, u32[]{:S(2)}, u32[]{:S(2)}) %collective-permute-start.13) | collective-permute-done | bytes 262176 | tf_op jit(solution)/shard_map/ppermute | solution.py:495
  37.0 8.4 %collective-permute-done.6.refs_5_ = bf16[2,256,256]{2,1,0:T(8,128)(2,1)} collective-permute-done((bf16[2,256,256]{2,1,0:T(8,128)(2,1)S(1)}, bf16[2,256,256]{2,1,0:T(8,128)(2,1)}, u32[]{:S(2)}, u32[]{:S(2)}) %collective-permute-start.6) | collective-permute-done | bytes 262176 | tf_op jit(solution)/shard_map/ppermute | solution.py:495
  45.4 0.5 collective-permute-start.11
  46.0 0.4 collective-permute-start.14
  46.5 1.9 %collective-permute-done.11.refs_11_ = bf16[2,256,256]{2,1,0:T(8,128)(2,1)S(1)} collective-permute-done((bf16[2,256,256]{2,1,0:T(8,128)(2,1)S(1)}, bf16[2,256,256]{2,1,0:T(8,128)(2,1)S(1)}, u32[]{:S(2)}, u32[]{:S(2)}) %collective-permute-start.11) | collective-permute-done | bytes 262176 | tf_op jit(solution)/shard_map/ppermute | solution.py:495
  48.4 0.7 copy-done.18
  49.1 0.1 collective-permute-start.9
  49.4 0.2 copy.13
  49.6 0.1 reshape.36
  49.8 0.6 concatenate.3.meta_ref
  50.4 0.4 collective-permute-start.22
  50.8 0.2 collective-permute-done.9.refs_9_
  51.1 7.6 %attend.1 = (bf16[512,128]{1,0:T(8,128)(2,1)}, f32[2,256,256]{2,1,0:T(8,128)}, bf16[2,272,256]{2,1,0:T(8,128)(2,1)}) custom-call(s32[76]{0:T(128)} %concatenate.3.meta_ref, bf16[2,256,256]{2,1,0:T(8,128)(2,1)} %bitcast.43, bf16[2,256,256]{2,1,0:T(8,128)(2,1)} %copy-done.14, bf16[2,256,512]{2,1,0:T(8,128)(2,1)} %bitcast.36, bf16[2,256,256]{2,1,0:T(8,128)(2,1)} %copy-done.13, ...), custom_call_target="tpu_custom_call" | custom-call | flops 8999999488 | bytes 8000000 | tf_op jit(solution)/shard_map/attend/pallas_call | solution.py:326
  58.8 1.6 %collective-permute-start.18 = (bf16[2,272,256]{2,1,0:T(8,128)(2,1)}, bf16[2,272,256]{2,1,0:T(8,128)(2,1)S(1)}, u32[]{:S(2)}, u32[]{:S(2)}) collective-permute-start(bf16[2,272,256]{2,1,0:T(8,128)(2,1)} %get-tuple-element.28), channel_id=1, source_target_pairs={{0,8},{8,0},{1,9},{9,1},{2,10},{10,2},{3,11},{11,3},{4,12},{12,4},... | collective-permute-start | bytes 835592 | tf_op jit(solution)/shard_map/ppermute | solution.py:495
  60.4 1.6 %collective-permute-start.23 = (bf16[192,768]{1,0:T(8,128)(2,1)}, bf16[192,768]{1,0:T(8,128)(2,1)S(1)}, u32[]{:S(2)}, u32[]{:S(2)}) collective-permute-start(bf16[192,768]{1,0:T(8,128)(2,1)} %copy-done.4), channel_id=1, source_target_pairs={{0,16},{16,0},{32,48},{48,32},{64,80},{80,64},{96,112},{112,96},{1... | collective-permute-start | bytes 884744 | tf_op jit(solution)/shard_map/ppermute | solution.py:495
  61.9 5.8 %collective-permute-done.18.got_ref = bf16[2,272,256]{2,1,0:T(8,128)(2,1)S(1)} collective-permute-done((bf16[2,272,256]{2,1,0:T(8,128)(2,1)}, bf16[2,272,256]{2,1,0:T(8,128)(2,1)S(1)}, u32[]{:S(2)}, u32[]{:S(2)}) %collective-permute-start.18) | collective-permute-done | bytes 278560 | tf_op jit(solution)/shard_map/ppermute | solution.py:495
  67.7 1.0 copy-done.8
  68.8 0.9 copy-done.9
  69.7 1.1 %combine.1 = (bf16[256,384]{1,0:T(8,128)(2,1)S(1)}, bf16[256,384]{1,0:T(8,128)(2,1)S(1)}) custom-call(s32[8]{0:T(128)S(1)} %copy-done.10, bf16[512,128]{1,0:T(8,128)(2,1)S(1)} %copy-done.9, f32[2,256,256]{2,1,0:T(8,128)S(1)} %copy-done.8, bf16[2,272,256]{2,1,0:T(8,128)(2,1)S(1)} %collective-permute-done.18.got_ref), custom_call_target="tpu_custom_call" | custom-call | flops 50000000 | bytes 1500000 | tf_op jit(solution)/shard_map/combine/pallas_call | solution.py:389
  70.7 2.0 %collective-permute-start.25 = (bf16[256,384]{1,0:T(8,128)(2,1)S(1)}, bf16[256,384]{1,0:T(8,128)(2,1)S(1)}, u32[]{:S(2)}, u32[]{:S(2)}) collective-permute-start(bf16[256,384]{1,0:T(8,128)(2,1)S(1)} %get-tuple-element.32.refs_0_), channel_id=1, source_target_pairs={{0,1},{1,2},{2,3},{3,0},{4,5},{5,6},{6,7},{7,4},{16,19},{17,16},{1... | collective-permute-start | bytes 589832 | tf_op jit(solution)/shard_map/ppermute | solution.py:495
  72.7 2.2 %collective-permute-start.26 = (bf16[256,384]{1,0:T(8,128)(2,1)S(1)}, bf16[256,384]{1,0:T(8,128)(2,1)S(1)}, u32[]{:S(2)}, u32[]{:S(2)}) collective-permute-start(bf16[256,384]{1,0:T(8,128)(2,1)S(1)} %get-tuple-element.32.refs_0_), channel_id=1, source_target_pairs={{0,3},{1,0},{2,1},{3,2},{4,7},{5,4},{6,5},{7,6},{16,17},{17,18},{1... | collective-permute-start | bytes 589832 | tf_op jit(solution)/shard_map/ppermute | solution.py:495
  74.9 1.8 %collective-permute-start.27 = (bf16[256,384]{1,0:T(8,128)(2,1)S(1)}, bf16[256,384]{1,0:T(8,128)(2,1)S(1)}, u32[]{:S(2)}, u32[]{:S(2)}) collective-permute-start(bf16[256,384]{1,0:T(8,128)(2,1)S(1)} %get-tuple-element.32.refs_0_), channel_id=1, source_target_pairs={{0,2},{1,3},{2,0},{3,1},{4,6},{5,7},{6,4},{7,5},{8,10},{9,11},{10,... | collective-permute-start | bytes 589832 | tf_op jit(solution)/shard_map/ppermute | solution.py:495
  76.7 1.0 collective-permute-start.19
  77.8 2.2 %collective-permute-start.20 = (bf16[256,384]{1,0:T(8,128)(2,1)S(1)}, bf16[256,384]{1,0:T(8,128)(2,1)S(1)}, u32[]{:S(2)}, u32[]{:S(2)}) collective-permute-start(bf16[256,384]{1,0:T(8,128)(2,1)S(1)} %get-tuple-element.29.refs_0_), channel_id=1, source_target_pairs={{0,3},{1,0},{2,1},{3,2},{4,7},{5,4},{6,5},{7,6},{16,17},{17,18},{1... | collective-permute-start | bytes 589832 | tf_op jit(solution)/shard_map/ppermute | solution.py:495
  80.0 6.6 %collective-permute-start.21 = (bf16[256,384]{1,0:T(8,128)(2,1)S(1)}, bf16[256,384]{1,0:T(8,128)(2,1)S(1)}, u32[]{:S(2)}, u32[]{:S(2)}) collective-permute-start(bf16[256,384]{1,0:T(8,128)(2,1)S(1)} %get-tuple-element.29.refs_0_), channel_id=1, source_target_pairs={{0,2},{1,3},{2,0},{3,1},{4,6},{5,7},{6,4},{7,5},{8,10},{9,11},{10,... | collective-permute-start | bytes 589832 | tf_op jit(solution)/shard_map/ppermute | solution.py:495
  86.6 1.1 copy-done.3
  87.7 1.0 copy-done.5
  88.7 2.2 %output.3 = (f32[256,384]{1,0:T(8,128)S(1)}, bf16[256,384]{1,0:T(8,128)(2,1)S(1)}) custom-call(s32[8]{0:T(128)S(1)} %copy-done.10, bf16[256,384]{1,0:T(8,128)(2,1)S(1)} %get-tuple-element.32.refs_0_, bf16[256,384]{1,0:T(8,128)(2,1)S(1)} %collective-permute-done.25.refs_1_, bf16[256,384]{1,0:T(8,128)(2,1)S(1)} %collective-permute-done.26.refs_2_, ...), custom_call_target="tpu_custom_call" | custom-call | flops 603979776 | bytes 4000000 | tf_op jit(solution)/shard_map/output/pallas_call | solution.py:468
  90.8 3.2 %collective-permute-start.28 = (bf16[256,384]{1,0:T(8,128)(2,1)S(1)}, bf16[256,384]{1,0:T(8,128)(2,1)S(1)}, u32[]{:S(2)}, u32[]{:S(2)}) collective-permute-start(bf16[256,384]{1,0:T(8,128)(2,1)S(1)} %get-tuple-element.34), channel_id=1, source_target_pairs={{0,4},{1,5},{2,6},{3,7},{4,0},{5,1},{6,2},{7,3},{8,12},{9,13},{10,... | collective-permute-start | bytes 589832 | tf_op jit(solution)/shard_map/ppermute | solution.py:495
  94.0 0.6 collective-permute-done.21.refs_3_
  94.6 2.2 %output.2 = (f32[256,384]{1,0:T(8,128)S(1)}, bf16[256,384]{1,0:T(8,128)(2,1)S(1)}) custom-call(s32[8]{0:T(128)S(1)} %copy-done.10, bf16[256,384]{1,0:T(8,128)(2,1)S(1)} %get-tuple-element.29.refs_0_, bf16[256,384]{1,0:T(8,128)(2,1)S(1)} %collective-permute-done.19.refs_1_, bf16[256,384]{1,0:T(8,128)(2,1)S(1)} %collective-permute-done.20.refs_2_, ...), custom_call_target="tpu_custom_call" | custom-call | flops 603979776 | bytes 4000000 | tf_op jit(solution)/shard_map/output/pallas_call | solution.py:468
  96.8 3.1 %collective-permute-start.24 = (bf16[256,384]{1,0:T(8,128)(2,1)S(1)}, bf16[256,384]{1,0:T(8,128)(2,1)S(1)}, u32[]{:S(2)}, u32[]{:S(2)}) collective-permute-start(bf16[256,384]{1,0:T(8,128)(2,1)S(1)} %get-tuple-element.31), channel_id=1, source_target_pairs={{0,4},{1,5},{2,6},{3,7},{4,0},{5,1},{6,2},{7,3},{8,12},{9,13},{10,... | collective-permute-start | bytes 589832 | tf_op jit(solution)/shard_map/ppermute | solution.py:495
  99.9 5.2 %collective-permute-done.24 = bf16[256,384]{1,0:T(8,128)(2,1)S(1)} collective-permute-done((bf16[256,384]{1,0:T(8,128)(2,1)S(1)}, bf16[256,384]{1,0:T(8,128)(2,1)S(1)}, u32[]{:S(2)}, u32[]{:S(2)}) %collective-permute-start.24) | collective-permute-done | bytes 196640 | tf_op jit(solution)/shard_map/ppermute | solution.py:495
  105.1 0.1 fusion
  105.3 0.8 pad_maximum_fusion
  (64 shorter events, 0.6 us)
Async XLA Ops:
  0.0 49.3 %copy-start = (s32[16,4,4,2]{0,3,2,1:T(2,128)S(1)}, s32[16,4,4,2]{0,3,2,1:T(2,128)}, u32[]{:S(2)}) copy-start(s32[16,4,4,2]{0,3,2,1:T(2,128)} %param.19) | copy-start | bytes 6148
  0.6 49.1 %copy-start.19 = (s32[16]{0:T(128)S(1)}, s32[16]{0:T(128)}, u32[]{:S(2)}) copy-start(s32[16]{0:T(128)} %param.18) | copy-start | bytes 196
  11.5 14.5 %collective-permute-start.4 = (bf16[2,256,512]{2,1,0:T(8,128)(2,1)}, bf16[2,256,512]{2,1,0:T(8,128)(2,1)S(1)}, u32[]{:S(2)}, u32[]{:S(2)}) collective-permute-start(bf16[2,256,512]{2,1,0:T(8,128)(2,1)} %bitcast.33), channel_id=1, source_target_pairs={{0,32},{16,112},{32,64},{48,16},{64,96},{80,48},{96,0},{112,80},{1... | collective-permute-start | bytes 1572872 | tf_op jit(solution)/shard_map/ppermute | solution.py:495
  13.2 16.6 %collective-permute-start.5 = (bf16[2,256,512]{2,1,0:T(8,128)(2,1)}, bf16[2,256,512]{2,1,0:T(8,128)(2,1)S(1)}, u32[]{:S(2)}, u32[]{:S(2)}) collective-permute-start(bf16[2,256,512]{2,1,0:T(8,128)(2,1)} %bitcast.34), channel_id=1, source_target_pairs={{0,96},{16,48},{32,0},{48,80},{64,32},{80,112},{96,64},{112,16},{1... | collective-permute-start | bytes 1572872 | tf_op jit(solution)/shard_map/ppermute | solution.py:495
  14.8 9.5 %collective-permute-start.1 = (bf16[2,256,256]{2,1,0:T(8,128)(2,1)}, bf16[2,256,256]{2,1,0:T(8,128)(2,1)S(1)}, u32[]{:S(2)}, u32[]{:S(2)}) collective-permute-start(bf16[2,256,256]{2,1,0:T(8,128)(2,1)} %bitcast.38), channel_id=1, source_target_pairs={{0,8},{8,0},{1,9},{9,1},{2,10},{10,2},{3,11},{11,3},{4,12},{12,4},... | collective-permute-start | bytes 786440 | tf_op jit(solution)/shard_map/ppermute | solution.py:495
  16.4 13.5 %collective-permute-start = (bf16[2,256,256]{2,1,0:T(8,128)(2,1)}, bf16[2,256,256]{2,1,0:T(8,128)(2,1)S(1)}, u32[]{:S(2)}, u32[]{:S(2)}) collective-permute-start(bf16[2,256,256]{2,1,0:T(8,128)(2,1)} %bitcast.37), channel_id=1, source_target_pairs={{0,8},{8,0},{1,9},{9,1},{2,10},{10,2},{3,11},{11,3},{4,12},{12,4},... | collective-permute-start | bytes 786440 | tf_op jit(solution)/shard_map/ppermute | solution.py:495
  16.8 13.8 %collective-permute-start.17 = (bf16[192,768]{1,0:T(8,128)(2,1)}, bf16[192,768]{1,0:T(8,128)(2,1)S(1)}, u32[]{:S(2)}, u32[]{:S(2)}) collective-permute-start(bf16[192,768]{1,0:T(8,128)(2,1)} %get-tuple-element.25), channel_id=1, source_target_pairs={{0,2},{1,3},{2,0},{3,1},{4,6},{5,7},{6,4},{7,5},{8,10},{9,11},{10,... | collective-permute-start | bytes 884744 | tf_op jit(solution)/shard_map/ppermute | solution.py:495
  24.3 26.8 %copy-start.13 = (bf16[2,256,256]{2,1,0:T(8,128)(2,1)}, bf16[2,256,256]{2,1,0:T(8,128)(2,1)S(1)}, u32[]{:S(2)}) copy-start(bf16[2,256,256]{2,1,0:T(8,128)(2,1)S(1)} %collective-permute-done.1.refs_1_) | copy-start | bytes 786436
  24.3 9.9 %collective-permute-start.7 = (bf16[2,256,256]{2,1,0:T(8,128)(2,1)S(1)}, bf16[2,256,256]{2,1,0:T(8,128)(2,1)S(1)}, u32[]{:S(2)}, u32[]{:S(2)}) collective-permute-start(bf16[2,256,256]{2,1,0:T(8,128)(2,1)S(1)} %collective-permute-done.1.refs_1_), channel_id=1, source_target_pairs={{0,96},{16,48},{32,0},{48,80},{64,32},{80,112},{96,64},{112,16},{1... | collective-permute-start | bytes 786440 | tf_op jit(solution)/shard_map/ppermute | solution.py:495
  26.0 10.9 %collective-permute-start.13 = (bf16[2,256,256]{2,1,0:T(8,128)(2,1)S(1)}, bf16[2,256,256]{2,1,0:T(8,128)(2,1)S(1)}, u32[]{:S(2)}, u32[]{:S(2)}) collective-permute-start(bf16[2,256,256]{2,1,0:T(8,128)(2,1)S(1)} %collective-permute-done.1.refs_1_), channel_id=1, source_target_pairs={{0,64},{16,80},{32,96},{48,112},{64,0},{80,16},{96,32},{112,48},{1... | collective-permute-start | bytes 786440 | tf_op jit(solution)/shard_map/ppermute | solution.py:495
  29.8 21.2 %copy-start.6 = (bf16[2,256,512]{2,1,0:T(8,128)(2,1)}, bf16[2,256,512]{2,1,0:T(8,128)(2,1)S(1)}, u32[]{:S(2)}) copy-start(bf16[2,256,512]{2,1,0:T(8,128)(2,1)S(1)} %collective-permute-done.5.refs_1_.refs_6_) | copy-start | bytes 1572868
  29.8 16.1 %collective-permute-start.2 = (bf16[2,256,512]{2,1,0:T(8,128)(2,1)}, bf16[2,256,512]{2,1,0:T(8,128)(2,1)S(1)}, u32[]{:S(2)}, u32[]{:S(2)}) collective-permute-start(bf16[2,256,512]{2,1,0:T(8,128)(2,1)} %bitcast.35), channel_id=1, source_target_pairs={{0,16},{16,0},{32,48},{48,32},{64,80},{80,64},{96,112},{112,96},{1... | collective-permute-start | bytes 1572872 | tf_op jit(solution)/shard_map/ppermute | solution.py:495
  29.9 21.2 %copy-start.7 = (bf16[2,256,512]{2,1,0:T(8,128)(2,1)}, bf16[2,256,512]{2,1,0:T(8,128)(2,1)S(1)}, u32[]{:S(2)}) copy-start(bf16[2,256,512]{2,1,0:T(8,128)(2,1)S(1)} %after.1.refs_4_) | copy-start | bytes 1572868
  29.9 0.8 copy-start.14
  29.9 16.1 %collective-permute-start.12 = (bf16[2,256,512]{2,1,0:T(8,128)(2,1)S(1)}, bf16[2,256,512]{2,1,0:T(8,128)(2,1)}, u32[]{:S(2)}, u32[]{:S(2)}) collective-permute-start(bf16[2,256,512]{2,1,0:T(8,128)(2,1)S(1)} %after.1.refs_4_), channel_id=1, source_target_pairs={{0,32},{16,112},{32,64},{48,16},{64,96},{80,48},{96,0},{112,80},{1... | collective-permute-start | bytes 1572872 | tf_op jit(solution)/shard_map/ppermute | solution.py:495
  30.7 20.4 %copy-start.4 = (bf16[192,768]{1,0:T(8,128)(2,1)}, bf16[192,768]{1,0:T(8,128)(2,1)S(1)}, u32[]{:S(2)}) copy-start(bf16[192,768]{1,0:T(8,128)(2,1)S(1)} %collective-permute-done.17.refs_17_.refs_7_) | copy-start | bytes 884740
  30.7 15.8 %collective-permute-start.16 = (bf16[384,768]{1,0:T(8,128)(2,1)}, bf16[384,768]{1,0:T(8,128)(2,1)S(1)}, u32[]{:S(2)}, u32[]{:S(2)}) collective-permute-start(bf16[384,768]{1,0:T(8,128)(2,1)} %get-tuple-element.24), channel_id=1, source_target_pairs={{0,1},{1,2},{2,3},{3,0},{4,5},{5,6},{6,7},{7,4},{16,19},{17,16},{1... | collective-permute-start | bytes 1769480 | tf_op jit(solution)/shard_map/ppermute | solution.py:495
  34.1 15.1 %copy-start.15 = (bf16[2,256,256]{2,1,0:T(8,128)(2,1)}, bf16[2,256,256]{2,1,0:T(8,128)(2,1)S(1)}, u32[]{:S(2)}) copy-start(bf16[2,256,256]{2,1,0:T(8,128)(2,1)S(1)} %collective-permute-done.7.refs_7_) | copy-start | bytes 786436
  34.1 11.2 %collective-permute-start.6 = (bf16[2,256,256]{2,1,0:T(8,128)(2,1)S(1)}, bf16[2,256,256]{2,1,0:T(8,128)(2,1)}, u32[]{:S(2)}, u32[]{:S(2)}) collective-permute-start(bf16[2,256,256]{2,1,0:T(8,128)(2,1)S(1)} %collective-permute-done.1.refs_1_), channel_id=1, source_target_pairs={{0,32},{16,112},{32,64},{48,16},{64,96},{80,48},{96,0},{112,80},{1... | collective-permute-start | bytes 786440 | tf_op jit(solution)/shard_map/ppermute | solution.py:495
  37.0 13.5 %copy-start.16 = (bf16[2,256,256]{2,1,0:T(8,128)(2,1)}, bf16[2,256,256]{2,1,0:T(8,128)(2,1)S(1)}, u32[]{:S(2)}) copy-start(bf16[2,256,256]{2,1,0:T(8,128)(2,1)S(1)} %collective-permute-done.13.refs_13_) | copy-start | bytes 786436
  37.0 8.4 %collective-permute-start.3 = (bf16[2,256,256]{2,1,0:T(8,128)(2,1)S(1)}, bf16[2,256,256]{2,1,0:T(8,128)(2,1)S(1)}, u32[]{:S(2)}, u32[]{:S(2)}) collective-permute-start(bf16[2,256,256]{2,1,0:T(8,128)(2,1)S(1)} %collective-permute-done.1.refs_1_), channel_id=1, source_target_pairs={{0,16},{16,0},{32,48},{48,32},{64,80},{80,64},{96,112},{112,96},{1... | collective-permute-start | bytes 786440 | tf_op jit(solution)/shard_map/ppermute | solution.py:495
  45.4 5.6 %collective-permute-start.8 = (bf16[2,256,512]{2,1,0:T(8,128)(2,1)S(1)}, bf16[2,256,512]{2,1,0:T(8,128)(2,1)}, u32[]{:S(2)}, u32[]{:S(2)}) collective-permute-start(bf16[2,256,512]{2,1,0:T(8,128)(2,1)S(1)} %after.1.refs_4_), channel_id=1, source_target_pairs={{0,16},{16,0},{32,48},{48,32},{64,80},{80,64},{96,112},{112,96},{1... | collective-permute-start | bytes 1572872 | tf_op jit(solution)/shard_map/ppermute | solution.py:495
  45.4 3.0 %copy-start.17 = (bf16[2,256,256]{2,1,0:T(8,128)(2,1)}, bf16[2,256,256]{2,1,0:T(8,128)(2,1)S(1)}, u32[]{:S(2)}) copy-start(bf16[2,256,256]{2,1,0:T(8,128)(2,1)S(1)} %collective-permute-done.3.refs_3_) | copy-start | bytes 786436
  45.4 3.0 %collective-permute-start.11 = (bf16[2,256,256]{2,1,0:T(8,128)(2,1)S(1)}, bf16[2,256,256]{2,1,0:T(8,128)(2,1)S(1)}, u32[]{:S(2)}, u32[]{:S(2)}) collective-permute-start(bf16[2,256,256]{2,1,0:T(8,128)(2,1)S(1)} %collective-permute-done.7.refs_7_), channel_id=1, source_target_pairs={{0,16},{16,0},{32,48},{48,32},{64,80},{80,64},{96,112},{112,96},{1... | collective-permute-start | bytes 786440 | tf_op jit(solution)/shard_map/ppermute | solution.py:495
  45.9 5.2 %copy-start.12 = (bf16[2,256,512]{2,1,0:T(8,128)(2,1)}, bf16[2,256,512]{2,1,0:T(8,128)(2,1)S(1)}, u32[]{:S(2)}) copy-start(bf16[2,256,512]{2,1,0:T(8,128)(2,1)S(1)} %collective-permute-done.2.refs_2_) | copy-start | bytes 1572868
  45.9 5.1 %collective-permute-start.10 = (bf16[2,256,512]{2,1,0:T(8,128)(2,1)S(1)}, bf16[2,256,512]{2,1,0:T(8,128)(2,1)}, u32[]{:S(2)}, u32[]{:S(2)}) collective-permute-start(bf16[2,256,512]{2,1,0:T(8,128)(2,1)S(1)} %collective-permute-done.5.refs_1_.refs_6_), channel_id=1, source_target_pairs={{0,16},{16,0},{32,48},{48,32},{64,80},{80,64},{96,112},{112,96},{1... | collective-permute-start | bytes 1572872 | tf_op jit(solution)/shard_map/ppermute | solution.py:495
  46.0 5.0 %collective-permute-start.14 = (bf16[2,256,512]{2,1,0:T(8,128)(2,1)}, bf16[2,256,512]{2,1,0:T(8,128)(2,1)}, u32[]{:S(2)}, u32[]{:S(2)}) collective-permute-start(bf16[2,256,512]{2,1,0:T(8,128)(2,1)} %collective-permute-done.12.refs_12_), channel_id=1, source_target_pairs={{0,16},{16,0},{32,48},{48,32},{64,80},{80,64},{96,112},{112,96},{1... | collective-permute-start | bytes 1572872 | tf_op jit(solution)/shard_map/ppermute | solution.py:495
  46.4 4.7 %copy-start.2 = (bf16[384,768]{1,0:T(8,128)(2,1)}, bf16[384,768]{1,0:T(8,128)(2,1)S(1)}, u32[]{:S(2)}) copy-start(bf16[384,768]{1,0:T(8,128)(2,1)S(1)} %collective-permute-done.16.refs_16_.refs_5_) | copy-start | bytes 1769476
  46.4 4.0 %collective-permute-start.15 = (bf16[2,256,256]{2,1,0:T(8,128)(2,1)S(1)}, bf16[2,256,256]{2,1,0:T(8,128)(2,1)}, u32[]{:S(2)}, u32[]{:S(2)}) collective-permute-start(bf16[2,256,256]{2,1,0:T(8,128)(2,1)S(1)} %collective-permute-done.13.refs_13_), channel_id=1, source_target_pairs={{0,16},{16,0},{32,48},{48,32},{64,80},{80,64},{96,112},{112,96},{1... | collective-permute-start | bytes 786440 | tf_op jit(solution)/shard_map/ppermute | solution.py:495
  49.1 1.9 %collective-permute-start.9 = (bf16[2,256,256]{2,1,0:T(8,128)(2,1)}, bf16[2,256,256]{2,1,0:T(8,128)(2,1)}, u32[]{:S(2)}, u32[]{:S(2)}) collective-permute-start(bf16[2,256,256]{2,1,0:T(8,128)(2,1)} %collective-permute-done.6.refs_5_), channel_id=1, source_target_pairs={{0,16},{16,0},{32,48},{48,32},{64,80},{80,64},{96,112},{112,96},{1... | collective-permute-start | bytes 786440 | tf_op jit(solution)/shard_map/ppermute | solution.py:495
  50.4 27.3 %collective-permute-start.22 = (bf16[384,768]{1,0:T(8,128)(2,1)S(1)}, bf16[384,768]{1,0:T(8,128)(2,1)S(1)}, u32[]{:S(2)}, u32[]{:S(2)}) collective-permute-start(bf16[384,768]{1,0:T(8,128)(2,1)S(1)} %collective-permute-done.16.refs_16_.refs_5_), channel_id=1, source_target_pairs={{0,16},{16,0},{32,48},{48,32},{64,80},{80,64},{96,112},{112,96},{1... | collective-permute-start | bytes 1769480 | tf_op jit(solution)/shard_map/ppermute | solution.py:495
  51.1 16.6 %copy-start.10 = (s32[8]{0:T(128)S(1)}, s32[8]{0:T(128)}, u32[]{:S(2)}) copy-start(s32[8]{0:T(128)} %stack.68.place_ref) | copy-start | bytes 100
  51.1 35.5 %copy-start.1 = (bf16[384,3072]{1,0:T(8,128)(2,1)S(1)}, bf16[384,3072]{1,0:T(8,128)(2,1)}, u32[]{:S(2)}) copy-start(bf16[384,3072]{1,0:T(8,128)(2,1)} %refs_4_.3) | copy-start | bytes 7077892
  58.8 8.9 %collective-permute-start.18 = (bf16[2,272,256]{2,1,0:T(8,128)(2,1)}, bf16[2,272,256]{2,1,0:T(8,128)(2,1)S(1)}, u32[]{:S(2)}, u32[]{:S(2)}) collective-permute-start(bf16[2,272,256]{2,1,0:T(8,128)(2,1)} %get-tuple-element.28), channel_id=1, source_target_pairs={{0,8},{8,0},{1,9},{9,1},{2,10},{10,2},{3,11},{11,3},{4,12},{12,4},... | collective-permute-start | bytes 835592 | tf_op jit(solution)/shard_map/ppermute | solution.py:495
  60.4 16.4 %collective-permute-start.23 = (bf16[192,768]{1,0:T(8,128)(2,1)}, bf16[192,768]{1,0:T(8,128)(2,1)S(1)}, u32[]{:S(2)}, u32[]{:S(2)}) collective-permute-start(bf16[192,768]{1,0:T(8,128)(2,1)} %copy-done.4), channel_id=1, source_target_pairs={{0,16},{16,0},{32,48},{48,32},{64,80},{80,64},{96,112},{112,96},{1... | collective-permute-start | bytes 884744 | tf_op jit(solution)/shard_map/ppermute | solution.py:495
  67.7 1.0 copy-start.8
  68.7 0.9 copy-start.9
  70.7 9.2 %collective-permute-start.25 = (bf16[256,384]{1,0:T(8,128)(2,1)S(1)}, bf16[256,384]{1,0:T(8,128)(2,1)S(1)}, u32[]{:S(2)}, u32[]{:S(2)}) collective-permute-start(bf16[256,384]{1,0:T(8,128)(2,1)S(1)} %get-tuple-element.32.refs_0_), channel_id=1, source_target_pairs={{0,1},{1,2},{2,3},{3,0},{4,5},{5,6},{6,7},{7,4},{16,19},{17,16},{1... | collective-permute-start | bytes 589832 | tf_op jit(solution)/shard_map/ppermute | solution.py:495
  72.7 13.9 %collective-permute-start.26 = (bf16[256,384]{1,0:T(8,128)(2,1)S(1)}, bf16[256,384]{1,0:T(8,128)(2,1)S(1)}, u32[]{:S(2)}, u32[]{:S(2)}) collective-permute-start(bf16[256,384]{1,0:T(8,128)(2,1)S(1)} %get-tuple-element.32.refs_0_), channel_id=1, source_target_pairs={{0,3},{1,0},{2,1},{3,2},{4,7},{5,4},{6,5},{7,6},{16,17},{17,18},{1... | collective-permute-start | bytes 589832 | tf_op jit(solution)/shard_map/ppermute | solution.py:495
  74.9 11.7 %collective-permute-start.27 = (bf16[256,384]{1,0:T(8,128)(2,1)S(1)}, bf16[256,384]{1,0:T(8,128)(2,1)S(1)}, u32[]{:S(2)}, u32[]{:S(2)}) collective-permute-start(bf16[256,384]{1,0:T(8,128)(2,1)S(1)} %get-tuple-element.32.refs_0_), channel_id=1, source_target_pairs={{0,2},{1,3},{2,0},{3,1},{4,6},{5,7},{6,4},{7,5},{8,10},{9,11},{10,... | collective-permute-start | bytes 589832 | tf_op jit(solution)/shard_map/ppermute | solution.py:495
  76.7 17.3 %collective-permute-start.19 = (bf16[256,384]{1,0:T(8,128)(2,1)S(1)}, bf16[256,384]{1,0:T(8,128)(2,1)S(1)}, u32[]{:S(2)}, u32[]{:S(2)}) collective-permute-start(bf16[256,384]{1,0:T(8,128)(2,1)S(1)} %get-tuple-element.29.refs_0_), channel_id=1, source_target_pairs={{0,1},{1,2},{2,3},{3,0},{4,5},{5,6},{6,7},{7,4},{16,19},{17,16},{1... | collective-permute-start | bytes 589832 | tf_op jit(solution)/shard_map/ppermute | solution.py:495
  77.8 16.3 %collective-permute-start.20 = (bf16[256,384]{1,0:T(8,128)(2,1)S(1)}, bf16[256,384]{1,0:T(8,128)(2,1)S(1)}, u32[]{:S(2)}, u32[]{:S(2)}) collective-permute-start(bf16[256,384]{1,0:T(8,128)(2,1)S(1)} %get-tuple-element.29.refs_0_), channel_id=1, source_target_pairs={{0,3},{1,0},{2,1},{3,2},{4,7},{5,4},{6,5},{7,6},{16,17},{17,18},{1... | collective-permute-start | bytes 589832 | tf_op jit(solution)/shard_map/ppermute | solution.py:495
  80.0 14.6 %collective-permute-start.21 = (bf16[256,384]{1,0:T(8,128)(2,1)S(1)}, bf16[256,384]{1,0:T(8,128)(2,1)S(1)}, u32[]{:S(2)}, u32[]{:S(2)}) collective-permute-start(bf16[256,384]{1,0:T(8,128)(2,1)S(1)} %get-tuple-element.29.refs_0_), channel_id=1, source_target_pairs={{0,2},{1,3},{2,0},{3,1},{4,6},{5,7},{6,4},{7,5},{8,10},{9,11},{10,... | collective-permute-start | bytes 589832 | tf_op jit(solution)/shard_map/ppermute | solution.py:495
  86.6 1.1 %copy-start.3 = (bf16[384,768]{1,0:T(8,128)(2,1)S(1)}, bf16[384,768]{1,0:T(8,128)(2,1)}, u32[]{:S(2)}) copy-start(bf16[384,768]{1,0:T(8,128)(2,1)} %copy-done.2) | copy-start | bytes 1769476
  87.7 1.0 copy-start.5
  90.8 14.3 %copy-start.11 = (f32[384]{0:T(512)S(1)}, f32[384]{0:T(512)}, u32[]{:S(2)}) copy-start(f32[384]{0:T(512)} %param.15) | copy-start | bytes 4612
  90.8 9.1 %collective-permute-start.28 = (bf16[256,384]{1,0:T(8,128)(2,1)S(1)}, bf16[256,384]{1,0:T(8,128)(2,1)S(1)}, u32[]{:S(2)}, u32[]{:S(2)}) collective-permute-start(bf16[256,384]{1,0:T(8,128)(2,1)S(1)} %get-tuple-element.34), channel_id=1, source_target_pairs={{0,4},{1,5},{2,6},{3,7},{4,0},{5,1},{6,2},{7,3},{8,12},{9,13},{10,... | collective-permute-start | bytes 589832 | tf_op jit(solution)/shard_map/ppermute | solution.py:495
  96.8 8.4 %collective-permute-start.24 = (bf16[256,384]{1,0:T(8,128)(2,1)S(1)}, bf16[256,384]{1,0:T(8,128)(2,1)S(1)}, u32[]{:S(2)}, u32[]{:S(2)}) collective-permute-start(bf16[256,384]{1,0:T(8,128)(2,1)S(1)} %get-tuple-element.31), channel_id=1, source_target_pairs={{0,4},{1,5},{2,6},{3,7},{4,0},{5,1},{6,2},{7,3},{8,12},{9,13},{10,... | collective-permute-start | bytes 589832 | tf_op jit(solution)/shard_map/ppermute | solution.py:495
  (1 other events, 0.7 us)

commit v4 on v3

--- a/solution.py
+++ b/solution.py
@@ -65,12 +65,12 @@
         for at, j in enumerate((1, 2, 0))
     ]
     o_load = pltpu.make_async_copy(w_out_ref, o_scr, o_sem.at[0])
-    for copy in x_copies + w_copies + [o_load]:
+    for copy in x_copies + w_copies[:1]:
         copy.start()
     gain = 1.0 + scale_ref[...]
     shift = shift_ref[...]
     first = place_ref[0] == 0
-    spans = [slice(i * chunk, (i + 1) * chunk) for i in range(CHUNKS)]
+    spans = [slice(i * rows // 2, (i + 1) * rows // 2) for i in range(2)]
 
     def normalise(i):
         x_copies[i].wait()
@@ -85,12 +85,14 @@
 
         lax.fori_loop(0, chunk // 16, one_block, 0, unroll=True)
 
-    normalise(0)
+    for i in range(CHUNKS):
+        if i == 1:
+            for copy in w_copies[1:] + [o_load]:
+                copy.start()
+        normalise(i)
     w_copies[0].wait()
     w_copies[1].wait()
     for i, at in enumerate(spans):
-        if i + 1 < CHUNKS:
-            normalise(i + 1)
         full = jnp.dot(n_scr[at, :], w_scr[:, :2 * wide], preferred_element_type=F32)
         for j, gain_row in ((0, kg_ref[...]), (1, None)):
             own, mid, other = split_heads(full[:, j * wide:(j + 1) * wide], gain_row, first)
@@ -350,7 +352,7 @@
     )(meta, q_home, q_away, *pieces, *waited)
 
 
-def combine_kernel(place_ref, home_ref, mid_ref, got_ref, out0_ref, out1_ref, home, mid, got, sem):
+def combine_kernel(place_ref, home_ref, mid_ref, got_ref, _, out0_ref, out1_ref, home, mid, got, sem):
     half = mid.shape[1]
     copies = [
         pltpu.make_async_copy(source, target, sem.at[k])
@@ -384,12 +386,12 @@
             out_ref[at, HEAD_DIM:2 * HEAD_DIM] = (num / (mid[fi, at, HEAD_DIM:] + den)).astype(BF16)
 
 
-def combine(place, home, mid, got):
+def combine(place, home, mid, got, later):
     frames, half, _ = mid.shape
     return pl.pallas_call(
         combine_kernel,
         out_shape=[jax.ShapeDtypeStruct((half, 3 * HEAD_DIM), BF16)] * frames,
-        in_specs=[SMEM, ANY, ANY, ANY],
+        in_specs=[SMEM, ANY, ANY, ANY, ANY],
         out_specs=[VMEM] * frames,
         scratch_shapes=[
             pltpu.VMEM(home.shape, home.dtype),
@@ -402,7 +404,7 @@
             flops=50_000_000, bytes_accessed=1_500_000, transcendentals=0
         ),
         name="combine",
-    )(place, home, mid, got)
+    )(place, home, mid, got, later)
 
 
 def after_kernel(*refs):
@@ -421,24 +423,18 @@
     )(x, *waited)
 
 
-def output_kernel(place_ref, *refs):
-    mixed, w_out_ref = refs[0:4], refs[4]
-    ahead_ref, behind_ref, apart_ref, swapped_ref = refs[5:9]
-    kept_ref, sent_ref, h_scr, w_scr, h_sem, w_sem = refs[9:15]
-    cols = kept_ref.shape[1]
+def assemble_kernel(place_ref, w_out_ref, ahead_ref, behind_ref, apart_ref, swapped_ref, *refs):
+    all_ref, w_sem = refs[-2:]
     core = place_ref[1]
-    width = mixed[0].shape[1]
-    copies = [
-        pltpu.make_async_copy(mixed[k], h_scr.at[:, pl.ds(k * width, width)], h_sem.at[k])
-        for k in range(4)
-    ]
     depth, part = ahead_ref.shape[0], apart_ref.shape[0]
+    cols = all_ref.shape[1] // 2
+    copies = []
     for j in range(2):
         block = pl.ds(pl.multiple_of(place_ref[6 + j] * cols, TILE), cols)
         copies.append(
             pltpu.make_async_copy(
                 w_out_ref.at[:, block],
-                w_scr.at[pl.ds(0, depth), pl.ds(j * cols, cols)],
+                all_ref.at[pl.ds(0, depth), pl.ds(j * cols, cols)],
                 w_sem.at[j],
             )
         )
@@ -451,40 +447,67 @@
         )
     ):
         at = pl.ds(pl.multiple_of(base, 16), source.shape[0])
-        copies.append(pltpu.make_async_copy(source, w_scr.at[at], w_sem.at[2 + k]))
+        copies.append(pltpu.make_async_copy(source, all_ref.at[at], w_sem.at[2 + k]))
+    for copy in copies:
+        copy.start()
+    for copy in copies:
+        copy.wait()
+
+
+def assemble(place, w_out, w_parts, later):
+    depth, cols = w_parts[0].shape
+    return pl.pallas_call(
+        assemble_kernel,
+        out_shape=jax.ShapeDtypeStruct((4 * depth, cols), BF16),
+        in_specs=[SMEM] + [ANY] * 6,
+        out_specs=VMEM,
+        scratch_shapes=[pltpu.SemaphoreType.DMA((6,))],
+        compiler_params=vmem(8),
+        cost_estimate=pl.CostEstimate(flops=0, bytes_accessed=4_000_000, transcendentals=0),
+        name="assemble",
+    )(place, w_out, *w_parts, later)
+
+
+def output_kernel(*refs):
+    mixed, w_ref = refs[0:4], refs[4]
+    kept_ref, sent_ref, h_scr, h_sem = refs[5:9]
+    cols = kept_ref.shape[1]
+    width = mixed[0].shape[1]
+    copies = [
+        pltpu.make_async_copy(mixed[k], h_scr.at[:, pl.ds(k * width, width)], h_sem.at[k])
+        for k in range(4)
+    ]
     for copy in copies:
         copy.start()
     for copy in copies:
         copy.wait()
     sent_ref[...] = jnp.dot(
-        h_scr[...], w_scr[:, cols:], preferred_element_type=F32
+        h_scr[...], w_ref[:, cols:], preferred_element_type=F32
     ).astype(BF16)
-    kept_ref[...] = jnp.dot(h_scr[...], w_scr[:, :cols], preferred_element_type=F32)
-
-
-def output(place, mixed, w_out, w_parts):
+    kept_ref[...] = jnp.dot(h_scr[...], w_ref[:, :cols], preferred_element_type=F32)
+
+
+def output(mixed, w_all):
     rows, width = mixed[0].shape
-    cols = w_parts[0].shape[1] // 2
+    cols = w_all.shape[1] // 2
     return pl.pallas_call(
         output_kernel,
         out_shape=[
             jax.ShapeDtypeStruct((rows, cols), F32),
             jax.ShapeDtypeStruct((rows, cols), BF16),
         ],
-        in_specs=[SMEM] + [ANY] * 9,
+        in_specs=[ANY] * 4 + [VMEM],
         out_specs=[VMEM] * 2,
         scratch_shapes=[
             pltpu.VMEM((rows, 4 * width), BF16),
-            pltpu.VMEM((4 * width, 2 * cols), BF16),
             pltpu.SemaphoreType.DMA((4,)),
-            pltpu.SemaphoreType.DMA((6,)),
         ],
         compiler_params=vmem(10),
         cost_estimate=pl.CostEstimate(
             flops=16 * rows * width * cols, bytes_accessed=4_000_000, transcendentals=0
         ),
         name="output",
-    )(place, *mixed, w_out, *w_parts)
+    )(*mixed, w_all)
 
 
 def move(axis, to, x):
@@ -516,7 +539,8 @@
 
 
 def gather_z(x):
-    return [x, out_z(x), in_z(x), cross_z(x)]
+    ahead = out_z(x)
+    return [x, ahead, in_z(x), out_z(ahead)]
 
 
 def shards(tokens, w_qkv, w_out, shift, scale, gate, q_gain, k_gain, band, far_tiles):
@@ -560,7 +584,7 @@
             lax.dynamic_slice_in_dim(far_tiles, start, frames_dev, 0).reshape(-1),
         ]
     ).astype(jnp.int32)
-    kept_first = after(kept_first, kept_second)
+    kept_first = after(kept_first, kept_second, meta)
     kept_across = out_y(kept_first)
     w_ahead, w_apart = out_z(w_ahead), cross_z(w_apart)
     pieces = [kept, away, kept_other, away_other]
@@ -580,8 +604,9 @@
     )
     w_parts = [w_ahead, swap_core(w_ahead), w_apart, swap_core(w_apart)]
     totals = []
-    for mixed in combine(place, home, mid_sums, swap_half(back)):
-        kept_part, sent_part = output(place, gather_z(mixed), w_out, w_parts)
+    w_all = assemble(place, w_out, w_parts, home)
+    for mixed in combine(place, home, mid_sums, swap_half(back), w_all):
+        kept_part, sent_part = output(gather_z(mixed), w_all)
         totals.append(kept_part + swap_x(sent_part).astype(F32))
     return jnp.stack([(total * gate).astype(BF16) for total in totals])
 

time: 106 us -> 99.1 us (0.935)
  starting transfers between devices: 44.4 us -> 35.4 us
  waiting for transfers between devices: 30.1 us -> 34.1 us
  Pallas kernels: 23.9 us -> 22.5 us
    ppermute x29, starting transfers between devices: 44.4 us -> 35.4 us  [move(): return lax.ppermute(x, axis, [(i, to(i)) for i in range(count)])]
    ppermute x29, waiting for transfers between devices: 30.1 us -> 34.1 us  [move(): return lax.ppermute(x, axis, [(i, to(i)) for i in range(count)])]
    pallas_call x2, Pallas kernels: 4.32 us -> 2.21 us  [output(): pl.pallas_call(output_kernel, out_shape=[jax.ShapeDtypeStruct((rows, cols...]
    unnamed x40 -> x54, local copies, waits for them, and re-layouts: 4.8 us -> 4.19 us
  transfers between devices with their start and end apart: 29 -> 29, of which waited for: 9 -> 13; matrix products, arithmetic and copies ran while one was open for 1% -> 1% of each run, Pallas kernels for 12% -> 12%
where the time goes in v4:
time: 99.1 us; the launch traced here: 98.6 us
  starting transfers between devices  35.4 us (36%)
  waiting for transfers between devices  34.1 us (34%)
  Pallas kernels  22.5 us (23%)
  local copies, waits for them, and re-layouts  5.44 us (5%)
    ppermute x29, starting transfers between devices, move(): return lax.ppermute(x, axis, [(i, to(i)) for i in range(count)])  35.4 us
    ppermute x29, waiting for transfers between devices, move(): return lax.ppermute(x, axis, [(i, to(i)) for i in range(count)])  34.1 us
    pallas_call x1, Pallas kernels, project(): pl.pallas_call(project_kernel, out_shape=[jax.ShapeDtypeStruct(shape, BF1...  9.91 us
    pallas_call x1, Pallas kernels, attend(): pl.pallas_call(attend_kernel, out_shape=[jax.ShapeDtypeStruct((frames * h...  8.23 us
    unnamed x54, local copies, waits for them, and re-layouts  4.19 us
    pallas_call x2, Pallas kernels, output(): pl.pallas_call(output_kernel, out_shape=[jax.ShapeDtypeStruct((rows, cols...  2.21 us
  transfers between devices with their start and end apart: 29, of which 13 were waited for; matrix products, arithmetic and copies ran while one was open for 1% of the time, Pallas kernels for 12%

profile of v4, /device:TPU:0, one launch (start us, length us, event | category | flops | bytes accessed | tf_op | source)
XLA Modules:
  0.0 98.6 jit_solution(13076627301484943260)
XLA Ops:
  0.0 0.7 stack.68.place_ref
  0.7 9.9 %project.1 = (bf16[512,512]{1,0:T(8,128)(2,1)}, bf16[512,256]{1,0:T(8,128)(2,1)}, bf16[512,256]{1,0:T(8,128)(2,1)}, bf16[512,256]{1,0:T(8,128)(2,1)}, bf16[384,7...) custom-call(s32[8]{0:T(128)} %stack.68.place_ref, bf16[512,3072]{1,0:T(8,128)(2,1)} %bitcast.32, bf16[3,3072,384]{2,1,0:T(8,128)(2,1)} %bitcast.31, ...), custom_call_target="tpu_custom_call" | custom-call | flops 3623878656 | bytes 12000000 | tf_op jit(solution)/shard_map/project/pallas_call | solution.py:144
  10.6 1.7 %collective-permute-start.4 = (bf16[2,256,512]{2,1,0:T(8,128)(2,1)}, bf16[2,256,512]{2,1,0:T(8,128)(2,1)S(1)}, u32[]{:S(2)}, u32[]{:S(2)}) collective-permute-start(bf16[2,256,512]{2,1,0:T(8,128)(2,1)} %bitcast.33), channel_id=1, source_target_pairs={{0,32},{16,112},{32,64},{48,16},{64,96},{80,48},{96,0},{112,80},{1... | collective-permute-start | bytes 1572872 | tf_op jit(solution)/shard_map/ppermute | solution.py:518
  12.3 1.6 %collective-permute-start.5 = (bf16[2,256,512]{2,1,0:T(8,128)(2,1)}, bf16[2,256,512]{2,1,0:T(8,128)(2,1)S(1)}, u32[]{:S(2)}, u32[]{:S(2)}) collective-permute-start(bf16[2,256,512]{2,1,0:T(8,128)(2,1)} %bitcast.34), channel_id=1, source_target_pairs={{0,96},{16,48},{32,0},{48,80},{64,32},{80,112},{96,64},{112,16},{1... | collective-permute-start | bytes 1572872 | tf_op jit(solution)/shard_map/ppermute | solution.py:518
  13.9 1.6 %collective-permute-start.1 = (bf16[2,256,256]{2,1,0:T(8,128)(2,1)}, bf16[2,256,256]{2,1,0:T(8,128)(2,1)S(1)}, u32[]{:S(2)}, u32[]{:S(2)}) collective-permute-start(bf16[2,256,256]{2,1,0:T(8,128)(2,1)} %bitcast.38), channel_id=1, source_target_pairs={{0,8},{8,0},{1,9},{9,1},{2,10},{10,2},{3,11},{11,3},{4,12},{12,4},... | collective-permute-start | bytes 786440 | tf_op jit(solution)/shard_map/ppermute | solution.py:518
  15.5 0.5 collective-permute-start
  15.9 4.0 %collective-permute-start.17 = (bf16[192,768]{1,0:T(8,128)(2,1)}, bf16[192,768]{1,0:T(8,128)(2,1)S(1)}, u32[]{:S(2)}, u32[]{:S(2)}) collective-permute-start(bf16[192,768]{1,0:T(8,128)(2,1)} %get-tuple-element.25), channel_id=1, source_target_pairs={{0,2},{1,3},{2,0},{3,1},{4,6},{5,7},{6,4},{7,5},{8,10},{9,11},{10,... | collective-permute-start | bytes 884744 | tf_op jit(solution)/shard_map/ppermute | solution.py:518
  20.5 2.9 %collective-permute-done.1.refs_1_ = bf16[2,256,256]{2,1,0:T(8,128)(2,1)S(1)} collective-permute-done((bf16[2,256,256]{2,1,0:T(8,128)(2,1)}, bf16[2,256,256]{2,1,0:T(8,128)(2,1)S(1)}, u32[]{:S(2)}, u32[]{:S(2)}) %collective-permute-start.1) | collective-permute-done | bytes 262176 | tf_op jit(solution)/shard_map/ppermute | solution.py:518
  23.4 1.7 %collective-permute-start.7 = (bf16[2,256,256]{2,1,0:T(8,128)(2,1)S(1)}, bf16[2,256,256]{2,1,0:T(8,128)(2,1)S(1)}, u32[]{:S(2)}, u32[]{:S(2)}) collective-permute-start(bf16[2,256,256]{2,1,0:T(8,128)(2,1)S(1)} %collective-permute-done.1.refs_1_), channel_id=1, source_target_pairs={{0,96},{16,48},{32,0},{48,80},{64,32},{80,112},{96,64},{112,16},{1... | collective-permute-start | bytes 786440 | tf_op jit(solution)/shard_map/ppermute | solution.py:518
  25.1 3.8 %collective-permute-start.13 = (bf16[2,256,256]{2,1,0:T(8,128)(2,1)S(1)}, bf16[2,256,256]{2,1,0:T(8,128)(2,1)S(1)}, u32[]{:S(2)}, u32[]{:S(2)}) collective-permute-start(bf16[2,256,256]{2,1,0:T(8,128)(2,1)S(1)} %collective-permute-done.1.refs_1_), channel_id=1, source_target_pairs={{0,64},{16,80},{32,96},{48,112},{64,0},{80,16},{96,32},{112,48},{1... | collective-permute-start | bytes 786440 | tf_op jit(solution)/shard_map/ppermute | solution.py:518
  29.0 0.7 collective-permute-start.12
  29.8 1.9 %collective-permute-start.16 = (bf16[384,768]{1,0:T(8,128)(2,1)}, bf16[384,768]{1,0:T(8,128)(2,1)S(1)}, u32[]{:S(2)}, u32[]{:S(2)}) collective-permute-start(bf16[384,768]{1,0:T(8,128)(2,1)} %get-tuple-element.24), channel_id=1, source_target_pairs={{0,1},{1,2},{2,3},{3,0},{4,5},{5,6},{6,7},{7,4},{16,19},{17,16},{1... | collective-permute-start | bytes 1769480 | tf_op jit(solution)/shard_map/ppermute | solution.py:518
  31.7 1.5 %collective-permute-done.7.refs_7_ = bf16[2,256,256]{2,1,0:T(8,128)(2,1)S(1)} collective-permute-done((bf16[2,256,256]{2,1,0:T(8,128)(2,1)S(1)}, bf16[2,256,256]{2,1,0:T(8,128)(2,1)S(1)}, u32[]{:S(2)}, u32[]{:S(2)}) %collective-permute-start.7) | collective-permute-done | bytes 262176 | tf_op jit(solution)/shard_map/ppermute | solution.py:518
  33.2 2.9 %collective-permute-done.13.refs_13_ = bf16[2,256,256]{2,1,0:T(8,128)(2,1)S(1)} collective-permute-done((bf16[2,256,256]{2,1,0:T(8,128)(2,1)S(1)}, bf16[2,256,256]{2,1,0:T(8,128)(2,1)S(1)}, u32[]{:S(2)}, u32[]{:S(2)}) %collective-permute-start.13) | collective-permute-done | bytes 262176 | tf_op jit(solution)/shard_map/ppermute | solution.py:518
  36.1 8.3 %collective-permute-done.6.refs_5_ = bf16[2,256,256]{2,1,0:T(8,128)(2,1)S(1)} collective-permute-done((bf16[2,256,256]{2,1,0:T(8,128)(2,1)S(1)}, bf16[2,256,256]{2,1,0:T(8,128)(2,1)S(1)}, u32[]{:S(2)}, u32[]{:S(2)}) %collective-permute-start.6) | collective-permute-done | bytes 262176 | tf_op jit(solution)/shard_map/ppermute | solution.py:518
  44.4 0.5 collective-permute-start.8
  45.0 0.4 collective-permute-start.14
  45.4 0.3 collective-permute-start.15
  46.1 2.5 %collective-permute-done.15.refs_15_ = bf16[2,256,256]{2,1,0:T(8,128)(2,1)S(1)} collective-permute-done((bf16[2,256,256]{2,1,0:T(8,128)(2,1)S(1)}, bf16[2,256,256]{2,1,0:T(8,128)(2,1)S(1)}, u32[]{:S(2)}, u32[]{:S(2)}) %collective-permute-start.15) | collective-permute-done | bytes 262176 | tf_op jit(solution)/shard_map/ppermute | solution.py:518
  48.7 0.2 collective-permute-done.9.refs_9_
  48.9 0.2 collective-permute-start.19
  49.3 0.4 copy-done.25
  49.7 0.3 copy-done.15
  50.0 0.2 copy-done.16
  50.4 8.2 %attend.1 = (bf16[512,128]{1,0:T(8,128)(2,1)}, f32[2,256,256]{2,1,0:T(8,128)}, bf16[2,272,256]{2,1,0:T(8,128)(2,1)}) custom-call(s32[76]{0:T(128)} %copy-done.11, bf16[2,256,256]{2,1,0:T(8,128)(2,1)} %bitcast.43, bf16[2,256,256]{2,1,0:T(8,128)(2,1)} %copy-done.19, bf16[2,256,512]{2,1,0:T(8,128)(2,1)} %bitcast.36, bf16[2,256,256]{2,1,0:T(8,128)(2,1)} %copy-done.18, ...), custom_call_target="tpu_custom_call" | custom-call | flops 8999999488 | bytes 8000000 | tf_op jit(solution)/shard_map/attend/pallas_call | solution.py:328
  58.6 1.6 %collective-permute-start.18 = (bf16[2,272,256]{2,1,0:T(8,128)(2,1)}, bf16[2,272,256]{2,1,0:T(8,128)(2,1)S(1)}, u32[]{:S(2)}, u32[]{:S(2)}) collective-permute-start(bf16[2,272,256]{2,1,0:T(8,128)(2,1)} %get-tuple-element.28), channel_id=1, source_target_pairs={{0,8},{8,0},{1,9},{9,1},{2,10},{10,2},{3,11},{11,3},{4,12},{12,4},... | collective-permute-start | bytes 835592 | tf_op jit(solution)/shard_map/ppermute | solution.py:518
  60.2 1.1 %copy-done.3 = bf16[384,768]{1,0:T(8,128)(2,1)S(1)} copy-done((bf16[384,768]{1,0:T(8,128)(2,1)S(1)}, bf16[384,768]{1,0:T(8,128)(2,1)}, u32[]{:S(2)}) %copy-start.3) | copy-done | bytes 589848
  61.3 0.9 copy-done.7
  62.2 1.0 copy-done.9
  63.2 1.1 %assemble.1._.refs_4_ = bf16[1536,768]{1,0:T(8,128)(2,1)S(1)} custom-call(s32[8]{0:T(128)S(1)} %copy-done.10, bf16[384,3072]{1,0:T(8,128)(2,1)S(1)} %copy-done.1, bf16[384,768]{1,0:T(8,128)(2,1)S(1)} %copy-done.3, bf16[384,768]{1,0:T(8,128)(2,1)S(1)} %collective-permute-done.19.behind_ref, bf16[192,768]{1,0:T(8,128)(2,1)S(1)} %copy-done.9, ...), custom_call_target="tpu_custom_call" | custom-call | bytes 4000000 | tf_op jit(solution)/shard_map/assemble/pallas_call | solution.py:459
  64.2 3.9 %collective-permute-done.18.got_ref = bf16[2,272,256]{2,1,0:T(8,128)(2,1)S(1)} collective-permute-done((bf16[2,272,256]{2,1,0:T(8,128)(2,1)}, bf16[2,272,256]{2,1,0:T(8,128)(2,1)S(1)}, u32[]{:S(2)}, u32[]{:S(2)}) %collective-permute-start.18) | collective-permute-done | bytes 278560 | tf_op jit(solution)/shard_map/ppermute | solution.py:518
  68.1 1.1 %combine.1 = (bf16[256,384]{1,0:T(8,128)(2,1)S(1)}, bf16[256,384]{1,0:T(8,128)(2,1)S(1)}) custom-call(s32[8]{0:T(128)S(1)} %copy-done.10, bf16[512,128]{1,0:T(8,128)(2,1)S(1)} %copy-done.7, f32[2,256,256]{2,1,0:T(8,128)S(1)} %copy-done.6, bf16[2,272,256]{2,1,0:T(8,128)(2,1)S(1)} %collective-permute-done.18.got_ref, bf16[1536,768]{1,0:T(8,128)(2,1)S(1)} %assemble.1._.refs_4_), custom_call_target="tpu_custom_call" | custom-call | flops 50000000 | bytes 1500000 | tf_op jit(solution)/shard_map/combine/pallas_call | solution.py:391
  69.2 2.0 %collective-permute-start.25 = (bf16[256,384]{1,0:T(8,128)(2,1)S(1)}, bf16[256,384]{1,0:T(8,128)(2,1)S(1)}, u32[]{:S(2)}, u32[]{:S(2)}) collective-permute-start(bf16[256,384]{1,0:T(8,128)(2,1)S(1)} %get-tuple-element.32.refs_0_), channel_id=1, source_target_pairs={{0,1},{1,2},{2,3},{3,0},{4,5},{5,6},{6,7},{7,4},{16,19},{17,16},{1... | collective-permute-start | bytes 589832 | tf_op jit(solution)/shard_map/ppermute | solution.py:518
  71.2 1.9 %collective-permute-start.21 = (bf16[256,384]{1,0:T(8,128)(2,1)S(1)}, bf16[256,384]{1,0:T(8,128)(2,1)S(1)}, u32[]{:S(2)}, u32[]{:S(2)}) collective-permute-start(bf16[256,384]{1,0:T(8,128)(2,1)S(1)} %get-tuple-element.29.refs_0_), channel_id=1, source_target_pairs={{0,1},{1,2},{2,3},{3,0},{4,5},{5,6},{6,7},{7,4},{16,19},{17,16},{1... | collective-permute-start | bytes 589832 | tf_op jit(solution)/shard_map/ppermute | solution.py:518
  73.1 1.3 %collective-permute-start.26 = (bf16[256,384]{1,0:T(8,128)(2,1)S(1)}, bf16[256,384]{1,0:T(8,128)(2,1)S(1)}, u32[]{:S(2)}, u32[]{:S(2)}) collective-permute-start(bf16[256,384]{1,0:T(8,128)(2,1)S(1)} %get-tuple-element.32.refs_0_), channel_id=1, source_target_pairs={{0,3},{1,0},{2,1},{3,2},{4,7},{5,4},{6,5},{7,6},{16,17},{17,18},{1... | collective-permute-start | bytes 589832 | tf_op jit(solution)/shard_map/ppermute | solution.py:518
  74.4 2.5 %collective-permute-done.25.refs_1_ = bf16[256,384]{1,0:T(8,128)(2,1)S(1)} collective-permute-done((bf16[256,384]{1,0:T(8,128)(2,1)S(1)}, bf16[256,384]{1,0:T(8,128)(2,1)S(1)}, u32[]{:S(2)}, u32[]{:S(2)}) %collective-permute-start.25) | collective-permute-done | bytes 196640 | tf_op jit(solution)/shard_map/ppermute | solution.py:518
  76.9 0.3 collective-permute-start.27
  77.2 3.3 %collective-permute-start.22 = (bf16[256,384]{1,0:T(8,128)(2,1)S(1)}, bf16[256,384]{1,0:T(8,128)(2,1)S(1)}, u32[]{:S(2)}, u32[]{:S(2)}) collective-permute-start(bf16[256,384]{1,0:T(8,128)(2,1)S(1)} %get-tuple-element.29.refs_0_), channel_id=1, source_target_pairs={{0,3},{1,0},{2,1},{3,2},{4,7},{5,4},{6,5},{7,6},{16,17},{17,18},{1... | collective-permute-start | bytes 589832 | tf_op jit(solution)/shard_map/ppermute | solution.py:518
  80.5 0.3 collective-permute-done.21.refs_1_
  80.9 0.5 collective-permute-start.23
  81.4 3.7 %collective-permute-done.27.refs_3_ = bf16[256,384]{1,0:T(8,128)(2,1)S(1)} collective-permute-done((bf16[256,384]{1,0:T(8,128)(2,1)S(1)}, bf16[256,384]{1,0:T(8,128)(2,1)S(1)}, u32[]{:S(2)}, u32[]{:S(2)}) %collective-permute-start.27) | collective-permute-done | bytes 196640 | tf_op jit(solution)/shard_map/ppermute | solution.py:518
  85.1 1.1 %output.3 = (f32[256,384]{1,0:T(8,128)S(1)}, bf16[256,384]{1,0:T(8,128)(2,1)S(1)}) custom-call(bf16[256,384]{1,0:T(8,128)(2,1)S(1)} %get-tuple-element.32.refs_0_, bf16[256,384]{1,0:T(8,128)(2,1)S(1)} %collective-permute-done.25.refs_1_, bf16[256,384]{1,0:T(8,128)(2,1)S(1)} %collective-permute-done.26.refs_2_, ...), custom_call_target="tpu_custom_call" | custom-call | flops 603979776 | bytes 4000000 | tf_op jit(solution)/shard_map/output/pallas_call | solution.py:493
  86.3 3.1 %collective-permute-start.28 = (bf16[256,384]{1,0:T(8,128)(2,1)S(1)}, bf16[256,384]{1,0:T(8,128)(2,1)S(1)}, u32[]{:S(2)}, u32[]{:S(2)}) collective-permute-start(bf16[256,384]{1,0:T(8,128)(2,1)S(1)} %get-tuple-element.34), channel_id=1, source_target_pairs={{0,4},{1,5},{2,6},{3,7},{4,0},{5,1},{6,2},{7,3},{8,12},{9,13},{10,... | collective-permute-start | bytes 589832 | tf_op jit(solution)/shard_map/ppermute | solution.py:518
  89.4 1.1 %output.2 = (f32[256,384]{1,0:T(8,128)S(1)}, bf16[256,384]{1,0:T(8,128)(2,1)S(1)}) custom-call(bf16[256,384]{1,0:T(8,128)(2,1)S(1)} %get-tuple-element.29.refs_0_, bf16[256,384]{1,0:T(8,128)(2,1)S(1)} %collective-permute-done.21.refs_1_, bf16[256,384]{1,0:T(8,128)(2,1)S(1)} %collective-permute-done.22.refs_2_, ...), custom_call_target="tpu_custom_call" | custom-call | flops 603979776 | bytes 4000000 | tf_op jit(solution)/shard_map/output/pallas_call | solution.py:493
  90.5 2.1 %collective-permute-start.24 = (bf16[256,384]{1,0:T(8,128)(2,1)S(1)}, bf16[256,384]{1,0:T(8,128)(2,1)S(1)}, u32[]{:S(2)}, u32[]{:S(2)}) collective-permute-start(bf16[256,384]{1,0:T(8,128)(2,1)S(1)} %get-tuple-element.31), channel_id=1, source_target_pairs={{0,4},{1,5},{2,6},{3,7},{4,0},{5,1},{6,2},{7,3},{8,12},{9,13},{10,... | collective-permute-start | bytes 589832 | tf_op jit(solution)/shard_map/ppermute | solution.py:518
  92.6 1.9 %collective-permute-done.28 = bf16[256,384]{1,0:T(8,128)(2,1)S(1)} collective-permute-done((bf16[256,384]{1,0:T(8,128)(2,1)S(1)}, bf16[256,384]{1,0:T(8,128)(2,1)S(1)}, u32[]{:S(2)}, u32[]{:S(2)}) %collective-permute-start.28) | collective-permute-done | bytes 196640 | tf_op jit(solution)/shard_map/ppermute | solution.py:518
  94.5 3.3 %collective-permute-done.24 = bf16[256,384]{1,0:T(8,128)(2,1)S(1)} collective-permute-done((bf16[256,384]{1,0:T(8,128)(2,1)S(1)}, bf16[256,384]{1,0:T(8,128)(2,1)S(1)}, u32[]{:S(2)}, u32[]{:S(2)}) %collective-permute-start.24) | collective-permute-done | bytes 196640 | tf_op jit(solution)/shard_map/ppermute | solution.py:518
  97.9 0.8 pad_maximum_fusion
  (79 shorter events, 1.7 us)
Async XLA Ops:
  0.0 19.9 %copy-start = (s32[16,4,4,2]{0,3,2,1:T(2,128)S(1)}, s32[16,4,4,2]{0,3,2,1:T(2,128)}, u32[]{:S(2)}) copy-start(s32[16,4,4,2]{0,3,2,1:T(2,128)} %param.19) | copy-start | bytes 6148
  0.7 19.6 %copy-start.26 = (s32[16]{0:T(128)S(1)}, s32[16]{0:T(128)}, u32[]{:S(2)}) copy-start(s32[16]{0:T(128)} %param.18) | copy-start | bytes 196
  10.6 14.5 %collective-permute-start.4 = (bf16[2,256,512]{2,1,0:T(8,128)(2,1)}, bf16[2,256,512]{2,1,0:T(8,128)(2,1)S(1)}, u32[]{:S(2)}, u32[]{:S(2)}) collective-permute-start(bf16[2,256,512]{2,1,0:T(8,128)(2,1)} %bitcast.33), channel_id=1, source_target_pairs={{0,32},{16,112},{32,64},{48,16},{64,96},{80,48},{96,0},{112,80},{1... | collective-permute-start | bytes 1572872 | tf_op jit(solution)/shard_map/ppermute | solution.py:518
  12.3 16.6 %collective-permute-start.5 = (bf16[2,256,512]{2,1,0:T(8,128)(2,1)}, bf16[2,256,512]{2,1,0:T(8,128)(2,1)S(1)}, u32[]{:S(2)}, u32[]{:S(2)}) collective-permute-start(bf16[2,256,512]{2,1,0:T(8,128)(2,1)} %bitcast.34), channel_id=1, source_target_pairs={{0,96},{16,48},{32,0},{48,80},{64,32},{80,112},{96,64},{112,16},{1... | collective-permute-start | bytes 1572872 | tf_op jit(solution)/shard_map/ppermute | solution.py:518
  13.9 9.5 %collective-permute-start.1 = (bf16[2,256,256]{2,1,0:T(8,128)(2,1)}, bf16[2,256,256]{2,1,0:T(8,128)(2,1)S(1)}, u32[]{:S(2)}, u32[]{:S(2)}) collective-permute-start(bf16[2,256,256]{2,1,0:T(8,128)(2,1)} %bitcast.38), channel_id=1, source_target_pairs={{0,8},{8,0},{1,9},{9,1},{2,10},{10,2},{3,11},{11,3},{4,12},{12,4},... | collective-permute-start | bytes 786440 | tf_op jit(solution)/shard_map/ppermute | solution.py:518
  15.5 13.5 %collective-permute-start = (bf16[2,256,256]{2,1,0:T(8,128)(2,1)}, bf16[2,256,256]{2,1,0:T(8,128)(2,1)S(1)}, u32[]{:S(2)}, u32[]{:S(2)}) collective-permute-start(bf16[2,256,256]{2,1,0:T(8,128)(2,1)} %bitcast.37), channel_id=1, source_target_pairs={{0,8},{8,0},{1,9},{9,1},{2,10},{10,2},{3,11},{11,3},{4,12},{12,4},... | collective-permute-start | bytes 786440 | tf_op jit(solution)/shard_map/ppermute | solution.py:518
  15.9 13.8 %collective-permute-start.17 = (bf16[192,768]{1,0:T(8,128)(2,1)}, bf16[192,768]{1,0:T(8,128)(2,1)S(1)}, u32[]{:S(2)}, u32[]{:S(2)}) collective-permute-start(bf16[192,768]{1,0:T(8,128)(2,1)} %get-tuple-element.25), channel_id=1, source_target_pairs={{0,2},{1,3},{2,0},{3,1},{4,6},{5,7},{6,4},{7,5},{8,10},{9,11},{10,... | collective-permute-start | bytes 884744 | tf_op jit(solution)/shard_map/ppermute | solution.py:518
  20.5 29.9 %copy-start.11 = (s32[76]{0:T(128)}, s32[76]{0:T(128)S(1)}, u32[]{:S(2)}) copy-start(s32[76]{0:T(128)S(1)} %concatenate.3.refs_2_.meta_ref) | copy-start | bytes 916
  23.4 22.7 %copy-start.18 = (bf16[2,256,256]{2,1,0:T(8,128)(2,1)}, bf16[2,256,256]{2,1,0:T(8,128)(2,1)S(1)}, u32[]{:S(2)}) copy-start(bf16[2,256,256]{2,1,0:T(8,128)(2,1)S(1)} %collective-permute-done.1.refs_1_) | copy-start | bytes 786436
  23.4 9.8 %collective-permute-start.7 = (bf16[2,256,256]{2,1,0:T(8,128)(2,1)S(1)}, bf16[2,256,256]{2,1,0:T(8,128)(2,1)S(1)}, u32[]{:S(2)}, u32[]{:S(2)}) collective-permute-start(bf16[2,256,256]{2,1,0:T(8,128)(2,1)S(1)} %collective-permute-done.1.refs_1_), channel_id=1, source_target_pairs={{0,96},{16,48},{32,0},{48,80},{64,32},{80,112},{96,64},{112,16},{1... | collective-permute-start | bytes 786440 | tf_op jit(solution)/shard_map/ppermute | solution.py:518
  25.1 10.9 %collective-permute-start.13 = (bf16[2,256,256]{2,1,0:T(8,128)(2,1)S(1)}, bf16[2,256,256]{2,1,0:T(8,128)(2,1)S(1)}, u32[]{:S(2)}, u32[]{:S(2)}) collective-permute-start(bf16[2,256,256]{2,1,0:T(8,128)(2,1)S(1)} %collective-permute-done.1.refs_1_), channel_id=1, source_target_pairs={{0,64},{16,80},{32,96},{48,112},{64,0},{80,16},{96,32},{112,48},{1... | collective-permute-start | bytes 786440 | tf_op jit(solution)/shard_map/ppermute | solution.py:518
  29.0 21.4 %copy-start.4 = (bf16[2,256,512]{2,1,0:T(8,128)(2,1)}, bf16[2,256,512]{2,1,0:T(8,128)(2,1)S(1)}, u32[]{:S(2)}) copy-start(bf16[2,256,512]{2,1,0:T(8,128)(2,1)S(1)} %collective-permute-done.5.refs_1_.refs_6_) | copy-start | bytes 1572868
  29.0 16.0 %collective-permute-start.2 = (bf16[2,256,512]{2,1,0:T(8,128)(2,1)}, bf16[2,256,512]{2,1,0:T(8,128)(2,1)S(1)}, u32[]{:S(2)}, u32[]{:S(2)}) collective-permute-start(bf16[2,256,512]{2,1,0:T(8,128)(2,1)} %bitcast.35), channel_id=1, source_target_pairs={{0,16},{16,0},{32,48},{48,32},{64,80},{80,64},{96,112},{112,96},{1... | collective-permute-start | bytes 1572872 | tf_op jit(solution)/shard_map/ppermute | solution.py:518
  29.0 21.4 %copy-start.5 = (bf16[2,256,512]{2,1,0:T(8,128)(2,1)}, bf16[2,256,512]{2,1,0:T(8,128)(2,1)S(1)}, u32[]{:S(2)}) copy-start(bf16[2,256,512]{2,1,0:T(8,128)(2,1)S(1)} %after.1.refs_4_) | copy-start | bytes 1572868
  29.0 16.0 %collective-permute-start.12 = (bf16[2,256,512]{2,1,0:T(8,128)(2,1)S(1)}, bf16[2,256,512]{2,1,0:T(8,128)(2,1)S(1)}, u32[]{:S(2)}, u32[]{:S(2)}) collective-permute-start(bf16[2,256,512]{2,1,0:T(8,128)(2,1)S(1)} %after.1.refs_4_), channel_id=1, source_target_pairs={{0,32},{16,112},{32,64},{48,16},{64,96},{80,48},{96,0},{112,80},{1... | collective-permute-start | bytes 1572872 | tf_op jit(solution)/shard_map/ppermute | solution.py:518
  29.8 20.6 %copy-start.8 = (bf16[192,768]{1,0:T(8,128)(2,1)}, bf16[192,768]{1,0:T(8,128)(2,1)S(1)}, u32[]{:S(2)}) copy-start(bf16[192,768]{1,0:T(8,128)(2,1)S(1)} %collective-permute-done.17.refs_17_.apart_ref) | copy-start | bytes 884740
  29.8 15.6 %collective-permute-start.16 = (bf16[384,768]{1,0:T(8,128)(2,1)}, bf16[384,768]{1,0:T(8,128)(2,1)S(1)}, u32[]{:S(2)}, u32[]{:S(2)}) collective-permute-start(bf16[384,768]{1,0:T(8,128)(2,1)} %get-tuple-element.24), channel_id=1, source_target_pairs={{0,1},{1,2},{2,3},{3,0},{4,5},{5,6},{6,7},{7,4},{16,19},{17,16},{1... | collective-permute-start | bytes 1769480 | tf_op jit(solution)/shard_map/ppermute | solution.py:518
  33.2 17.2 %copy-start.20 = (bf16[2,256,256]{2,1,0:T(8,128)(2,1)}, bf16[2,256,256]{2,1,0:T(8,128)(2,1)S(1)}, u32[]{:S(2)}) copy-start(bf16[2,256,256]{2,1,0:T(8,128)(2,1)S(1)} %collective-permute-done.7.refs_7_) | copy-start | bytes 786436
  33.2 11.2 %collective-permute-start.6 = (bf16[2,256,256]{2,1,0:T(8,128)(2,1)S(1)}, bf16[2,256,256]{2,1,0:T(8,128)(2,1)S(1)}, u32[]{:S(2)}, u32[]{:S(2)}) collective-permute-start(bf16[2,256,256]{2,1,0:T(8,128)(2,1)S(1)} %collective-permute-done.1.refs_1_), channel_id=1, source_target_pairs={{0,32},{16,112},{32,64},{48,16},{64,96},{80,48},{96,0},{112,80},{1... | collective-permute-start | bytes 786440 | tf_op jit(solution)/shard_map/ppermute | solution.py:518
  36.1 12.6 %copy-start.21 = (bf16[2,256,256]{2,1,0:T(8,128)(2,1)}, bf16[2,256,256]{2,1,0:T(8,128)(2,1)S(1)}, u32[]{:S(2)}) copy-start(bf16[2,256,256]{2,1,0:T(8,128)(2,1)S(1)} %collective-permute-done.13.refs_13_) | copy-start | bytes 786436
  36.1 8.3 %collective-permute-start.3 = (bf16[2,256,256]{2,1,0:T(8,128)(2,1)S(1)}, bf16[2,256,256]{2,1,0:T(8,128)(2,1)}, u32[]{:S(2)}, u32[]{:S(2)}) collective-permute-start(bf16[2,256,256]{2,1,0:T(8,128)(2,1)S(1)} %collective-permute-done.1.refs_1_), channel_id=1, source_target_pairs={{0,16},{16,0},{32,48},{48,32},{64,80},{80,64},{96,112},{112,96},{1... | collective-permute-start | bytes 786440 | tf_op jit(solution)/shard_map/ppermute | solution.py:518
  44.4 4.3 %copy-start.22 = (bf16[2,256,256]{2,1,0:T(8,128)(2,1)}, bf16[2,256,256]{2,1,0:T(8,128)(2,1)S(1)}, u32[]{:S(2)}) copy-start(bf16[2,256,256]{2,1,0:T(8,128)(2,1)S(1)} %collective-permute-done.6.refs_5_) | copy-start | bytes 786436
  44.4 1.5 %collective-permute-start.11 = (bf16[2,256,256]{2,1,0:T(8,128)(2,1)S(1)}, bf16[2,256,256]{2,1,0:T(8,128)(2,1)S(1)}, u32[]{:S(2)}, u32[]{:S(2)}) collective-permute-start(bf16[2,256,256]{2,1,0:T(8,128)(2,1)S(1)} %collective-permute-done.7.refs_7_), channel_id=1, source_target_pairs={{0,16},{16,0},{32,48},{48,32},{64,80},{80,64},{96,112},{112,96},{1... | collective-permute-start | bytes 786440 | tf_op jit(solution)/shard_map/ppermute | solution.py:518
  44.4 4.8 %collective-permute-start.8 = (bf16[2,256,512]{2,1,0:T(8,128)(2,1)S(1)}, bf16[2,256,512]{2,1,0:T(8,128)(2,1)S(1)}, u32[]{:S(2)}, u32[]{:S(2)}) collective-permute-start(bf16[2,256,512]{2,1,0:T(8,128)(2,1)S(1)} %after.1.refs_4_), channel_id=1, source_target_pairs={{0,16},{16,0},{32,48},{48,32},{64,80},{80,64},{96,112},{112,96},{1... | collective-permute-start | bytes 1572872 | tf_op jit(solution)/shard_map/ppermute | solution.py:518
  44.9 5.5 %copy-start.13 = (bf16[2,256,512]{2,1,0:T(8,128)(2,1)}, bf16[2,256,512]{2,1,0:T(8,128)(2,1)S(1)}, u32[]{:S(2)}) copy-start(bf16[2,256,512]{2,1,0:T(8,128)(2,1)S(1)} %collective-permute-done.2.refs_2_) | copy-start | bytes 1572868
  44.9 4.3 %collective-permute-start.10 = (bf16[2,256,512]{2,1,0:T(8,128)(2,1)S(1)}, bf16[2,256,512]{2,1,0:T(8,128)(2,1)S(1)}, u32[]{:S(2)}, u32[]{:S(2)}) collective-permute-start(bf16[2,256,512]{2,1,0:T(8,128)(2,1)S(1)} %collective-permute-done.5.refs_1_.refs_6_), channel_id=1, source_target_pairs={{0,16},{16,0},{32,48},{48,32},{64,80},{80,64},{96,112},{112,96},{1... | collective-permute-start | bytes 1572872 | tf_op jit(solution)/shard_map/ppermute | solution.py:518
  45.0 4.2 %copy-start.14 = (bf16[2,256,512]{2,1,0:T(8,128)(2,1)}, bf16[2,256,512]{2,1,0:T(8,128)(2,1)S(1)}, u32[]{:S(2)}) copy-start(bf16[2,256,512]{2,1,0:T(8,128)(2,1)S(1)} %collective-permute-done.12.refs_12_) | copy-start | bytes 1572868
  45.0 4.2 %collective-permute-start.14 = (bf16[2,256,512]{2,1,0:T(8,128)(2,1)S(1)}, bf16[2,256,512]{2,1,0:T(8,128)(2,1)S(1)}, u32[]{:S(2)}, u32[]{:S(2)}) collective-permute-start(bf16[2,256,512]{2,1,0:T(8,128)(2,1)S(1)} %collective-permute-done.12.refs_12_), channel_id=1, source_target_pairs={{0,16},{16,0},{32,48},{48,32},{64,80},{80,64},{96,112},{112,96},{1... | collective-permute-start | bytes 1572872 | tf_op jit(solution)/shard_map/ppermute | solution.py:518
  45.4 4.9 %copy-start.2 = (bf16[384,768]{1,0:T(8,128)(2,1)}, bf16[384,768]{1,0:T(8,128)(2,1)S(1)}, u32[]{:S(2)}) copy-start(bf16[384,768]{1,0:T(8,128)(2,1)S(1)} %collective-permute-done.16.refs_16_.ahead_ref) | copy-start | bytes 1769476
  45.4 3.1 %collective-permute-start.15 = (bf16[2,256,256]{2,1,0:T(8,128)(2,1)S(1)}, bf16[2,256,256]{2,1,0:T(8,128)(2,1)S(1)}, u32[]{:S(2)}, u32[]{:S(2)}) collective-permute-start(bf16[2,256,256]{2,1,0:T(8,128)(2,1)S(1)} %collective-permute-done.13.refs_13_), channel_id=1, source_target_pairs={{0,16},{16,0},{32,48},{48,32},{64,80},{80,64},{96,112},{112,96},{1... | collective-permute-start | bytes 786440 | tf_op jit(solution)/shard_map/ppermute | solution.py:518
  45.9 3.3 %copy-start.23 = (bf16[2,256,256]{2,1,0:T(8,128)(2,1)}, bf16[2,256,256]{2,1,0:T(8,128)(2,1)S(1)}, u32[]{:S(2)}) copy-start(bf16[2,256,256]{2,1,0:T(8,128)(2,1)S(1)} %collective-permute-done.11.refs_11_) | copy-start | bytes 786436
  45.9 3.0 %collective-permute-start.9 = (bf16[2,256,256]{2,1,0:T(8,128)(2,1)S(1)}, bf16[2,256,256]{2,1,0:T(8,128)(2,1)S(1)}, u32[]{:S(2)}, u32[]{:S(2)}) collective-permute-start(bf16[2,256,256]{2,1,0:T(8,128)(2,1)S(1)} %collective-permute-done.6.refs_5_), channel_id=1, source_target_pairs={{0,16},{16,0},{32,48},{48,32},{64,80},{80,64},{96,112},{112,96},{1... | collective-permute-start | bytes 786440 | tf_op jit(solution)/shard_map/ppermute | solution.py:518
  48.6 11.7 %collective-permute-start.20 = (bf16[192,768]{1,0:T(8,128)(2,1)S(1)}, bf16[192,768]{1,0:T(8,128)(2,1)S(1)}, u32[]{:S(2)}, u32[]{:S(2)}) collective-permute-start(bf16[192,768]{1,0:T(8,128)(2,1)S(1)} %collective-permute-done.17.refs_17_.apart_ref), channel_id=1, source_target_pairs={{0,16},{16,0},{32,48},{48,32},{64,80},{80,64},{96,112},{112,96},{1... | collective-permute-start | bytes 884744 | tf_op jit(solution)/shard_map/ppermute | solution.py:518
  48.9 11.3 %collective-permute-start.19 = (bf16[384,768]{1,0:T(8,128)(2,1)S(1)}, bf16[384,768]{1,0:T(8,128)(2,1)S(1)}, u32[]{:S(2)}, u32[]{:S(2)}) collective-permute-start(bf16[384,768]{1,0:T(8,128)(2,1)S(1)} %collective-permute-done.16.refs_16_.ahead_ref), channel_id=1, source_target_pairs={{0,16},{16,0},{32,48},{48,32},{64,80},{80,64},{96,112},{112,96},{1... | collective-permute-start | bytes 1769480 | tf_op jit(solution)/shard_map/ppermute | solution.py:518
  49.2 1.1 %copy-start.17 = (bf16[2,256,512]{2,1,0:T(8,128)(2,1)}, bf16[2,256,512]{2,1,0:T(8,128)(2,1)S(1)}, u32[]{:S(2)}) copy-start(bf16[2,256,512]{2,1,0:T(8,128)(2,1)S(1)} %collective-permute-done.14.refs_14_) | copy-start | bytes 1572868
  50.4 9.8 %copy-start.1 = (bf16[384,3072]{1,0:T(8,128)(2,1)S(1)}, bf16[384,3072]{1,0:T(8,128)(2,1)}, u32[]{:S(2)}) copy-start(bf16[384,3072]{1,0:T(8,128)(2,1)} %w_out_ref.3) | copy-start | bytes 7077892
  50.4 9.8 %copy-start.10 = (s32[8]{0:T(128)S(1)}, s32[8]{0:T(128)}, u32[]{:S(2)}) copy-start(s32[8]{0:T(128)} %stack.68.place_ref) | copy-start | bytes 100
  58.6 9.4 %collective-permute-start.18 = (bf16[2,272,256]{2,1,0:T(8,128)(2,1)}, bf16[2,272,256]{2,1,0:T(8,128)(2,1)S(1)}, u32[]{:S(2)}, u32[]{:S(2)}) collective-permute-start(bf16[2,272,256]{2,1,0:T(8,128)(2,1)} %get-tuple-element.28), channel_id=1, source_target_pairs={{0,8},{8,0},{1,9},{9,1},{2,10},{10,2},{3,11},{11,3},{4,12},{12,4},... | collective-permute-start | bytes 835592 | tf_op jit(solution)/shard_map/ppermute | solution.py:518
  63.2 4.9 %copy-start.6 = (f32[2,256,256]{2,1,0:T(8,128)S(1)}, f32[2,256,256]{2,1,0:T(8,128)}, u32[]{:S(2)}) copy-start(f32[2,256,256]{2,1,0:T(8,128)} %get-tuple-element.27.mid_ref) | copy-start | bytes 1572868
  69.2 7.8 %collective-permute-start.25 = (bf16[256,384]{1,0:T(8,128)(2,1)S(1)}, bf16[256,384]{1,0:T(8,128)(2,1)S(1)}, u32[]{:S(2)}, u32[]{:S(2)}) collective-permute-start(bf16[256,384]{1,0:T(8,128)(2,1)S(1)} %get-tuple-element.32.refs_0_), channel_id=1, source_target_pairs={{0,1},{1,2},{2,3},{3,0},{4,5},{5,6},{6,7},{7,4},{16,19},{17,16},{1... | collective-permute-start | bytes 589832 | tf_op jit(solution)/shard_map/ppermute | solution.py:518
  71.2 26.6 %copy-start.12 = (f32[384]{0:T(512)S(1)}, f32[384]{0:T(512)}, u32[]{:S(2)}) copy-start(f32[384]{0:T(512)} %param.15) | copy-start | bytes 4612
  71.2 9.7 %collective-permute-start.21 = (bf16[256,384]{1,0:T(8,128)(2,1)S(1)}, bf16[256,384]{1,0:T(8,128)(2,1)S(1)}, u32[]{:S(2)}, u32[]{:S(2)}) collective-permute-start(bf16[256,384]{1,0:T(8,128)(2,1)S(1)} %get-tuple-element.29.refs_0_), channel_id=1, source_target_pairs={{0,1},{1,2},{2,3},{3,0},{4,5},{5,6},{6,7},{7,4},{16,19},{17,16},{1... | collective-permute-start | bytes 589832 | tf_op jit(solution)/shard_map/ppermute | solution.py:518
  73.1 8.3 %collective-permute-start.26 = (bf16[256,384]{1,0:T(8,128)(2,1)S(1)}, bf16[256,384]{1,0:T(8,128)(2,1)S(1)}, u32[]{:S(2)}, u32[]{:S(2)}) collective-permute-start(bf16[256,384]{1,0:T(8,128)(2,1)S(1)} %get-tuple-element.32.refs_0_), channel_id=1, source_target_pairs={{0,3},{1,0},{2,1},{3,2},{4,7},{5,4},{6,5},{7,6},{16,17},{17,18},{1... | collective-permute-start | bytes 589832 | tf_op jit(solution)/shard_map/ppermute | solution.py:518
  76.9 8.2 %collective-permute-start.27 = (bf16[256,384]{1,0:T(8,128)(2,1)S(1)}, bf16[256,384]{1,0:T(8,128)(2,1)S(1)}, u32[]{:S(2)}, u32[]{:S(2)}) collective-permute-start(bf16[256,384]{1,0:T(8,128)(2,1)S(1)} %collective-permute-done.25.refs_1_), channel_id=1, source_target_pairs={{0,1},{1,2},{2,3},{3,0},{4,5},{5,6},{6,7},{7,4},{16,19},{17,16},{1... | collective-permute-start | bytes 589832 | tf_op jit(solution)/shard_map/ppermute | solution.py:518
  77.2 12.2 %collective-permute-start.22 = (bf16[256,384]{1,0:T(8,128)(2,1)S(1)}, bf16[256,384]{1,0:T(8,128)(2,1)S(1)}, u32[]{:S(2)}, u32[]{:S(2)}) collective-permute-start(bf16[256,384]{1,0:T(8,128)(2,1)S(1)} %get-tuple-element.29.refs_0_), channel_id=1, source_target_pairs={{0,3},{1,0},{2,1},{3,2},{4,7},{5,4},{6,5},{7,6},{16,17},{17,18},{1... | collective-permute-start | bytes 589832 | tf_op jit(solution)/shard_map/ppermute | solution.py:518
  80.9 8.5 %collective-permute-start.23 = (bf16[256,384]{1,0:T(8,128)(2,1)S(1)}, bf16[256,384]{1,0:T(8,128)(2,1)S(1)}, u32[]{:S(2)}, u32[]{:S(2)}) collective-permute-start(bf16[256,384]{1,0:T(8,128)(2,1)S(1)} %collective-permute-done.21.refs_1_), channel_id=1, source_target_pairs={{0,1},{1,2},{2,3},{3,0},{4,5},{5,6},{6,7},{7,4},{16,19},{17,16},{1... | collective-permute-start | bytes 589832 | tf_op jit(solution)/shard_map/ppermute | solution.py:518
  86.3 8.2 %collective-permute-start.28 = (bf16[256,384]{1,0:T(8,128)(2,1)S(1)}, bf16[256,384]{1,0:T(8,128)(2,1)S(1)}, u32[]{:S(2)}, u32[]{:S(2)}) collective-permute-start(bf16[256,384]{1,0:T(8,128)(2,1)S(1)} %get-tuple-element.34), channel_id=1, source_target_pairs={{0,4},{1,5},{2,6},{3,7},{4,0},{5,1},{6,2},{7,3},{8,12},{9,13},{10,... | collective-permute-start | bytes 589832 | tf_op jit(solution)/shard_map/ppermute | solution.py:518
  90.5 7.3 %collective-permute-start.24 = (bf16[256,384]{1,0:T(8,128)(2,1)S(1)}, bf16[256,384]{1,0:T(8,128)(2,1)S(1)}, u32[]{:S(2)}, u32[]{:S(2)}) collective-permute-start(bf16[256,384]{1,0:T(8,128)(2,1)S(1)} %get-tuple-element.31), channel_id=1, source_target_pairs={{0,4},{1,5},{2,6},{3,7},{4,0},{5,1},{6,2},{7,3},{8,12},{9,13},{10,... | collective-permute-start | bytes 589832 | tf_op jit(solution)/shard_map/ppermute | solution.py:518
  (8 other events, 7.0 us)

commit v5 on v4

--- a/solution.py
+++ b/solution.py
@@ -344,7 +344,7 @@
             pltpu.VMEM((frames, 2 * half, 2 * HEAD_DIM), F32),
             pltpu.SemaphoreType.DMA((26,)),
         ],
-        compiler_params=vmem(58),
+        compiler_params=vmem(55),
         cost_estimate=pl.CostEstimate(
             flops=9_000_000_000, bytes_accessed=8_000_000, transcendentals=5_000_000
         ),

time: 99.1 us -> 99.6 us (level)
  waiting for transfers between devices: 34.1 us -> 35.9 us
  starting transfers between devices: 35.4 us -> 34.3 us
    ppermute x29, waiting for transfers between devices: 34.1 us -> 35.9 us  [move(): return lax.ppermute(x, axis, [(i, to(i)) for i in range(count)])]
    ppermute x29, starting transfers between devices: 35.4 us -> 34.3 us  [move(): return lax.ppermute(x, axis, [(i, to(i)) for i in range(count)])]
  transfers between devices with their start and end apart: 29 -> 29, of which waited for: 13 -> 12; matrix products, arithmetic and copies ran while one was open for 1% -> 1% of each run, Pallas kernels for 12% -> 12%
where the time goes in v5:
time: 99.6 us; the launch traced here: 99.7 us
  waiting for transfers between devices  35.9 us (36%)
  starting transfers between devices  34.3 us (34%)
  Pallas kernels  22.5 us (23%)
  local copies, waits for them, and re-layouts  5.86 us (6%)
    ppermute x29, waiting for transfers between devices, move(): return lax.ppermute(x, axis, [(i, to(i)) for i in range(count)])  35.9 us
    ppermute x29, starting transfers between devices, move(): return lax.ppermute(x, axis, [(i, to(i)) for i in range(count)])  34.3 us
    pallas_call x1, Pallas kernels, project(): pl.pallas_call(project_kernel, out_shape=[jax.ShapeDtypeStruct(shape, BF1...  9.91 us
    pallas_call x1, Pallas kernels, attend(): pl.pallas_call(attend_kernel, out_shape=[jax.ShapeDtypeStruct((frames * h...  8.21 us
    unnamed x54, local copies, waits for them, and re-layouts  4.61 us
    pallas_call x2, Pallas kernels, output(): pl.pallas_call(output_kernel, out_shape=[jax.ShapeDtypeStruct((rows, cols...  2.21 us
  transfers between devices with their start and end apart: 29, of which 12 were waited for; matrix products, arithmetic and copies ran while one was open for 1% of the time, Pallas kernels for 12%

profile of v5, /device:TPU:0, one launch (start us, length us, event | category | flops | bytes accessed | tf_op | source)
XLA Modules:
  0.0 99.7 jit_solution(3110932889411639244)
XLA Ops:
  0.0 0.7 stack.68.place_ref
  0.7 9.9 %project.1 = (bf16[512,512]{1,0:T(8,128)(2,1)}, bf16[512,256]{1,0:T(8,128)(2,1)}, bf16[512,256]{1,0:T(8,128)(2,1)}, bf16[512,256]{1,0:T(8,128)(2,1)}, bf16[384,7...) custom-call(s32[8]{0:T(128)} %stack.68.place_ref, bf16[512,3072]{1,0:T(8,128)(2,1)} %bitcast.32, bf16[3,3072,384]{2,1,0:T(8,128)(2,1)} %bitcast.31, ...), custom_call_target="tpu_custom_call" | custom-call | flops 3623878656 | bytes 12000000 | tf_op jit(solution)/shard_map/project/pallas_call | solution.py:144
  10.6 1.7 %collective-permute-start.4 = (bf16[2,256,512]{2,1,0:T(8,128)(2,1)}, bf16[2,256,512]{2,1,0:T(8,128)(2,1)S(1)}, u32[]{:S(2)}, u32[]{:S(2)}) collective-permute-start(bf16[2,256,512]{2,1,0:T(8,128)(2,1)} %bitcast.33), channel_id=1, source_target_pairs={{0,32},{16,112},{32,64},{48,16},{64,96},{80,48},{96,0},{112,80},{1... | collective-permute-start | bytes 1572872 | tf_op jit(solution)/shard_map/ppermute | solution.py:518
  12.3 1.6 %collective-permute-start.5 = (bf16[2,256,512]{2,1,0:T(8,128)(2,1)}, bf16[2,256,512]{2,1,0:T(8,128)(2,1)S(1)}, u32[]{:S(2)}, u32[]{:S(2)}) collective-permute-start(bf16[2,256,512]{2,1,0:T(8,128)(2,1)} %bitcast.34), channel_id=1, source_target_pairs={{0,96},{16,48},{32,0},{48,80},{64,32},{80,112},{96,64},{112,16},{1... | collective-permute-start | bytes 1572872 | tf_op jit(solution)/shard_map/ppermute | solution.py:518
  13.9 1.6 %collective-permute-start.1 = (bf16[2,256,256]{2,1,0:T(8,128)(2,1)}, bf16[2,256,256]{2,1,0:T(8,128)(2,1)S(1)}, u32[]{:S(2)}, u32[]{:S(2)}) collective-permute-start(bf16[2,256,256]{2,1,0:T(8,128)(2,1)} %bitcast.38), channel_id=1, source_target_pairs={{0,8},{8,0},{1,9},{9,1},{2,10},{10,2},{3,11},{11,3},{4,12},{12,4},... | collective-permute-start | bytes 786440 | tf_op jit(solution)/shard_map/ppermute | solution.py:518
  15.5 0.5 collective-permute-start
  15.9 4.0 %collective-permute-start.17 = (bf16[192,768]{1,0:T(8,128)(2,1)}, bf16[192,768]{1,0:T(8,128)(2,1)S(1)}, u32[]{:S(2)}, u32[]{:S(2)}) collective-permute-start(bf16[192,768]{1,0:T(8,128)(2,1)} %get-tuple-element.25), channel_id=1, source_target_pairs={{0,2},{1,3},{2,0},{3,1},{4,6},{5,7},{6,4},{7,5},{8,10},{9,11},{10,... | collective-permute-start | bytes 884744 | tf_op jit(solution)/shard_map/ppermute | solution.py:518
  20.0 0.2 copy.13
  20.5 2.9 %collective-permute-done.1.refs_1_ = bf16[2,256,256]{2,1,0:T(8,128)(2,1)S(1)} collective-permute-done((bf16[2,256,256]{2,1,0:T(8,128)(2,1)}, bf16[2,256,256]{2,1,0:T(8,128)(2,1)S(1)}, u32[]{:S(2)}, u32[]{:S(2)}) %collective-permute-start.1) | collective-permute-done | bytes 262176 | tf_op jit(solution)/shard_map/ppermute | solution.py:518
  23.4 1.7 %collective-permute-start.7 = (bf16[2,256,256]{2,1,0:T(8,128)(2,1)S(1)}, bf16[2,256,256]{2,1,0:T(8,128)(2,1)S(1)}, u32[]{:S(2)}, u32[]{:S(2)}) collective-permute-start(bf16[2,256,256]{2,1,0:T(8,128)(2,1)S(1)} %collective-permute-done.1.refs_1_), channel_id=1, source_target_pairs={{0,96},{16,48},{32,0},{48,80},{64,32},{80,112},{96,64},{112,16},{1... | collective-permute-start | bytes 786440 | tf_op jit(solution)/shard_map/ppermute | solution.py:518
  25.1 3.8 %collective-permute-start.13 = (bf16[2,256,256]{2,1,0:T(8,128)(2,1)S(1)}, bf16[2,256,256]{2,1,0:T(8,128)(2,1)S(1)}, u32[]{:S(2)}, u32[]{:S(2)}) collective-permute-start(bf16[2,256,256]{2,1,0:T(8,128)(2,1)S(1)} %collective-permute-done.1.refs_1_), channel_id=1, source_target_pairs={{0,64},{16,80},{32,96},{48,112},{64,0},{80,16},{96,32},{112,48},{1... | collective-permute-start | bytes 786440 | tf_op jit(solution)/shard_map/ppermute | solution.py:518
  29.0 0.7 collective-permute-start.12
  29.7 1.9 %collective-permute-start.16 = (bf16[384,768]{1,0:T(8,128)(2,1)}, bf16[384,768]{1,0:T(8,128)(2,1)S(1)}, u32[]{:S(2)}, u32[]{:S(2)}) collective-permute-start(bf16[384,768]{1,0:T(8,128)(2,1)} %get-tuple-element.24), channel_id=1, source_target_pairs={{0,1},{1,2},{2,3},{3,0},{4,5},{5,6},{6,7},{7,4},{16,19},{17,16},{1... | collective-permute-start | bytes 1769480 | tf_op jit(solution)/shard_map/ppermute | solution.py:518
  31.6 1.6 %collective-permute-done.7.refs_7_ = bf16[2,256,256]{2,1,0:T(8,128)(2,1)S(1)} collective-permute-done((bf16[2,256,256]{2,1,0:T(8,128)(2,1)S(1)}, bf16[2,256,256]{2,1,0:T(8,128)(2,1)S(1)}, u32[]{:S(2)}, u32[]{:S(2)}) %collective-permute-start.7) | collective-permute-done | bytes 262176 | tf_op jit(solution)/shard_map/ppermute | solution.py:518
  33.2 2.9 %collective-permute-done.13.refs_13_ = bf16[2,256,256]{2,1,0:T(8,128)(2,1)S(1)} collective-permute-done((bf16[2,256,256]{2,1,0:T(8,128)(2,1)S(1)}, bf16[2,256,256]{2,1,0:T(8,128)(2,1)S(1)}, u32[]{:S(2)}, u32[]{:S(2)}) %collective-permute-start.13) | collective-permute-done | bytes 262176 | tf_op jit(solution)/shard_map/ppermute | solution.py:518
  36.1 8.3 %collective-permute-done.6.refs_5_ = bf16[2,256,256]{2,1,0:T(8,128)(2,1)S(1)} collective-permute-done((bf16[2,256,256]{2,1,0:T(8,128)(2,1)S(1)}, bf16[2,256,256]{2,1,0:T(8,128)(2,1)S(1)}, u32[]{:S(2)}, u32[]{:S(2)}) %collective-permute-start.6) | collective-permute-done | bytes 262176 | tf_op jit(solution)/shard_map/ppermute | solution.py:518
  44.4 0.5 collective-permute-start.8
  45.0 0.4 collective-permute-start.14
  45.4 0.3 collective-permute-start.15
  45.7 0.2 collective-permute-done.11.refs_11_
  46.1 2.5 %collective-permute-done.15.refs_15_ = bf16[2,256,256]{2,1,0:T(8,128)(2,1)S(1)} collective-permute-done((bf16[2,256,256]{2,1,0:T(8,128)(2,1)S(1)}, bf16[2,256,256]{2,1,0:T(8,128)(2,1)S(1)}, u32[]{:S(2)}, u32[]{:S(2)}) %collective-permute-start.15) | collective-permute-done | bytes 262176 | tf_op jit(solution)/shard_map/ppermute | solution.py:518
  48.7 0.6 copy-done.24
  49.5 0.5 copy-done.25
  50.2 0.2 copy-done.16
  50.6 8.2 %attend.1 = (bf16[512,128]{1,0:T(8,128)(2,1)}, f32[2,256,256]{2,1,0:T(8,128)}, bf16[2,272,256]{2,1,0:T(8,128)(2,1)}) custom-call(s32[76]{0:T(128)} %copy-done.11, bf16[2,256,256]{2,1,0:T(8,128)(2,1)} %bitcast.43, bf16[2,256,256]{2,1,0:T(8,128)(2,1)} %copy-done.19, bf16[2,256,512]{2,1,0:T(8,128)(2,1)} %bitcast.36, bf16[2,256,256]{2,1,0:T(8,128)(2,1)} %copy-done.18, ...), custom_call_target="tpu_custom_call" | custom-call | flops 8999999488 | bytes 8000000 | tf_op jit(solution)/shard_map/attend/pallas_call | solution.py:328
  58.8 1.6 %collective-permute-start.18 = (bf16[2,272,256]{2,1,0:T(8,128)(2,1)}, bf16[2,272,256]{2,1,0:T(8,128)(2,1)S(1)}, u32[]{:S(2)}, u32[]{:S(2)}) collective-permute-start(bf16[2,272,256]{2,1,0:T(8,128)(2,1)} %get-tuple-element.28), channel_id=1, source_target_pairs={{0,8},{8,0},{1,9},{9,1},{2,10},{10,2},{3,11},{11,3},{4,12},{12,4},... | collective-permute-start | bytes 835592 | tf_op jit(solution)/shard_map/ppermute | solution.py:518
  60.4 1.1 %copy-done.3 = bf16[384,768]{1,0:T(8,128)(2,1)S(1)} copy-done((bf16[384,768]{1,0:T(8,128)(2,1)S(1)}, bf16[384,768]{1,0:T(8,128)(2,1)}, u32[]{:S(2)}) %copy-start.3) | copy-done | bytes 589848
  61.5 0.9 copy-done.7
  62.4 1.0 copy-done.9
  63.3 1.1 %assemble.1._.refs_4_ = bf16[1536,768]{1,0:T(8,128)(2,1)S(1)} custom-call(s32[8]{0:T(128)S(1)} %copy-done.10, bf16[384,3072]{1,0:T(8,128)(2,1)S(1)} %copy-done.1, bf16[384,768]{1,0:T(8,128)(2,1)S(1)} %copy-done.3, bf16[384,768]{1,0:T(8,128)(2,1)S(1)} %collective-permute-done.19.behind_ref, bf16[192,768]{1,0:T(8,128)(2,1)S(1)} %copy-done.9, ...), custom_call_target="tpu_custom_call" | custom-call | bytes 4000000 | tf_op jit(solution)/shard_map/assemble/pallas_call | solution.py:459
  64.4 3.6 %collective-permute-done.18.got_ref = bf16[2,272,256]{2,1,0:T(8,128)(2,1)S(1)} collective-permute-done((bf16[2,272,256]{2,1,0:T(8,128)(2,1)}, bf16[2,272,256]{2,1,0:T(8,128)(2,1)S(1)}, u32[]{:S(2)}, u32[]{:S(2)}) %collective-permute-start.18) | collective-permute-done | bytes 278560 | tf_op jit(solution)/shard_map/ppermute | solution.py:518
  68.0 1.1 %combine.1 = (bf16[256,384]{1,0:T(8,128)(2,1)S(1)}, bf16[256,384]{1,0:T(8,128)(2,1)S(1)}) custom-call(s32[8]{0:T(128)S(1)} %copy-done.10, bf16[512,128]{1,0:T(8,128)(2,1)S(1)} %copy-done.7, f32[2,256,256]{2,1,0:T(8,128)S(1)} %copy-done.6, bf16[2,272,256]{2,1,0:T(8,128)(2,1)S(1)} %collective-permute-done.18.got_ref, bf16[1536,768]{1,0:T(8,128)(2,1)S(1)} %assemble.1._.refs_4_), custom_call_target="tpu_custom_call" | custom-call | flops 50000000 | bytes 1500000 | tf_op jit(solution)/shard_map/combine/pallas_call | solution.py:391
  69.1 2.0 %collective-permute-start.25 = (bf16[256,384]{1,0:T(8,128)(2,1)S(1)}, bf16[256,384]{1,0:T(8,128)(2,1)S(1)}, u32[]{:S(2)}, u32[]{:S(2)}) collective-permute-start(bf16[256,384]{1,0:T(8,128)(2,1)S(1)} %get-tuple-element.32.refs_0_), channel_id=1, source_target_pairs={{0,1},{1,2},{2,3},{3,0},{4,5},{5,6},{6,7},{7,4},{16,19},{17,16},{1... | collective-permute-start | bytes 589832 | tf_op jit(solution)/shard_map/ppermute | solution.py:518
  71.1 1.9 %collective-permute-start.21 = (bf16[256,384]{1,0:T(8,128)(2,1)S(1)}, bf16[256,384]{1,0:T(8,128)(2,1)S(1)}, u32[]{:S(2)}, u32[]{:S(2)}) collective-permute-start(bf16[256,384]{1,0:T(8,128)(2,1)S(1)} %get-tuple-element.29.refs_0_), channel_id=1, source_target_pairs={{0,1},{1,2},{2,3},{3,0},{4,5},{5,6},{6,7},{7,4},{16,19},{17,16},{1... | collective-permute-start | bytes 589832 | tf_op jit(solution)/shard_map/ppermute | solution.py:518
  73.0 1.3 %collective-permute-start.26 = (bf16[256,384]{1,0:T(8,128)(2,1)S(1)}, bf16[256,384]{1,0:T(8,128)(2,1)S(1)}, u32[]{:S(2)}, u32[]{:S(2)}) collective-permute-start(bf16[256,384]{1,0:T(8,128)(2,1)S(1)} %get-tuple-element.32.refs_0_), channel_id=1, source_target_pairs={{0,3},{1,0},{2,1},{3,2},{4,7},{5,4},{6,5},{7,6},{16,17},{17,18},{1... | collective-permute-start | bytes 589832 | tf_op jit(solution)/shard_map/ppermute | solution.py:518
  74.3 2.9 %collective-permute-done.25.refs_1_ = bf16[256,384]{1,0:T(8,128)(2,1)S(1)} collective-permute-done((bf16[256,384]{1,0:T(8,128)(2,1)S(1)}, bf16[256,384]{1,0:T(8,128)(2,1)S(1)}, u32[]{:S(2)}, u32[]{:S(2)}) %collective-permute-start.25) | collective-permute-done | bytes 196640 | tf_op jit(solution)/shard_map/ppermute | solution.py:518
  77.3 0.6 collective-permute-start.27
  77.9 2.6 %collective-permute-start.22 = (bf16[256,384]{1,0:T(8,128)(2,1)S(1)}, bf16[256,384]{1,0:T(8,128)(2,1)S(1)}, u32[]{:S(2)}, u32[]{:S(2)}) collective-permute-start(bf16[256,384]{1,0:T(8,128)(2,1)S(1)} %get-tuple-element.29.refs_0_), channel_id=1, source_target_pairs={{0,3},{1,0},{2,1},{3,2},{4,7},{5,4},{6,5},{7,6},{16,17},{17,18},{1... | collective-permute-start | bytes 589832 | tf_op jit(solution)/shard_map/ppermute | solution.py:518
  80.5 0.6 collective-permute-done.21.refs_1_
  81.1 1.0 collective-permute-start.23
  82.1 4.2 %collective-permute-done.27.refs_3_ = bf16[256,384]{1,0:T(8,128)(2,1)S(1)} collective-permute-done((bf16[256,384]{1,0:T(8,128)(2,1)S(1)}, bf16[256,384]{1,0:T(8,128)(2,1)S(1)}, u32[]{:S(2)}, u32[]{:S(2)}) %collective-permute-start.27) | collective-permute-done | bytes 196640 | tf_op jit(solution)/shard_map/ppermute | solution.py:518
  86.2 1.1 %output.3 = (f32[256,384]{1,0:T(8,128)S(1)}, bf16[256,384]{1,0:T(8,128)(2,1)S(1)}) custom-call(bf16[256,384]{1,0:T(8,128)(2,1)S(1)} %get-tuple-element.32.refs_0_, bf16[256,384]{1,0:T(8,128)(2,1)S(1)} %collective-permute-done.25.refs_1_, bf16[256,384]{1,0:T(8,128)(2,1)S(1)} %collective-permute-done.26.refs_2_, ...), custom_call_target="tpu_custom_call" | custom-call | flops 603979776 | bytes 4000000 | tf_op jit(solution)/shard_map/output/pallas_call | solution.py:493
  87.4 3.1 %collective-permute-start.28 = (bf16[256,384]{1,0:T(8,128)(2,1)S(1)}, bf16[256,384]{1,0:T(8,128)(2,1)S(1)}, u32[]{:S(2)}, u32[]{:S(2)}) collective-permute-start(bf16[256,384]{1,0:T(8,128)(2,1)S(1)} %get-tuple-element.34), channel_id=1, source_target_pairs={{0,4},{1,5},{2,6},{3,7},{4,0},{5,1},{6,2},{7,3},{8,12},{9,13},{10,... | collective-permute-start | bytes 589832 | tf_op jit(solution)/shard_map/ppermute | solution.py:518
  90.5 1.1 %output.2 = (f32[256,384]{1,0:T(8,128)S(1)}, bf16[256,384]{1,0:T(8,128)(2,1)S(1)}) custom-call(bf16[256,384]{1,0:T(8,128)(2,1)S(1)} %get-tuple-element.29.refs_0_, bf16[256,384]{1,0:T(8,128)(2,1)S(1)} %collective-permute-done.21.refs_1_, bf16[256,384]{1,0:T(8,128)(2,1)S(1)} %collective-permute-done.22.refs_2_, ...), custom_call_target="tpu_custom_call" | custom-call | flops 603979776 | bytes 4000000 | tf_op jit(solution)/shard_map/output/pallas_call | solution.py:493
  91.6 1.0 collective-permute-start.24
  92.6 3.3 %collective-permute-done.28 = bf16[256,384]{1,0:T(8,128)(2,1)S(1)} collective-permute-done((bf16[256,384]{1,0:T(8,128)(2,1)S(1)}, bf16[256,384]{1,0:T(8,128)(2,1)S(1)}, u32[]{:S(2)}, u32[]{:S(2)}) %collective-permute-start.28) | collective-permute-done | bytes 196640 | tf_op jit(solution)/shard_map/ppermute | solution.py:518
  95.9 3.0 %collective-permute-done.24 = bf16[256,384]{1,0:T(8,128)(2,1)S(1)} collective-permute-done((bf16[256,384]{1,0:T(8,128)(2,1)S(1)}, bf16[256,384]{1,0:T(8,128)(2,1)S(1)}, u32[]{:S(2)}, u32[]{:S(2)}) %collective-permute-start.24) | collective-permute-done | bytes 196640 | tf_op jit(solution)/shard_map/ppermute | solution.py:518
  98.9 0.8 pad_maximum_fusion
  (79 shorter events, 1.4 us)
Async XLA Ops:
  0.0 19.9 %copy-start = (s32[16,4,4,2]{0,3,2,1:T(2,128)S(1)}, s32[16,4,4,2]{0,3,2,1:T(2,128)}, u32[]{:S(2)}) copy-start(s32[16,4,4,2]{0,3,2,1:T(2,128)} %param.19) | copy-start | bytes 6148
  0.7 19.6 %copy-start.26 = (s32[16]{0:T(128)S(1)}, s32[16]{0:T(128)}, u32[]{:S(2)}) copy-start(s32[16]{0:T(128)} %param.18) | copy-start | bytes 196
  10.6 14.5 %collective-permute-start.4 = (bf16[2,256,512]{2,1,0:T(8,128)(2,1)}, bf16[2,256,512]{2,1,0:T(8,128)(2,1)S(1)}, u32[]{:S(2)}, u32[]{:S(2)}) collective-permute-start(bf16[2,256,512]{2,1,0:T(8,128)(2,1)} %bitcast.33), channel_id=1, source_target_pairs={{0,32},{16,112},{32,64},{48,16},{64,96},{80,48},{96,0},{112,80},{1... | collective-permute-start | bytes 1572872 | tf_op jit(solution)/shard_map/ppermute | solution.py:518
  12.3 16.6 %collective-permute-start.5 = (bf16[2,256,512]{2,1,0:T(8,128)(2,1)}, bf16[2,256,512]{2,1,0:T(8,128)(2,1)S(1)}, u32[]{:S(2)}, u32[]{:S(2)}) collective-permute-start(bf16[2,256,512]{2,1,0:T(8,128)(2,1)} %bitcast.34), channel_id=1, source_target_pairs={{0,96},{16,48},{32,0},{48,80},{64,32},{80,112},{96,64},{112,16},{1... | collective-permute-start | bytes 1572872 | tf_op jit(solution)/shard_map/ppermute | solution.py:518
  13.9 9.5 %collective-permute-start.1 = (bf16[2,256,256]{2,1,0:T(8,128)(2,1)}, bf16[2,256,256]{2,1,0:T(8,128)(2,1)S(1)}, u32[]{:S(2)}, u32[]{:S(2)}) collective-permute-start(bf16[2,256,256]{2,1,0:T(8,128)(2,1)} %bitcast.38), channel_id=1, source_target_pairs={{0,8},{8,0},{1,9},{9,1},{2,10},{10,2},{3,11},{11,3},{4,12},{12,4},... | collective-permute-start | bytes 786440 | tf_op jit(solution)/shard_map/ppermute | solution.py:518
  15.5 13.5 %collective-permute-start = (bf16[2,256,256]{2,1,0:T(8,128)(2,1)}, bf16[2,256,256]{2,1,0:T(8,128)(2,1)S(1)}, u32[]{:S(2)}, u32[]{:S(2)}) collective-permute-start(bf16[2,256,256]{2,1,0:T(8,128)(2,1)} %bitcast.37), channel_id=1, source_target_pairs={{0,8},{8,0},{1,9},{9,1},{2,10},{10,2},{3,11},{11,3},{4,12},{12,4},... | collective-permute-start | bytes 786440 | tf_op jit(solution)/shard_map/ppermute | solution.py:518
  15.9 13.8 %collective-permute-start.17 = (bf16[192,768]{1,0:T(8,128)(2,1)}, bf16[192,768]{1,0:T(8,128)(2,1)S(1)}, u32[]{:S(2)}, u32[]{:S(2)}) collective-permute-start(bf16[192,768]{1,0:T(8,128)(2,1)} %get-tuple-element.25), channel_id=1, source_target_pairs={{0,2},{1,3},{2,0},{3,1},{4,6},{5,7},{6,4},{7,5},{8,10},{9,11},{10,... | collective-permute-start | bytes 884744 | tf_op jit(solution)/shard_map/ppermute | solution.py:518
  20.5 29.5 %copy-start.11 = (s32[76]{0:T(128)}, s32[76]{0:T(128)S(1)}, u32[]{:S(2)}) copy-start(s32[76]{0:T(128)S(1)} %concatenate.3.refs_2_.meta_ref) | copy-start | bytes 916
  23.4 26.6 %copy-start.18 = (bf16[2,256,256]{2,1,0:T(8,128)(2,1)}, bf16[2,256,256]{2,1,0:T(8,128)(2,1)S(1)}, u32[]{:S(2)}) copy-start(bf16[2,256,256]{2,1,0:T(8,128)(2,1)S(1)} %collective-permute-done.1.refs_1_) | copy-start | bytes 786436
  23.4 9.8 %collective-permute-start.7 = (bf16[2,256,256]{2,1,0:T(8,128)(2,1)S(1)}, bf16[2,256,256]{2,1,0:T(8,128)(2,1)S(1)}, u32[]{:S(2)}, u32[]{:S(2)}) collective-permute-start(bf16[2,256,256]{2,1,0:T(8,128)(2,1)S(1)} %collective-permute-done.1.refs_1_), channel_id=1, source_target_pairs={{0,96},{16,48},{32,0},{48,80},{64,32},{80,112},{96,64},{112,16},{1... | collective-permute-start | bytes 786440 | tf_op jit(solution)/shard_map/ppermute | solution.py:518
  25.1 10.9 %collective-permute-start.13 = (bf16[2,256,256]{2,1,0:T(8,128)(2,1)S(1)}, bf16[2,256,256]{2,1,0:T(8,128)(2,1)S(1)}, u32[]{:S(2)}, u32[]{:S(2)}) collective-permute-start(bf16[2,256,256]{2,1,0:T(8,128)(2,1)S(1)} %collective-permute-done.1.refs_1_), channel_id=1, source_target_pairs={{0,64},{16,80},{32,96},{48,112},{64,0},{80,16},{96,32},{112,48},{1... | collective-permute-start | bytes 786440 | tf_op jit(solution)/shard_map/ppermute | solution.py:518
  29.0 21.1 %copy-start.4 = (bf16[2,256,512]{2,1,0:T(8,128)(2,1)}, bf16[2,256,512]{2,1,0:T(8,128)(2,1)S(1)}, u32[]{:S(2)}) copy-start(bf16[2,256,512]{2,1,0:T(8,128)(2,1)S(1)} %collective-permute-done.5.refs_1_.refs_6_) | copy-start | bytes 1572868
  29.0 16.0 %collective-permute-start.2 = (bf16[2,256,512]{2,1,0:T(8,128)(2,1)}, bf16[2,256,512]{2,1,0:T(8,128)(2,1)S(1)}, u32[]{:S(2)}, u32[]{:S(2)}) collective-permute-start(bf16[2,256,512]{2,1,0:T(8,128)(2,1)} %bitcast.35), channel_id=1, source_target_pairs={{0,16},{16,0},{32,48},{48,32},{64,80},{80,64},{96,112},{112,96},{1... | collective-permute-start | bytes 1572872 | tf_op jit(solution)/shard_map/ppermute | solution.py:518
  29.0 21.0 %copy-start.5 = (bf16[2,256,512]{2,1,0:T(8,128)(2,1)}, bf16[2,256,512]{2,1,0:T(8,128)(2,1)S(1)}, u32[]{:S(2)}) copy-start(bf16[2,256,512]{2,1,0:T(8,128)(2,1)S(1)} %after.1.refs_4_) | copy-start | bytes 1572868
  29.0 21.0 %copy-start.19 = (bf16[2,256,256]{2,1,0:T(8,128)(2,1)}, bf16[2,256,256]{2,1,0:T(8,128)(2,1)S(1)}, u32[]{:S(2)}) copy-start(bf16[2,256,256]{2,1,0:T(8,128)(2,1)S(1)} %collective-permute-done.away_ref) | copy-start | bytes 786436
  29.0 16.0 %collective-permute-start.12 = (bf16[2,256,512]{2,1,0:T(8,128)(2,1)S(1)}, bf16[2,256,512]{2,1,0:T(8,128)(2,1)S(1)}, u32[]{:S(2)}, u32[]{:S(2)}) collective-permute-start(bf16[2,256,512]{2,1,0:T(8,128)(2,1)S(1)} %after.1.refs_4_), channel_id=1, source_target_pairs={{0,32},{16,112},{32,64},{48,16},{64,96},{80,48},{96,0},{112,80},{1... | collective-permute-start | bytes 1572872 | tf_op jit(solution)/shard_map/ppermute | solution.py:518
  29.7 20.3 %copy-start.8 = (bf16[192,768]{1,0:T(8,128)(2,1)}, bf16[192,768]{1,0:T(8,128)(2,1)S(1)}, u32[]{:S(2)}) copy-start(bf16[192,768]{1,0:T(8,128)(2,1)S(1)} %collective-permute-done.17.refs_17_.apart_ref) | copy-start | bytes 884740
  29.7 15.7 %collective-permute-start.16 = (bf16[384,768]{1,0:T(8,128)(2,1)}, bf16[384,768]{1,0:T(8,128)(2,1)S(1)}, u32[]{:S(2)}, u32[]{:S(2)}) collective-permute-start(bf16[384,768]{1,0:T(8,128)(2,1)} %get-tuple-element.24), channel_id=1, source_target_pairs={{0,1},{1,2},{2,3},{3,0},{4,5},{5,6},{6,7},{7,4},{16,19},{17,16},{1... | collective-permute-start | bytes 1769480 | tf_op jit(solution)/shard_map/ppermute | solution.py:518
  33.2 16.8 %copy-start.20 = (bf16[2,256,256]{2,1,0:T(8,128)(2,1)}, bf16[2,256,256]{2,1,0:T(8,128)(2,1)S(1)}, u32[]{:S(2)}) copy-start(bf16[2,256,256]{2,1,0:T(8,128)(2,1)S(1)} %collective-permute-done.7.refs_7_) | copy-start | bytes 786436
  33.2 11.2 %collective-permute-start.6 = (bf16[2,256,256]{2,1,0:T(8,128)(2,1)S(1)}, bf16[2,256,256]{2,1,0:T(8,128)(2,1)S(1)}, u32[]{:S(2)}, u32[]{:S(2)}) collective-permute-start(bf16[2,256,256]{2,1,0:T(8,128)(2,1)S(1)} %collective-permute-done.1.refs_1_), channel_id=1, source_target_pairs={{0,32},{16,112},{32,64},{48,16},{64,96},{80,48},{96,0},{112,80},{1... | collective-permute-start | bytes 786440 | tf_op jit(solution)/shard_map/ppermute | solution.py:518
  36.1 14.0 %copy-start.21 = (bf16[2,256,256]{2,1,0:T(8,128)(2,1)}, bf16[2,256,256]{2,1,0:T(8,128)(2,1)S(1)}, u32[]{:S(2)}) copy-start(bf16[2,256,256]{2,1,0:T(8,128)(2,1)S(1)} %collective-permute-done.13.refs_13_) | copy-start | bytes 786436
  36.1 8.3 %collective-permute-start.3 = (bf16[2,256,256]{2,1,0:T(8,128)(2,1)S(1)}, bf16[2,256,256]{2,1,0:T(8,128)(2,1)}, u32[]{:S(2)}, u32[]{:S(2)}) collective-permute-start(bf16[2,256,256]{2,1,0:T(8,128)(2,1)S(1)} %collective-permute-done.1.refs_1_), channel_id=1, source_target_pairs={{0,16},{16,0},{32,48},{48,32},{64,80},{80,64},{96,112},{112,96},{1... | collective-permute-start | bytes 786440 | tf_op jit(solution)/shard_map/ppermute | solution.py:518
  44.4 5.7 %copy-start.22 = (bf16[2,256,256]{2,1,0:T(8,128)(2,1)}, bf16[2,256,256]{2,1,0:T(8,128)(2,1)S(1)}, u32[]{:S(2)}) copy-start(bf16[2,256,256]{2,1,0:T(8,128)(2,1)S(1)} %collective-permute-done.6.refs_5_) | copy-start | bytes 786436
  44.4 1.5 %collective-permute-start.11 = (bf16[2,256,256]{2,1,0:T(8,128)(2,1)S(1)}, bf16[2,256,256]{2,1,0:T(8,128)(2,1)S(1)}, u32[]{:S(2)}, u32[]{:S(2)}) collective-permute-start(bf16[2,256,256]{2,1,0:T(8,128)(2,1)S(1)} %collective-permute-done.7.refs_7_), channel_id=1, source_target_pairs={{0,16},{16,0},{32,48},{48,32},{64,80},{80,64},{96,112},{112,96},{1... | collective-permute-start | bytes 786440 | tf_op jit(solution)/shard_map/ppermute | solution.py:518
  44.4 5.0 %collective-permute-start.8 = (bf16[2,256,512]{2,1,0:T(8,128)(2,1)S(1)}, bf16[2,256,512]{2,1,0:T(8,128)(2,1)S(1)}, u32[]{:S(2)}, u32[]{:S(2)}) collective-permute-start(bf16[2,256,512]{2,1,0:T(8,128)(2,1)S(1)} %after.1.refs_4_), channel_id=1, source_target_pairs={{0,16},{16,0},{32,48},{48,32},{64,80},{80,64},{96,112},{112,96},{1... | collective-permute-start | bytes 1572872 | tf_op jit(solution)/shard_map/ppermute | solution.py:518
  44.9 5.1 %copy-start.13 = (bf16[2,256,512]{2,1,0:T(8,128)(2,1)}, bf16[2,256,512]{2,1,0:T(8,128)(2,1)S(1)}, u32[]{:S(2)}) copy-start(bf16[2,256,512]{2,1,0:T(8,128)(2,1)S(1)} %collective-permute-done.2.refs_2_) | copy-start | bytes 1572868
  44.9 4.5 %collective-permute-start.10 = (bf16[2,256,512]{2,1,0:T(8,128)(2,1)S(1)}, bf16[2,256,512]{2,1,0:T(8,128)(2,1)S(1)}, u32[]{:S(2)}, u32[]{:S(2)}) collective-permute-start(bf16[2,256,512]{2,1,0:T(8,128)(2,1)S(1)} %collective-permute-done.5.refs_1_.refs_6_), channel_id=1, source_target_pairs={{0,16},{16,0},{32,48},{48,32},{64,80},{80,64},{96,112},{112,96},{1... | collective-permute-start | bytes 1572872 | tf_op jit(solution)/shard_map/ppermute | solution.py:518
  45.0 5.1 %copy-start.14 = (bf16[2,256,512]{2,1,0:T(8,128)(2,1)}, bf16[2,256,512]{2,1,0:T(8,128)(2,1)S(1)}, u32[]{:S(2)}) copy-start(bf16[2,256,512]{2,1,0:T(8,128)(2,1)S(1)} %collective-permute-done.12.refs_12_) | copy-start | bytes 1572868
  45.0 4.4 %collective-permute-start.14 = (bf16[2,256,512]{2,1,0:T(8,128)(2,1)S(1)}, bf16[2,256,512]{2,1,0:T(8,128)(2,1)S(1)}, u32[]{:S(2)}, u32[]{:S(2)}) collective-permute-start(bf16[2,256,512]{2,1,0:T(8,128)(2,1)S(1)} %collective-permute-done.12.refs_12_), channel_id=1, source_target_pairs={{0,16},{16,0},{32,48},{48,32},{64,80},{80,64},{96,112},{112,96},{1... | collective-permute-start | bytes 1572872 | tf_op jit(solution)/shard_map/ppermute | solution.py:518
  45.4 4.6 %copy-start.2 = (bf16[384,768]{1,0:T(8,128)(2,1)}, bf16[384,768]{1,0:T(8,128)(2,1)S(1)}, u32[]{:S(2)}) copy-start(bf16[384,768]{1,0:T(8,128)(2,1)S(1)} %collective-permute-done.16.refs_16_.ahead_ref) | copy-start | bytes 1769476
  45.4 3.1 %collective-permute-start.15 = (bf16[2,256,256]{2,1,0:T(8,128)(2,1)S(1)}, bf16[2,256,256]{2,1,0:T(8,128)(2,1)S(1)}, u32[]{:S(2)}, u32[]{:S(2)}) collective-permute-start(bf16[2,256,256]{2,1,0:T(8,128)(2,1)S(1)} %collective-permute-done.13.refs_13_), channel_id=1, source_target_pairs={{0,16},{16,0},{32,48},{48,32},{64,80},{80,64},{96,112},{112,96},{1... | collective-permute-start | bytes 786440 | tf_op jit(solution)/shard_map/ppermute | solution.py:518
  45.9 2.8 %copy-start.23 = (bf16[2,256,256]{2,1,0:T(8,128)(2,1)}, bf16[2,256,256]{2,1,0:T(8,128)(2,1)S(1)}, u32[]{:S(2)}) copy-start(bf16[2,256,256]{2,1,0:T(8,128)(2,1)S(1)} %collective-permute-done.11.refs_11_) | copy-start | bytes 786436
  45.9 3.3 %collective-permute-start.9 = (bf16[2,256,256]{2,1,0:T(8,128)(2,1)S(1)}, bf16[2,256,256]{2,1,0:T(8,128)(2,1)S(1)}, u32[]{:S(2)}, u32[]{:S(2)}) collective-permute-start(bf16[2,256,256]{2,1,0:T(8,128)(2,1)S(1)} %collective-permute-done.6.refs_5_), channel_id=1, source_target_pairs={{0,16},{16,0},{32,48},{48,32},{64,80},{80,64},{96,112},{112,96},{1... | collective-permute-start | bytes 786440 | tf_op jit(solution)/shard_map/ppermute | solution.py:518
  48.6 11.8 %collective-permute-start.20 = (bf16[192,768]{1,0:T(8,128)(2,1)S(1)}, bf16[192,768]{1,0:T(8,128)(2,1)S(1)}, u32[]{:S(2)}, u32[]{:S(2)}) collective-permute-start(bf16[192,768]{1,0:T(8,128)(2,1)S(1)} %collective-permute-done.17.refs_17_.apart_ref), channel_id=1, source_target_pairs={{0,16},{16,0},{32,48},{48,32},{64,80},{80,64},{96,112},{112,96},{1... | collective-permute-start | bytes 884744 | tf_op jit(solution)/shard_map/ppermute | solution.py:518
  49.3 11.1 %collective-permute-start.19 = (bf16[384,768]{1,0:T(8,128)(2,1)S(1)}, bf16[384,768]{1,0:T(8,128)(2,1)S(1)}, u32[]{:S(2)}, u32[]{:S(2)}) collective-permute-start(bf16[384,768]{1,0:T(8,128)(2,1)S(1)} %collective-permute-done.16.refs_16_.ahead_ref), channel_id=1, source_target_pairs={{0,16},{16,0},{32,48},{48,32},{64,80},{80,64},{96,112},{112,96},{1... | collective-permute-start | bytes 1769480 | tf_op jit(solution)/shard_map/ppermute | solution.py:518
  50.6 9.8 %copy-start.1 = (bf16[384,3072]{1,0:T(8,128)(2,1)S(1)}, bf16[384,3072]{1,0:T(8,128)(2,1)}, u32[]{:S(2)}) copy-start(bf16[384,3072]{1,0:T(8,128)(2,1)} %w_out_ref.3) | copy-start | bytes 7077892
  50.6 9.8 %copy-start.10 = (s32[8]{0:T(128)S(1)}, s32[8]{0:T(128)}, u32[]{:S(2)}) copy-start(s32[8]{0:T(128)} %stack.68.place_ref) | copy-start | bytes 100
  58.8 9.2 %collective-permute-start.18 = (bf16[2,272,256]{2,1,0:T(8,128)(2,1)}, bf16[2,272,256]{2,1,0:T(8,128)(2,1)S(1)}, u32[]{:S(2)}, u32[]{:S(2)}) collective-permute-start(bf16[2,272,256]{2,1,0:T(8,128)(2,1)} %get-tuple-element.28), channel_id=1, source_target_pairs={{0,8},{8,0},{1,9},{9,1},{2,10},{10,2},{3,11},{11,3},{4,12},{12,4},... | collective-permute-start | bytes 835592 | tf_op jit(solution)/shard_map/ppermute | solution.py:518
  63.3 4.7 %copy-start.6 = (f32[2,256,256]{2,1,0:T(8,128)S(1)}, f32[2,256,256]{2,1,0:T(8,128)}, u32[]{:S(2)}) copy-start(f32[2,256,256]{2,1,0:T(8,128)} %get-tuple-element.27.mid_ref) | copy-start | bytes 1572868
  69.1 8.1 %collective-permute-start.25 = (bf16[256,384]{1,0:T(8,128)(2,1)S(1)}, bf16[256,384]{1,0:T(8,128)(2,1)S(1)}, u32[]{:S(2)}, u32[]{:S(2)}) collective-permute-start(bf16[256,384]{1,0:T(8,128)(2,1)S(1)} %get-tuple-element.32.refs_0_), channel_id=1, source_target_pairs={{0,1},{1,2},{2,3},{3,0},{4,5},{5,6},{6,7},{7,4},{16,19},{17,16},{1... | collective-permute-start | bytes 589832 | tf_op jit(solution)/shard_map/ppermute | solution.py:518
  71.1 27.7 %copy-start.12 = (f32[384]{0:T(512)S(1)}, f32[384]{0:T(512)}, u32[]{:S(2)}) copy-start(f32[384]{0:T(512)} %param.15) | copy-start | bytes 4612
  71.1 10.0 %collective-permute-start.21 = (bf16[256,384]{1,0:T(8,128)(2,1)S(1)}, bf16[256,384]{1,0:T(8,128)(2,1)S(1)}, u32[]{:S(2)}, u32[]{:S(2)}) collective-permute-start(bf16[256,384]{1,0:T(8,128)(2,1)S(1)} %get-tuple-element.29.refs_0_), channel_id=1, source_target_pairs={{0,1},{1,2},{2,3},{3,0},{4,5},{5,6},{6,7},{7,4},{16,19},{17,16},{1... | collective-permute-start | bytes 589832 | tf_op jit(solution)/shard_map/ppermute | solution.py:518
  73.0 9.0 %collective-permute-start.26 = (bf16[256,384]{1,0:T(8,128)(2,1)S(1)}, bf16[256,384]{1,0:T(8,128)(2,1)S(1)}, u32[]{:S(2)}, u32[]{:S(2)}) collective-permute-start(bf16[256,384]{1,0:T(8,128)(2,1)S(1)} %get-tuple-element.32.refs_0_), channel_id=1, source_target_pairs={{0,3},{1,0},{2,1},{3,2},{4,7},{5,4},{6,5},{7,6},{16,17},{17,18},{1... | collective-permute-start | bytes 589832 | tf_op jit(solution)/shard_map/ppermute | solution.py:518
  77.3 9.0 %collective-permute-start.27 = (bf16[256,384]{1,0:T(8,128)(2,1)S(1)}, bf16[256,384]{1,0:T(8,128)(2,1)S(1)}, u32[]{:S(2)}, u32[]{:S(2)}) collective-permute-start(bf16[256,384]{1,0:T(8,128)(2,1)S(1)} %collective-permute-done.25.refs_1_), channel_id=1, source_target_pairs={{0,1},{1,2},{2,3},{3,0},{4,5},{5,6},{6,7},{7,4},{16,19},{17,16},{1... | collective-permute-start | bytes 589832 | tf_op jit(solution)/shard_map/ppermute | solution.py:518
  77.9 12.6 %collective-permute-start.22 = (bf16[256,384]{1,0:T(8,128)(2,1)S(1)}, bf16[256,384]{1,0:T(8,128)(2,1)S(1)}, u32[]{:S(2)}, u32[]{:S(2)}) collective-permute-start(bf16[256,384]{1,0:T(8,128)(2,1)S(1)} %get-tuple-element.29.refs_0_), channel_id=1, source_target_pairs={{0,3},{1,0},{2,1},{3,2},{4,7},{5,4},{6,5},{7,6},{16,17},{17,18},{1... | collective-permute-start | bytes 589832 | tf_op jit(solution)/shard_map/ppermute | solution.py:518
  81.1 9.4 %collective-permute-start.23 = (bf16[256,384]{1,0:T(8,128)(2,1)S(1)}, bf16[256,384]{1,0:T(8,128)(2,1)S(1)}, u32[]{:S(2)}, u32[]{:S(2)}) collective-permute-start(bf16[256,384]{1,0:T(8,128)(2,1)S(1)} %collective-permute-done.21.refs_1_), channel_id=1, source_target_pairs={{0,1},{1,2},{2,3},{3,0},{4,5},{5,6},{6,7},{7,4},{16,19},{17,16},{1... | collective-permute-start | bytes 589832 | tf_op jit(solution)/shard_map/ppermute | solution.py:518
  87.4 8.5 %collective-permute-start.28 = (bf16[256,384]{1,0:T(8,128)(2,1)S(1)}, bf16[256,384]{1,0:T(8,128)(2,1)S(1)}, u32[]{:S(2)}, u32[]{:S(2)}) collective-permute-start(bf16[256,384]{1,0:T(8,128)(2,1)S(1)} %get-tuple-element.34), channel_id=1, source_target_pairs={{0,4},{1,5},{2,6},{3,7},{4,0},{5,1},{6,2},{7,3},{8,12},{9,13},{10,... | collective-permute-start | bytes 589832 | tf_op jit(solution)/shard_map/ppermute | solution.py:518
  91.6 7.3 %collective-permute-start.24 = (bf16[256,384]{1,0:T(8,128)(2,1)S(1)}, bf16[256,384]{1,0:T(8,128)(2,1)S(1)}, u32[]{:S(2)}, u32[]{:S(2)}) collective-permute-start(bf16[256,384]{1,0:T(8,128)(2,1)S(1)} %get-tuple-element.31), channel_id=1, source_target_pairs={{0,4},{1,5},{2,6},{3,7},{4,0},{5,1},{6,2},{7,3},{8,12},{9,13},{10,... | collective-permute-start | bytes 589832 | tf_op jit(solution)/shard_map/ppermute | solution.py:518
  (8 other events, 7.3 us)

commit v6 on v4

--- a/solution.py
+++ b/solution.py
@@ -469,13 +469,17 @@
 
 
 def output_kernel(*refs):
-    mixed, w_ref = refs[0:4], refs[4]
-    kept_ref, sent_ref, h_scr, h_sem = refs[5:9]
+    mixed, w_ref = refs[0:8], refs[8]
+    kept_ref, sent_ref, h_scr, h_sem = refs[9:13]
     cols = kept_ref.shape[1]
-    width = mixed[0].shape[1]
+    half, width = mixed[0].shape
     copies = [
-        pltpu.make_async_copy(mixed[k], h_scr.at[:, pl.ds(k * width, width)], h_sem.at[k])
-        for k in range(4)
+        pltpu.make_async_copy(
+            mixed[k],
+            h_scr.at[pl.ds(k // 4 * half, half), pl.ds(k % 4 * width, width)],
+            h_sem.at[k],
+        )
+        for k in range(8)
     ]
     for copy in copies:
         copy.start()
@@ -488,7 +492,7 @@
 
 
 def output(mixed, w_all):
-    rows, width = mixed[0].shape
+    rows, width = 2 * mixed[0].shape[0], mixed[0].shape[1]
     cols = w_all.shape[1] // 2
     return pl.pallas_call(
         output_kernel,
@@ -496,13 +500,13 @@
             jax.ShapeDtypeStruct((rows, cols), F32),
             jax.ShapeDtypeStruct((rows, cols), BF16),
         ],
-        in_specs=[ANY] * 4 + [VMEM],
+        in_specs=[ANY] * 8 + [VMEM],
         out_specs=[VMEM] * 2,
         scratch_shapes=[
             pltpu.VMEM((rows, 4 * width), BF16),
-            pltpu.SemaphoreType.DMA((4,)),
+            pltpu.SemaphoreType.DMA((8,)),
         ],
-        compiler_params=vmem(10),
+        compiler_params=vmem(14),
         cost_estimate=pl.CostEstimate(
             flops=16 * rows * width * cols, bytes_accessed=4_000_000, transcendentals=0
         ),
@@ -603,12 +607,13 @@
         meta, q_home, q_away, pieces, [w_ahead, w_apart], n_frames
     )
     w_parts = [w_ahead, swap_core(w_ahead), w_apart, swap_core(w_apart)]
-    totals = []
     w_all = assemble(place, w_out, w_parts, home)
+    gathered = []
     for mixed in combine(place, home, mid_sums, swap_half(back), w_all):
-        kept_part, sent_part = output(gather_z(mixed), w_all)
-        totals.append(kept_part + swap_x(sent_part).astype(F32))
-    return jnp.stack([(total * gate).astype(BF16) for total in totals])
+        gathered += gather_z(mixed)
+    kept_part, sent_part = output(gathered, w_all)
+    total = kept_part + swap_x(sent_part).astype(F32)
+    return (total * gate).astype(BF16).reshape(frames_dev, half_tok, -1)
 
 
 def solution(mesh):

time: 99.1 us -> 102 us (1.029); the launches traced: 98.6 us -> 100 us
  waiting for transfers between devices: 34.1 us -> 40.5 us
  starting transfers between devices: 35.4 us -> 31.2 us
    ppermute x29 -> x28, waiting for transfers between devices: 34.1 us -> 40.5 us  [move(): return lax.ppermute(x, axis, [(i, to(i)) for i in range(count)])]
    ppermute x29 -> x28, starting transfers between devices: 35.4 us -> 31.2 us  [move(): return lax.ppermute(x, axis, [(i, to(i)) for i in range(count)])]
    pallas_call x2 -> x1, Pallas kernels: 2.21 us -> 2.04 us  [output(): pl.pallas_call(output_kernel, out_shape=[jax.ShapeDtypeStruct((rows, cols...]
  transfers between devices with their start and end apart: 29 -> 28, of which waited for: 13 -> 14; matrix products, arithmetic and copies ran while one was open for 1% -> 1% of each run, Pallas kernels for 12% -> 9%
where the time goes in v6:
time: 102 us; the launch traced here: 100 us
  waiting for transfers between devices  40.5 us (40%)
  starting transfers between devices  31.2 us (31%)
  Pallas kernels  21.7 us (21%)
  local copies, waits for them, and re-layouts  5.42 us (5%)
    ppermute x28, waiting for transfers between devices, move(): return lax.ppermute(x, axis, [(i, to(i)) for i in range(count)])  40.5 us
    ppermute x28, starting transfers between devices, move(): return lax.ppermute(x, axis, [(i, to(i)) for i in range(count)])  31.2 us
    pallas_call x1, Pallas kernels, project(): pl.pallas_call(project_kernel, out_shape=[jax.ShapeDtypeStruct(shape, BF1...  9.91 us
    pallas_call x1, Pallas kernels, attend(): pl.pallas_call(attend_kernel, out_shape=[jax.ShapeDtypeStruct((frames * h...  7.63 us
    unnamed x54, local copies, waits for them, and re-layouts  4.19 us
  transfers between devices with their start and end apart: 28, of which 14 were waited for; matrix products, arithmetic and copies ran while one was open for 1% of the time, Pallas kernels for 9%

profile of v6, /device:TPU:0, one launch (start us, length us, event | category | flops | bytes accessed | tf_op | source)
XLA Modules:
  0.0 100.0 jit_solution(11911088762585923250)
XLA Ops:
  0.0 0.7 stack.59.place_ref
  0.7 9.9 %project.1 = (bf16[512,512]{1,0:T(8,128)(2,1)}, bf16[512,256]{1,0:T(8,128)(2,1)}, bf16[512,256]{1,0:T(8,128)(2,1)}, bf16[512,256]{1,0:T(8,128)(2,1)}, bf16[384,7...) custom-call(s32[8]{0:T(128)} %stack.59.place_ref, bf16[512,3072]{1,0:T(8,128)(2,1)} %bitcast.29, bf16[3,3072,384]{2,1,0:T(8,128)(2,1)} %bitcast.28, ...), custom_call_target="tpu_custom_call" | custom-call | flops 3623878656 | bytes 12000000 | tf_op jit(solution)/shard_map/project/pallas_call | solution.py:144
  10.6 1.7 %collective-permute-start.4 = (bf16[2,256,512]{2,1,0:T(8,128)(2,1)}, bf16[2,256,512]{2,1,0:T(8,128)(2,1)S(1)}, u32[]{:S(2)}, u32[]{:S(2)}) collective-permute-start(bf16[2,256,512]{2,1,0:T(8,128)(2,1)} %bitcast.30), channel_id=1, source_target_pairs={{0,32},{16,112},{32,64},{48,16},{64,96},{80,48},{96,0},{112,80},{1... | collective-permute-start | bytes 1572872 | tf_op jit(solution)/shard_map/ppermute | solution.py:522
  12.3 1.6 %collective-permute-start.5 = (bf16[2,256,512]{2,1,0:T(8,128)(2,1)}, bf16[2,256,512]{2,1,0:T(8,128)(2,1)S(1)}, u32[]{:S(2)}, u32[]{:S(2)}) collective-permute-start(bf16[2,256,512]{2,1,0:T(8,128)(2,1)} %bitcast.31), channel_id=1, source_target_pairs={{0,96},{16,48},{32,0},{48,80},{64,32},{80,112},{96,64},{112,16},{1... | collective-permute-start | bytes 1572872 | tf_op jit(solution)/shard_map/ppermute | solution.py:522
  13.9 1.6 %collective-permute-start.1 = (bf16[2,256,256]{2,1,0:T(8,128)(2,1)}, bf16[2,256,256]{2,1,0:T(8,128)(2,1)S(1)}, u32[]{:S(2)}, u32[]{:S(2)}) collective-permute-start(bf16[2,256,256]{2,1,0:T(8,128)(2,1)} %bitcast.35), channel_id=1, source_target_pairs={{0,8},{8,0},{1,9},{9,1},{2,10},{10,2},{3,11},{11,3},{4,12},{12,4},... | collective-permute-start | bytes 786440 | tf_op jit(solution)/shard_map/ppermute | solution.py:522
  15.5 0.5 collective-permute-start
  15.9 4.0 %collective-permute-start.17 = (bf16[192,768]{1,0:T(8,128)(2,1)}, bf16[192,768]{1,0:T(8,128)(2,1)S(1)}, u32[]{:S(2)}, u32[]{:S(2)}) collective-permute-start(bf16[192,768]{1,0:T(8,128)(2,1)} %get-tuple-element.23), channel_id=1, source_target_pairs={{0,2},{1,3},{2,0},{3,1},{4,6},{5,7},{6,4},{7,5},{8,10},{9,11},{10,... | collective-permute-start | bytes 884744 | tf_op jit(solution)/shard_map/ppermute | solution.py:522
  20.0 0.2 copy.13
  20.5 2.9 %collective-permute-done.1.refs_1_ = bf16[2,256,256]{2,1,0:T(8,128)(2,1)S(1)} collective-permute-done((bf16[2,256,256]{2,1,0:T(8,128)(2,1)}, bf16[2,256,256]{2,1,0:T(8,128)(2,1)S(1)}, u32[]{:S(2)}, u32[]{:S(2)}) %collective-permute-start.1) | collective-permute-done | bytes 262176 | tf_op jit(solution)/shard_map/ppermute | solution.py:522
  23.4 1.7 %collective-permute-start.7 = (bf16[2,256,256]{2,1,0:T(8,128)(2,1)S(1)}, bf16[2,256,256]{2,1,0:T(8,128)(2,1)S(1)}, u32[]{:S(2)}, u32[]{:S(2)}) collective-permute-start(bf16[2,256,256]{2,1,0:T(8,128)(2,1)S(1)} %collective-permute-done.1.refs_1_), channel_id=1, source_target_pairs={{0,96},{16,48},{32,0},{48,80},{64,32},{80,112},{96,64},{112,16},{1... | collective-permute-start | bytes 786440 | tf_op jit(solution)/shard_map/ppermute | solution.py:522
  25.1 3.8 %collective-permute-start.13 = (bf16[2,256,256]{2,1,0:T(8,128)(2,1)S(1)}, bf16[2,256,256]{2,1,0:T(8,128)(2,1)S(1)}, u32[]{:S(2)}, u32[]{:S(2)}) collective-permute-start(bf16[2,256,256]{2,1,0:T(8,128)(2,1)S(1)} %collective-permute-done.1.refs_1_), channel_id=1, source_target_pairs={{0,64},{16,80},{32,96},{48,112},{64,0},{80,16},{96,32},{112,48},{1... | collective-permute-start | bytes 786440 | tf_op jit(solution)/shard_map/ppermute | solution.py:522
  29.0 0.7 collective-permute-start.12
  29.8 1.9 %collective-permute-start.16 = (bf16[384,768]{1,0:T(8,128)(2,1)}, bf16[384,768]{1,0:T(8,128)(2,1)S(1)}, u32[]{:S(2)}, u32[]{:S(2)}) collective-permute-start(bf16[384,768]{1,0:T(8,128)(2,1)} %get-tuple-element.22), channel_id=1, source_target_pairs={{0,1},{1,2},{2,3},{3,0},{4,5},{5,6},{6,7},{7,4},{16,19},{17,16},{1... | collective-permute-start | bytes 1769480 | tf_op jit(solution)/shard_map/ppermute | solution.py:522
  31.7 0.6 collective-permute-start.6
  32.3 3.7 %collective-permute-done.13.refs_13_ = bf16[2,256,256]{2,1,0:T(8,128)(2,1)S(1)} collective-permute-done((bf16[2,256,256]{2,1,0:T(8,128)(2,1)S(1)}, bf16[2,256,256]{2,1,0:T(8,128)(2,1)S(1)}, u32[]{:S(2)}, u32[]{:S(2)}) %collective-permute-start.13) | collective-permute-done | bytes 262176 | tf_op jit(solution)/shard_map/ppermute | solution.py:522
  36.1 8.3 %collective-permute-done.6.refs_5_ = bf16[2,256,256]{2,1,0:T(8,128)(2,1)S(1)} collective-permute-done((bf16[2,256,256]{2,1,0:T(8,128)(2,1)S(1)}, bf16[2,256,256]{2,1,0:T(8,128)(2,1)S(1)}, u32[]{:S(2)}, u32[]{:S(2)}) %collective-permute-start.6) | collective-permute-done | bytes 262176 | tf_op jit(solution)/shard_map/ppermute | solution.py:522
  44.4 0.5 collective-permute-start.8
  45.0 0.4 collective-permute-start.14
  45.4 0.3 collective-permute-start.15
  45.7 0.2 collective-permute-done.11.refs_11_
  46.1 2.5 %collective-permute-done.15.refs_15_ = bf16[2,256,256]{2,1,0:T(8,128)(2,1)S(1)} collective-permute-done((bf16[2,256,256]{2,1,0:T(8,128)(2,1)S(1)}, bf16[2,256,256]{2,1,0:T(8,128)(2,1)S(1)}, u32[]{:S(2)}, u32[]{:S(2)}) %collective-permute-start.15) | collective-permute-done | bytes 262176 | tf_op jit(solution)/shard_map/ppermute | solution.py:522
  48.7 0.2 collective-permute-done.9.refs_9_
  48.9 0.2 collective-permute-start.19
  49.3 0.4 copy-done.25
  49.6 0.4 copy-done.15
  50.4 7.6 %attend.1 = (bf16[512,128]{1,0:T(8,128)(2,1)}, f32[2,256,256]{2,1,0:T(8,128)}, bf16[2,272,256]{2,1,0:T(8,128)(2,1)}) custom-call(s32[76]{0:T(128)} %copy-done.11, bf16[2,256,256]{2,1,0:T(8,128)(2,1)} %bitcast.40, bf16[2,256,256]{2,1,0:T(8,128)(2,1)} %copy-done.19, bf16[2,256,512]{2,1,0:T(8,128)(2,1)} %bitcast.33, bf16[2,256,256]{2,1,0:T(8,128)(2,1)} %copy-done.18, ...), custom_call_target="tpu_custom_call" | custom-call | flops 8999999488 | bytes 8000000 | tf_op jit(solution)/shard_map/attend/pallas_call | solution.py:328
  58.0 1.6 %collective-permute-start.18 = (bf16[2,272,256]{2,1,0:T(8,128)(2,1)}, bf16[2,272,256]{2,1,0:T(8,128)(2,1)S(1)}, u32[]{:S(2)}, u32[]{:S(2)}) collective-permute-start(bf16[2,272,256]{2,1,0:T(8,128)(2,1)} %get-tuple-element.26), channel_id=1, source_target_pairs={{0,8},{8,0},{1,9},{9,1},{2,10},{10,2},{3,11},{11,3},{4,12},{12,4},... | collective-permute-start | bytes 835592 | tf_op jit(solution)/shard_map/ppermute | solution.py:522
  59.6 1.1 %copy-done.3 = bf16[384,768]{1,0:T(8,128)(2,1)S(1)} copy-done((bf16[384,768]{1,0:T(8,128)(2,1)S(1)}, bf16[384,768]{1,0:T(8,128)(2,1)}, u32[]{:S(2)}) %copy-start.3) | copy-done | bytes 589848
  60.7 0.9 copy-done.7
  61.6 1.0 copy-done.9
  62.6 1.1 %assemble.1._.refs_8_ = bf16[1536,768]{1,0:T(8,128)(2,1)S(1)} custom-call(s32[8]{0:T(128)S(1)} %copy-done.10, bf16[384,3072]{1,0:T(8,128)(2,1)S(1)} %copy-done.1, bf16[384,768]{1,0:T(8,128)(2,1)S(1)} %copy-done.3, bf16[384,768]{1,0:T(8,128)(2,1)S(1)} %collective-permute-done.19.behind_ref, bf16[192,768]{1,0:T(8,128)(2,1)S(1)} %copy-done.9, ...), custom_call_target="tpu_custom_call" | custom-call | bytes 4000000 | tf_op jit(solution)/shard_map/assemble/pallas_call | solution.py:459
  63.6 2.0 %collective-permute-done.18.got_ref = bf16[2,272,256]{2,1,0:T(8,128)(2,1)S(1)} collective-permute-done((bf16[2,272,256]{2,1,0:T(8,128)(2,1)}, bf16[2,272,256]{2,1,0:T(8,128)(2,1)S(1)}, u32[]{:S(2)}, u32[]{:S(2)}) %collective-permute-start.18) | collective-permute-done | bytes 278560 | tf_op jit(solution)/shard_map/ppermute | solution.py:522
  65.6 1.1 %combine.1 = (bf16[256,384]{1,0:T(8,128)(2,1)S(1)}, bf16[256,384]{1,0:T(8,128)(2,1)S(1)}) custom-call(s32[8]{0:T(128)S(1)} %copy-done.10, bf16[512,128]{1,0:T(8,128)(2,1)S(1)} %copy-done.7, f32[2,256,256]{2,1,0:T(8,128)S(1)} %copy-done.6, bf16[2,272,256]{2,1,0:T(8,128)(2,1)S(1)} %collective-permute-done.18.got_ref, bf16[1536,768]{1,0:T(8,128)(2,1)S(1)} %assemble.1._.refs_8_), custom_call_target="tpu_custom_call" | custom-call | flops 50000000 | bytes 1500000 | tf_op jit(solution)/shard_map/combine/pallas_call | solution.py:391
  66.7 2.0 %collective-permute-start.21 = (bf16[256,384]{1,0:T(8,128)(2,1)S(1)}, bf16[256,384]{1,0:T(8,128)(2,1)S(1)}, u32[]{:S(2)}, u32[]{:S(2)}) collective-permute-start(bf16[256,384]{1,0:T(8,128)(2,1)S(1)} %get-tuple-element.27.refs_0_), channel_id=1, source_target_pairs={{0,1},{1,2},{2,3},{3,0},{4,5},{5,6},{6,7},{7,4},{16,19},{17,16},{1... | collective-permute-start | bytes 589832 | tf_op jit(solution)/shard_map/ppermute | solution.py:522
  68.7 1.9 %collective-permute-start.24 = (bf16[256,384]{1,0:T(8,128)(2,1)S(1)}, bf16[256,384]{1,0:T(8,128)(2,1)S(1)}, u32[]{:S(2)}, u32[]{:S(2)}) collective-permute-start(bf16[256,384]{1,0:T(8,128)(2,1)S(1)} %get-tuple-element.28.refs_4_), channel_id=1, source_target_pairs={{0,1},{1,2},{2,3},{3,0},{4,5},{5,6},{6,7},{7,4},{16,19},{17,16},{1... | collective-permute-start | bytes 589832 | tf_op jit(solution)/shard_map/ppermute | solution.py:522
  70.6 1.3 %collective-permute-start.22 = (bf16[256,384]{1,0:T(8,128)(2,1)S(1)}, bf16[256,384]{1,0:T(8,128)(2,1)S(1)}, u32[]{:S(2)}, u32[]{:S(2)}) collective-permute-start(bf16[256,384]{1,0:T(8,128)(2,1)S(1)} %get-tuple-element.27.refs_0_), channel_id=1, source_target_pairs={{0,3},{1,0},{2,1},{3,2},{4,7},{5,4},{6,5},{7,6},{16,17},{17,18},{1... | collective-permute-start | bytes 589832 | tf_op jit(solution)/shard_map/ppermute | solution.py:522
  71.9 1.0 %collective-permute-start.25 = (bf16[256,384]{1,0:T(8,128)(2,1)S(1)}, bf16[256,384]{1,0:T(8,128)(2,1)S(1)}, u32[]{:S(2)}, u32[]{:S(2)}) collective-permute-start(bf16[256,384]{1,0:T(8,128)(2,1)S(1)} %get-tuple-element.28.refs_4_), channel_id=1, source_target_pairs={{0,3},{1,0},{2,1},{3,2},{4,7},{5,4},{6,5},{7,6},{16,17},{17,18},{1... | collective-permute-start | bytes 589832 | tf_op jit(solution)/shard_map/ppermute | solution.py:522
  72.9 1.5 %collective-permute-done.21.refs_1_ = bf16[256,384]{1,0:T(8,128)(2,1)S(1)} collective-permute-done((bf16[256,384]{1,0:T(8,128)(2,1)S(1)}, bf16[256,384]{1,0:T(8,128)(2,1)S(1)}, u32[]{:S(2)}, u32[]{:S(2)}) %collective-permute-start.21) | collective-permute-done | bytes 196640 | tf_op jit(solution)/shard_map/ppermute | solution.py:522
  74.5 2.1 %collective-permute-done.24.refs_5_ = bf16[256,384]{1,0:T(8,128)(2,1)S(1)} collective-permute-done((bf16[256,384]{1,0:T(8,128)(2,1)S(1)}, bf16[256,384]{1,0:T(8,128)(2,1)S(1)}, u32[]{:S(2)}, u32[]{:S(2)}) %collective-permute-start.24) | collective-permute-done | bytes 196640 | tf_op jit(solution)/shard_map/ppermute | solution.py:522
  76.6 0.4 collective-permute-start.26
  77.0 0.4 collective-permute-done.22.refs_2_
  77.3 4.1 %collective-permute-done.25.refs_6_ = bf16[256,384]{1,0:T(8,128)(2,1)S(1)} collective-permute-done((bf16[256,384]{1,0:T(8,128)(2,1)S(1)}, bf16[256,384]{1,0:T(8,128)(2,1)S(1)}, u32[]{:S(2)}, u32[]{:S(2)}) %collective-permute-start.25) | collective-permute-done | bytes 196640 | tf_op jit(solution)/shard_map/ppermute | solution.py:522
  81.4 1.5 %collective-permute-done.23.refs_3_ = bf16[256,384]{1,0:T(8,128)(2,1)S(1)} collective-permute-done((bf16[256,384]{1,0:T(8,128)(2,1)S(1)}, bf16[256,384]{1,0:T(8,128)(2,1)S(1)}, u32[]{:S(2)}, u32[]{:S(2)}) %collective-permute-start.23) | collective-permute-done | bytes 196640 | tf_op jit(solution)/shard_map/ppermute | solution.py:522
  82.9 2.2 %collective-permute-done.26.refs_7_ = bf16[256,384]{1,0:T(8,128)(2,1)S(1)} collective-permute-done((bf16[256,384]{1,0:T(8,128)(2,1)S(1)}, bf16[256,384]{1,0:T(8,128)(2,1)S(1)}, u32[]{:S(2)}, u32[]{:S(2)}) %collective-permute-start.26) | collective-permute-done | bytes 196640 | tf_op jit(solution)/shard_map/ppermute | solution.py:522
  85.1 2.0 %output.1 = (f32[512,384]{1,0:T(8,128)S(1)}, bf16[512,384]{1,0:T(8,128)(2,1)S(1)}) custom-call(bf16[256,384]{1,0:T(8,128)(2,1)S(1)} %get-tuple-element.27.refs_0_, bf16[256,384]{1,0:T(8,128)(2,1)S(1)} %collective-permute-done.21.refs_1_, bf16[256,384]{1,0:T(8,128)(2,1)S(1)} %collective-permute-done.22.refs_2_, ...), custom_call_target="tpu_custom_call" | custom-call | flops 1207959552 | bytes 4000000 | tf_op jit(solution)/shard_map/output/pallas_call | solution.py:497
  87.1 3.1 %collective-permute-start.27 = (bf16[512,384]{1,0:T(8,128)(2,1)S(1)}, bf16[512,384]{1,0:T(8,128)(2,1)S(1)}, u32[]{:S(2)}, u32[]{:S(2)}) collective-permute-start(bf16[512,384]{1,0:T(8,128)(2,1)S(1)} %get-tuple-element.30), channel_id=1, source_target_pairs={{0,4},{1,5},{2,6},{3,7},{4,0},{5,1},{6,2},{7,3},{8,12},{9,13},{10,... | collective-permute-start | bytes 1179656 | tf_op jit(solution)/shard_map/ppermute | solution.py:522
  90.2 8.9 %collective-permute-done.27 = bf16[512,384]{1,0:T(8,128)(2,1)S(1)} collective-permute-done((bf16[512,384]{1,0:T(8,128)(2,1)S(1)}, bf16[512,384]{1,0:T(8,128)(2,1)S(1)}, u32[]{:S(2)}, u32[]{:S(2)}) %collective-permute-start.27) | collective-permute-done | bytes 393248 | tf_op jit(solution)/shard_map/ppermute | solution.py:522
  99.1 0.8 multiply_convert_fusion
  (75 shorter events, 1.4 us)
Async XLA Ops:
  0.0 19.9 %copy-start = (s32[16,4,4,2]{0,3,2,1:T(2,128)S(1)}, s32[16,4,4,2]{0,3,2,1:T(2,128)}, u32[]{:S(2)}) copy-start(s32[16,4,4,2]{0,3,2,1:T(2,128)} %param.19) | copy-start | bytes 6148
  0.7 19.6 %copy-start.26 = (s32[16]{0:T(128)S(1)}, s32[16]{0:T(128)}, u32[]{:S(2)}) copy-start(s32[16]{0:T(128)} %param.18) | copy-start | bytes 196
  10.6 14.5 %collective-permute-start.4 = (bf16[2,256,512]{2,1,0:T(8,128)(2,1)}, bf16[2,256,512]{2,1,0:T(8,128)(2,1)S(1)}, u32[]{:S(2)}, u32[]{:S(2)}) collective-permute-start(bf16[2,256,512]{2,1,0:T(8,128)(2,1)} %bitcast.30), channel_id=1, source_target_pairs={{0,32},{16,112},{32,64},{48,16},{64,96},{80,48},{96,0},{112,80},{1... | collective-permute-start | bytes 1572872 | tf_op jit(solution)/shard_map/ppermute | solution.py:522
  12.3 16.6 %collective-permute-start.5 = (bf16[2,256,512]{2,1,0:T(8,128)(2,1)}, bf16[2,256,512]{2,1,0:T(8,128)(2,1)S(1)}, u32[]{:S(2)}, u32[]{:S(2)}) collective-permute-start(bf16[2,256,512]{2,1,0:T(8,128)(2,1)} %bitcast.31), channel_id=1, source_target_pairs={{0,96},{16,48},{32,0},{48,80},{64,32},{80,112},{96,64},{112,16},{1... | collective-permute-start | bytes 1572872 | tf_op jit(solution)/shard_map/ppermute | solution.py:522
  13.9 9.5 %collective-permute-start.1 = (bf16[2,256,256]{2,1,0:T(8,128)(2,1)}, bf16[2,256,256]{2,1,0:T(8,128)(2,1)S(1)}, u32[]{:S(2)}, u32[]{:S(2)}) collective-permute-start(bf16[2,256,256]{2,1,0:T(8,128)(2,1)} %bitcast.35), channel_id=1, source_target_pairs={{0,8},{8,0},{1,9},{9,1},{2,10},{10,2},{3,11},{11,3},{4,12},{12,4},... | collective-permute-start | bytes 786440 | tf_op jit(solution)/shard_map/ppermute | solution.py:522
  15.5 13.5 %collective-permute-start = (bf16[2,256,256]{2,1,0:T(8,128)(2,1)}, bf16[2,256,256]{2,1,0:T(8,128)(2,1)S(1)}, u32[]{:S(2)}, u32[]{:S(2)}) collective-permute-start(bf16[2,256,256]{2,1,0:T(8,128)(2,1)} %bitcast.34), channel_id=1, source_target_pairs={{0,8},{8,0},{1,9},{9,1},{2,10},{10,2},{3,11},{11,3},{4,12},{12,4},... | collective-permute-start | bytes 786440 | tf_op jit(solution)/shard_map/ppermute | solution.py:522
  15.9 13.8 %collective-permute-start.17 = (bf16[192,768]{1,0:T(8,128)(2,1)}, bf16[192,768]{1,0:T(8,128)(2,1)S(1)}, u32[]{:S(2)}, u32[]{:S(2)}) collective-permute-start(bf16[192,768]{1,0:T(8,128)(2,1)} %get-tuple-element.23), channel_id=1, source_target_pairs={{0,2},{1,3},{2,0},{3,1},{4,6},{5,7},{6,4},{7,5},{8,10},{9,11},{10,... | collective-permute-start | bytes 884744 | tf_op jit(solution)/shard_map/ppermute | solution.py:522
  20.5 29.9 %copy-start.11 = (s32[76]{0:T(128)}, s32[76]{0:T(128)S(1)}, u32[]{:S(2)}) copy-start(s32[76]{0:T(128)S(1)} %concatenate.3.refs_2_.meta_ref) | copy-start | bytes 916
  23.4 22.7 %copy-start.18 = (bf16[2,256,256]{2,1,0:T(8,128)(2,1)}, bf16[2,256,256]{2,1,0:T(8,128)(2,1)S(1)}, u32[]{:S(2)}) copy-start(bf16[2,256,256]{2,1,0:T(8,128)(2,1)S(1)} %collective-permute-done.1.refs_1_) | copy-start | bytes 786436
  23.4 8.3 %collective-permute-start.7 = (bf16[2,256,256]{2,1,0:T(8,128)(2,1)S(1)}, bf16[2,256,256]{2,1,0:T(8,128)(2,1)S(1)}, u32[]{:S(2)}, u32[]{:S(2)}) collective-permute-start(bf16[2,256,256]{2,1,0:T(8,128)(2,1)S(1)} %collective-permute-done.1.refs_1_), channel_id=1, source_target_pairs={{0,96},{16,48},{32,0},{48,80},{64,32},{80,112},{96,64},{112,16},{1... | collective-permute-start | bytes 786440 | tf_op jit(solution)/shard_map/ppermute | solution.py:522
  25.1 10.9 %collective-permute-start.13 = (bf16[2,256,256]{2,1,0:T(8,128)(2,1)S(1)}, bf16[2,256,256]{2,1,0:T(8,128)(2,1)S(1)}, u32[]{:S(2)}, u32[]{:S(2)}) collective-permute-start(bf16[2,256,256]{2,1,0:T(8,128)(2,1)S(1)} %collective-permute-done.1.refs_1_), channel_id=1, source_target_pairs={{0,64},{16,80},{32,96},{48,112},{64,0},{80,16},{96,32},{112,48},{1... | collective-permute-start | bytes 786440 | tf_op jit(solution)/shard_map/ppermute | solution.py:522
  28.9 21.4 %copy-start.4 = (bf16[2,256,512]{2,1,0:T(8,128)(2,1)}, bf16[2,256,512]{2,1,0:T(8,128)(2,1)S(1)}, u32[]{:S(2)}) copy-start(bf16[2,256,512]{2,1,0:T(8,128)(2,1)S(1)} %collective-permute-done.5.refs_1_.refs_6_) | copy-start | bytes 1572868
  28.9 16.0 %collective-permute-start.2 = (bf16[2,256,512]{2,1,0:T(8,128)(2,1)}, bf16[2,256,512]{2,1,0:T(8,128)(2,1)S(1)}, u32[]{:S(2)}, u32[]{:S(2)}) collective-permute-start(bf16[2,256,512]{2,1,0:T(8,128)(2,1)} %bitcast.32), channel_id=1, source_target_pairs={{0,16},{16,0},{32,48},{48,32},{64,80},{80,64},{96,112},{112,96},{1... | collective-permute-start | bytes 1572872 | tf_op jit(solution)/shard_map/ppermute | solution.py:522
  29.0 21.4 %copy-start.5 = (bf16[2,256,512]{2,1,0:T(8,128)(2,1)}, bf16[2,256,512]{2,1,0:T(8,128)(2,1)S(1)}, u32[]{:S(2)}) copy-start(bf16[2,256,512]{2,1,0:T(8,128)(2,1)S(1)} %after.1.refs_4_) | copy-start | bytes 1572868
  29.0 16.0 %collective-permute-start.12 = (bf16[2,256,512]{2,1,0:T(8,128)(2,1)S(1)}, bf16[2,256,512]{2,1,0:T(8,128)(2,1)S(1)}, u32[]{:S(2)}, u32[]{:S(2)}) collective-permute-start(bf16[2,256,512]{2,1,0:T(8,128)(2,1)S(1)} %after.1.refs_4_), channel_id=1, source_target_pairs={{0,32},{16,112},{32,64},{48,16},{64,96},{80,48},{96,0},{112,80},{1... | collective-permute-start | bytes 1572872 | tf_op jit(solution)/shard_map/ppermute | solution.py:522
  29.8 20.6 %copy-start.8 = (bf16[192,768]{1,0:T(8,128)(2,1)}, bf16[192,768]{1,0:T(8,128)(2,1)S(1)}, u32[]{:S(2)}) copy-start(bf16[192,768]{1,0:T(8,128)(2,1)S(1)} %collective-permute-done.17.refs_17_.apart_ref) | copy-start | bytes 884740
  29.8 15.7 %collective-permute-start.16 = (bf16[384,768]{1,0:T(8,128)(2,1)}, bf16[384,768]{1,0:T(8,128)(2,1)S(1)}, u32[]{:S(2)}, u32[]{:S(2)}) collective-permute-start(bf16[384,768]{1,0:T(8,128)(2,1)} %get-tuple-element.22), channel_id=1, source_target_pairs={{0,1},{1,2},{2,3},{3,0},{4,5},{5,6},{6,7},{7,4},{16,19},{17,16},{1... | collective-permute-start | bytes 1769480 | tf_op jit(solution)/shard_map/ppermute | solution.py:522
  31.7 18.7 %copy-start.20 = (bf16[2,256,256]{2,1,0:T(8,128)(2,1)}, bf16[2,256,256]{2,1,0:T(8,128)(2,1)S(1)}, u32[]{:S(2)}) copy-start(bf16[2,256,256]{2,1,0:T(8,128)(2,1)S(1)} %collective-permute-done.7.refs_7_) | copy-start | bytes 786436
  31.7 12.7 %collective-permute-start.6 = (bf16[2,256,256]{2,1,0:T(8,128)(2,1)S(1)}, bf16[2,256,256]{2,1,0:T(8,128)(2,1)S(1)}, u32[]{:S(2)}, u32[]{:S(2)}) collective-permute-start(bf16[2,256,256]{2,1,0:T(8,128)(2,1)S(1)} %collective-permute-done.1.refs_1_), channel_id=1, source_target_pairs={{0,32},{16,112},{32,64},{48,16},{64,96},{80,48},{96,0},{112,80},{1... | collective-permute-start | bytes 786440 | tf_op jit(solution)/shard_map/ppermute | solution.py:522
  36.1 12.6 %copy-start.21 = (bf16[2,256,256]{2,1,0:T(8,128)(2,1)}, bf16[2,256,256]{2,1,0:T(8,128)(2,1)S(1)}, u32[]{:S(2)}) copy-start(bf16[2,256,256]{2,1,0:T(8,128)(2,1)S(1)} %collective-permute-done.13.refs_13_) | copy-start | bytes 786436
  36.1 8.3 %collective-permute-start.3 = (bf16[2,256,256]{2,1,0:T(8,128)(2,1)S(1)}, bf16[2,256,256]{2,1,0:T(8,128)(2,1)}, u32[]{:S(2)}, u32[]{:S(2)}) collective-permute-start(bf16[2,256,256]{2,1,0:T(8,128)(2,1)S(1)} %collective-permute-done.1.refs_1_), channel_id=1, source_target_pairs={{0,16},{16,0},{32,48},{48,32},{64,80},{80,64},{96,112},{112,96},{1... | collective-permute-start | bytes 786440 | tf_op jit(solution)/shard_map/ppermute | solution.py:522
  44.4 4.3 %copy-start.22 = (bf16[2,256,256]{2,1,0:T(8,128)(2,1)}, bf16[2,256,256]{2,1,0:T(8,128)(2,1)S(1)}, u32[]{:S(2)}) copy-start(bf16[2,256,256]{2,1,0:T(8,128)(2,1)S(1)} %collective-permute-done.6.refs_5_) | copy-start | bytes 786436
  44.4 1.5 %collective-permute-start.11 = (bf16[2,256,256]{2,1,0:T(8,128)(2,1)S(1)}, bf16[2,256,256]{2,1,0:T(8,128)(2,1)S(1)}, u32[]{:S(2)}, u32[]{:S(2)}) collective-permute-start(bf16[2,256,256]{2,1,0:T(8,128)(2,1)S(1)} %collective-permute-done.7.refs_7_), channel_id=1, source_target_pairs={{0,16},{16,0},{32,48},{48,32},{64,80},{80,64},{96,112},{112,96},{1... | collective-permute-start | bytes 786440 | tf_op jit(solution)/shard_map/ppermute | solution.py:522
  44.4 4.8 %collective-permute-start.8 = (bf16[2,256,512]{2,1,0:T(8,128)(2,1)S(1)}, bf16[2,256,512]{2,1,0:T(8,128)(2,1)S(1)}, u32[]{:S(2)}, u32[]{:S(2)}) collective-permute-start(bf16[2,256,512]{2,1,0:T(8,128)(2,1)S(1)} %after.1.refs_4_), channel_id=1, source_target_pairs={{0,16},{16,0},{32,48},{48,32},{64,80},{80,64},{96,112},{112,96},{1... | collective-permute-start | bytes 1572872 | tf_op jit(solution)/shard_map/ppermute | solution.py:522
  44.9 5.5 %copy-start.13 = (bf16[2,256,512]{2,1,0:T(8,128)(2,1)}, bf16[2,256,512]{2,1,0:T(8,128)(2,1)S(1)}, u32[]{:S(2)}) copy-start(bf16[2,256,512]{2,1,0:T(8,128)(2,1)S(1)} %collective-permute-done.2.refs_2_) | copy-start | bytes 1572868
  44.9 4.3 %collective-permute-start.10 = (bf16[2,256,512]{2,1,0:T(8,128)(2,1)S(1)}, bf16[2,256,512]{2,1,0:T(8,128)(2,1)S(1)}, u32[]{:S(2)}, u32[]{:S(2)}) collective-permute-start(bf16[2,256,512]{2,1,0:T(8,128)(2,1)S(1)} %collective-permute-done.5.refs_1_.refs_6_), channel_id=1, source_target_pairs={{0,16},{16,0},{32,48},{48,32},{64,80},{80,64},{96,112},{112,96},{1... | collective-permute-start | bytes 1572872 | tf_op jit(solution)/shard_map/ppermute | solution.py:522
  45.0 4.2 %copy-start.14 = (bf16[2,256,512]{2,1,0:T(8,128)(2,1)}, bf16[2,256,512]{2,1,0:T(8,128)(2,1)S(1)}, u32[]{:S(2)}) copy-start(bf16[2,256,512]{2,1,0:T(8,128)(2,1)S(1)} %collective-permute-done.12.refs_12_) | copy-start | bytes 1572868
  45.0 4.2 %collective-permute-start.14 = (bf16[2,256,512]{2,1,0:T(8,128)(2,1)S(1)}, bf16[2,256,512]{2,1,0:T(8,128)(2,1)S(1)}, u32[]{:S(2)}, u32[]{:S(2)}) collective-permute-start(bf16[2,256,512]{2,1,0:T(8,128)(2,1)S(1)} %collective-permute-done.12.refs_12_), channel_id=1, source_target_pairs={{0,16},{16,0},{32,48},{48,32},{64,80},{80,64},{96,112},{112,96},{1... | collective-permute-start | bytes 1572872 | tf_op jit(solution)/shard_map/ppermute | solution.py:522
  45.4 4.9 %copy-start.2 = (bf16[384,768]{1,0:T(8,128)(2,1)}, bf16[384,768]{1,0:T(8,128)(2,1)S(1)}, u32[]{:S(2)}) copy-start(bf16[384,768]{1,0:T(8,128)(2,1)S(1)} %collective-permute-done.16.refs_16_.ahead_ref) | copy-start | bytes 1769476
  45.4 3.1 %collective-permute-start.15 = (bf16[2,256,256]{2,1,0:T(8,128)(2,1)S(1)}, bf16[2,256,256]{2,1,0:T(8,128)(2,1)S(1)}, u32[]{:S(2)}, u32[]{:S(2)}) collective-permute-start(bf16[2,256,256]{2,1,0:T(8,128)(2,1)S(1)} %collective-permute-done.13.refs_13_), channel_id=1, source_target_pairs={{0,16},{16,0},{32,48},{48,32},{64,80},{80,64},{96,112},{112,96},{1... | collective-permute-start | bytes 786440 | tf_op jit(solution)/shard_map/ppermute | solution.py:522
  45.9 3.3 %copy-start.23 = (bf16[2,256,256]{2,1,0:T(8,128)(2,1)}, bf16[2,256,256]{2,1,0:T(8,128)(2,1)S(1)}, u32[]{:S(2)}) copy-start(bf16[2,256,256]{2,1,0:T(8,128)(2,1)S(1)} %collective-permute-done.11.refs_11_) | copy-start | bytes 786436
  45.9 3.0 %collective-permute-start.9 = (bf16[2,256,256]{2,1,0:T(8,128)(2,1)S(1)}, bf16[2,256,256]{2,1,0:T(8,128)(2,1)S(1)}, u32[]{:S(2)}, u32[]{:S(2)}) collective-permute-start(bf16[2,256,256]{2,1,0:T(8,128)(2,1)S(1)} %collective-permute-done.6.refs_5_), channel_id=1, source_target_pairs={{0,16},{16,0},{32,48},{48,32},{64,80},{80,64},{96,112},{112,96},{1... | collective-permute-start | bytes 786440 | tf_op jit(solution)/shard_map/ppermute | solution.py:522
  48.5 11.1 %collective-permute-start.20 = (bf16[192,768]{1,0:T(8,128)(2,1)S(1)}, bf16[192,768]{1,0:T(8,128)(2,1)S(1)}, u32[]{:S(2)}, u32[]{:S(2)}) collective-permute-start(bf16[192,768]{1,0:T(8,128)(2,1)S(1)} %collective-permute-done.17.refs_17_.apart_ref), channel_id=1, source_target_pairs={{0,16},{16,0},{32,48},{48,32},{64,80},{80,64},{96,112},{112,96},{1... | collective-permute-start | bytes 884744 | tf_op jit(solution)/shard_map/ppermute | solution.py:522
  48.9 10.7 %collective-permute-start.19 = (bf16[384,768]{1,0:T(8,128)(2,1)S(1)}, bf16[384,768]{1,0:T(8,128)(2,1)S(1)}, u32[]{:S(2)}, u32[]{:S(2)}) collective-permute-start(bf16[384,768]{1,0:T(8,128)(2,1)S(1)} %collective-permute-done.16.refs_16_.ahead_ref), channel_id=1, source_target_pairs={{0,16},{16,0},{32,48},{48,32},{64,80},{80,64},{96,112},{112,96},{1... | collective-permute-start | bytes 1769480 | tf_op jit(solution)/shard_map/ppermute | solution.py:522
  49.2 1.1 %copy-start.17 = (bf16[2,256,512]{2,1,0:T(8,128)(2,1)}, bf16[2,256,512]{2,1,0:T(8,128)(2,1)S(1)}, u32[]{:S(2)}) copy-start(bf16[2,256,512]{2,1,0:T(8,128)(2,1)S(1)} %collective-permute-done.14.refs_14_) | copy-start | bytes 1572868
  50.4 9.2 %copy-start.1 = (bf16[384,3072]{1,0:T(8,128)(2,1)S(1)}, bf16[384,3072]{1,0:T(8,128)(2,1)}, u32[]{:S(2)}) copy-start(bf16[384,3072]{1,0:T(8,128)(2,1)} %w_out_ref.3) | copy-start | bytes 7077892
  50.4 9.2 %copy-start.10 = (s32[8]{0:T(128)S(1)}, s32[8]{0:T(128)}, u32[]{:S(2)}) copy-start(s32[8]{0:T(128)} %stack.59.place_ref) | copy-start | bytes 100
  58.0 7.6 %collective-permute-start.18 = (bf16[2,272,256]{2,1,0:T(8,128)(2,1)}, bf16[2,272,256]{2,1,0:T(8,128)(2,1)S(1)}, u32[]{:S(2)}, u32[]{:S(2)}) collective-permute-start(bf16[2,272,256]{2,1,0:T(8,128)(2,1)} %get-tuple-element.26), channel_id=1, source_target_pairs={{0,8},{8,0},{1,9},{9,1},{2,10},{10,2},{3,11},{11,3},{4,12},{12,4},... | collective-permute-start | bytes 835592 | tf_op jit(solution)/shard_map/ppermute | solution.py:522
  59.6 1.1 %copy-start.3 = (bf16[384,768]{1,0:T(8,128)(2,1)S(1)}, bf16[384,768]{1,0:T(8,128)(2,1)}, u32[]{:S(2)}) copy-start(bf16[384,768]{1,0:T(8,128)(2,1)} %copy-done.2) | copy-start | bytes 1769476
  62.6 3.0 %copy-start.6 = (f32[2,256,256]{2,1,0:T(8,128)S(1)}, f32[2,256,256]{2,1,0:T(8,128)}, u32[]{:S(2)}) copy-start(f32[2,256,256]{2,1,0:T(8,128)} %get-tuple-element.25.mid_ref) | copy-start | bytes 1572868
  65.6 33.5 %copy-start.12 = (f32[384]{0:T(512)S(1)}, f32[384]{0:T(512)}, u32[]{:S(2)}) copy-start(f32[384]{0:T(512)} %param.15) | copy-start | bytes 4612
  66.7 7.8 %collective-permute-start.21 = (bf16[256,384]{1,0:T(8,128)(2,1)S(1)}, bf16[256,384]{1,0:T(8,128)(2,1)S(1)}, u32[]{:S(2)}, u32[]{:S(2)}) collective-permute-start(bf16[256,384]{1,0:T(8,128)(2,1)S(1)} %get-tuple-element.27.refs_0_), channel_id=1, source_target_pairs={{0,1},{1,2},{2,3},{3,0},{4,5},{5,6},{6,7},{7,4},{16,19},{17,16},{1... | collective-permute-start | bytes 589832 | tf_op jit(solution)/shard_map/ppermute | solution.py:522
  68.7 7.9 %collective-permute-start.24 = (bf16[256,384]{1,0:T(8,128)(2,1)S(1)}, bf16[256,384]{1,0:T(8,128)(2,1)S(1)}, u32[]{:S(2)}, u32[]{:S(2)}) collective-permute-start(bf16[256,384]{1,0:T(8,128)(2,1)S(1)} %get-tuple-element.28.refs_4_), channel_id=1, source_target_pairs={{0,1},{1,2},{2,3},{3,0},{4,5},{5,6},{6,7},{7,4},{16,19},{17,16},{1... | collective-permute-start | bytes 589832 | tf_op jit(solution)/shard_map/ppermute | solution.py:522
  70.6 6.7 %collective-permute-start.22 = (bf16[256,384]{1,0:T(8,128)(2,1)S(1)}, bf16[256,384]{1,0:T(8,128)(2,1)S(1)}, u32[]{:S(2)}, u32[]{:S(2)}) collective-permute-start(bf16[256,384]{1,0:T(8,128)(2,1)S(1)} %get-tuple-element.27.refs_0_), channel_id=1, source_target_pairs={{0,3},{1,0},{2,1},{3,2},{4,7},{5,4},{6,5},{7,6},{16,17},{17,18},{1... | collective-permute-start | bytes 589832 | tf_op jit(solution)/shard_map/ppermute | solution.py:522
  71.9 9.5 %collective-permute-start.25 = (bf16[256,384]{1,0:T(8,128)(2,1)S(1)}, bf16[256,384]{1,0:T(8,128)(2,1)S(1)}, u32[]{:S(2)}, u32[]{:S(2)}) collective-permute-start(bf16[256,384]{1,0:T(8,128)(2,1)S(1)} %get-tuple-element.28.refs_4_), channel_id=1, source_target_pairs={{0,3},{1,0},{2,1},{3,2},{4,7},{5,4},{6,5},{7,6},{16,17},{17,18},{1... | collective-permute-start | bytes 589832 | tf_op jit(solution)/shard_map/ppermute | solution.py:522
  74.4 8.4 %collective-permute-start.23 = (bf16[256,384]{1,0:T(8,128)(2,1)S(1)}, bf16[256,384]{1,0:T(8,128)(2,1)S(1)}, u32[]{:S(2)}, u32[]{:S(2)}) collective-permute-start(bf16[256,384]{1,0:T(8,128)(2,1)S(1)} %collective-permute-done.21.refs_1_), channel_id=1, source_target_pairs={{0,1},{1,2},{2,3},{3,0},{4,5},{5,6},{6,7},{7,4},{16,19},{17,16},{1... | collective-permute-start | bytes 589832 | tf_op jit(solution)/shard_map/ppermute | solution.py:522
  76.6 8.5 %collective-permute-start.26 = (bf16[256,384]{1,0:T(8,128)(2,1)S(1)}, bf16[256,384]{1,0:T(8,128)(2,1)S(1)}, u32[]{:S(2)}, u32[]{:S(2)}) collective-permute-start(bf16[256,384]{1,0:T(8,128)(2,1)S(1)} %collective-permute-done.24.refs_5_), channel_id=1, source_target_pairs={{0,1},{1,2},{2,3},{3,0},{4,5},{5,6},{6,7},{7,4},{16,19},{17,16},{1... | collective-permute-start | bytes 589832 | tf_op jit(solution)/shard_map/ppermute | solution.py:522
  87.1 12.0 %collective-permute-start.27 = (bf16[512,384]{1,0:T(8,128)(2,1)S(1)}, bf16[512,384]{1,0:T(8,128)(2,1)S(1)}, u32[]{:S(2)}, u32[]{:S(2)}) collective-permute-start(bf16[512,384]{1,0:T(8,128)(2,1)S(1)} %get-tuple-element.30), channel_id=1, source_target_pairs={{0,4},{1,5},{2,6},{3,7},{4,0},{5,1},{6,2},{7,3},{8,12},{9,13},{10,... | collective-permute-start | bytes 1179656 | tf_op jit(solution)/shard_map/ppermute | solution.py:522
  (7 other events, 5.9 us)
